TPU v7x, 256 devices: a whole 4x4x8 slice. The times are simulated.
256 devices in a mesh: row: 16 (over z_hi, x), col: 16 (over y, z_lo, core).
Axes of the slice: x: 4, y: 4, z: 8 (z_hi: 4, z_lo: 2; z = z_hi * 2 + z_lo), core: 2. Of those that a mesh axis runs over, the one named last changes fastest.
Arguments:
- matrix: float32 [16384, 16384], P('row', 'col'), as said below
- reflectors: float32 [5, 64, 16384], P(None, None, 'row'), may hold values from -0.09375 to 0.09375
- factors: float32 [5, 64, 64], replicated, as said below
Outputs:
- updated: float32 [16384, 16384], P('row', 'col')
Inputs may be any that keep to these rules, and one draw needn't show every extreme that they name: matrix is symmetric: matrix[r, c] equals matrix[c, r]; its entries are of order one, off the diagonal each the scaled sum of two independent draws of the same law (unbounded normal in one draw, bounded uniform with row and column scales in the other). Each 64 x 64 block of factors is zero below its diagonal.
All inputs are finite; a program needn't handle non-finite values.
Results may differ from a plain program's by a relative error of at most 0.0001.
Values sent between devices are 32-bit elements; how exact they have to be, the bound alone decides.
No kernel may reach another device: no remote copies, remote signals or barrier semaphores. Data moves between devices by JAX's collectives and lax.ppermute only.
A program may use at most 64 MiB of HBM per device.

v0:
```python
import jax
import jax.numpy as jnp
from jax import lax
from jax.sharding import PartitionSpec as P


def spread(x, axis, root):
    mine = lax.axis_index(axis) == root
    return lax.psum(jnp.where(mine, x, jnp.zeros_like(x)), axis)


def contract(former, latter, former_dim, latter_dim):
    return lax.dot_general(
        former,
        latter,
        (((former_dim,), (latter_dim,)), ((), ())),
        precision=lax.Precision.HIGHEST,
        preferred_element_type=jnp.float32,
    )


def body(matrix, reflectors, factors):
    row_count = lax.axis_size("row")
    col_count = lax.axis_size("col")
    stacking = row_count // col_count
    column = lax.axis_index("col")
    panels = factors.shape[0]
    current = matrix
    for panel_index in range(panels):
        row_side = reflectors[panel_index]
        factor = factors[panel_index]
        col_side = spread(reflectors[panel_index], "row", column * stacking + 0)
        products = contract(col_side, current, 1, 1)
        row_sums = lax.psum(products, "col")
        image_rows = contract(factor, row_sums, 0, 0)
        gram_matrix = lax.psum(contract(row_side, image_rows, 1, 1), "row")
        shifted = contract(factor, gram_matrix, 0, 0)
        update_rows = image_rows - 0.5 * contract(shifted, row_side, 0, 0)
        update_cols = spread(update_rows, "row", column * stacking + 0)
        left_side = jnp.concatenate([row_side, update_rows], axis=0)
        right_side = jnp.concatenate([update_cols, col_side], axis=0)
        current = current - contract(left_side, right_side, 0, 0)
    return current


def solution(mesh):
    in_specs = (P("row", "col"), P(None, None, "row"), P())
    out_specs = P("row", "col")
    return jax.shard_map(body, mesh=mesh, in_specs=in_specs, out_specs=out_specs, check_vma=False)
```

profile of v0, /device:TPU:1, one launch (start us, length us, event | category | flops | bytes accessed | tf_op | source)
XLA Modules:
  0.0 2061.1 jit_solution(9703611212908379906)
XLA Ops:
  6.5 2.4 broadcast_select_fusion.1
  9.1 159.0 %all-reduce.16.cloned.1.call-done = f32[64,1024]{1,0:T(8,128)} async-done(((f32[64,1024]{1,0:T(8,128)}), f32[64,1024]{1,0:T(8,128)}) %all-reduce.16.cloned.1.call-update) | async-done | bytes 262160 | tf_op jit(solution)/shard_map/psum | solution.py:9
  168.1 7.1 fusion.70
  175.2 130.1 %all-reduce.18.cloned.1.call-done = f32[64,1024]{1,0:T(8,128)} async-done(((f32[64,1024]{1,0:T(8,128)}), f32[64,1024]{1,0:T(8,128)}) %all-reduce.18.cloned.1.call-update) | async-done | bytes 262160 | tf_op jit(solution)/shard_map/psum | solution.py:34
  305.3 1.4 fusion.53
  307.1 68.0 %psum.142 = f32[64,64]{0,1:T(8,128)S(1)} all-reduce(f32[64,64]{0,1:T(8,128)S(1)} %convolution_bitcast_fusion.4), channel_id=1, replica_groups=mesh['row'=16,'col'=16] {'row'}, use_global_device_ids=true, to_apply=%region_2.3 | all-reduce | flops 4096 | bytes 32768 | tf_op jit(solution)/shard_map/psum | solution.py:36
  377.4 163.3 %all-reduce.36.cloned.1.call-done = (f32[64,1024]{1,0:T(8,128)}, f32[64,1024]{1,0:T(8,128)}) async-done(((f32[64,1024]{1,0:T(8,128)}, f32[64,1024]{1,0:T(8,128)}), (f32[64,1024]{1,0:T(8,128)}, f32[64,1024]{1,0:T(8,128)})) %all-reduce.36.cloned.1.call-update) | async-done | bytes 524304 | tf_op jit(solution)/shard_map/psum | solution.py:9
  540.6 5.4 convolution_subtract_fusion.4
  546.1 2.0 copy-done.2
  548.1 4.9 fusion.71
  553.0 130.1 %all-reduce.20.cloned.1.call-done = f32[64,1024]{1,0:T(8,128)} async-done(((f32[64,1024]{1,0:T(8,128)}), f32[64,1024]{1,0:T(8,128)}) %all-reduce.20.cloned.1.call-update) | async-done | bytes 262160 | tf_op jit(solution)/shard_map/psum | solution.py:34
  684.9 68.0 %psum.146 = f32[64,64]{0,1:T(8,128)S(1)} all-reduce(f32[64,64]{0,1:T(8,128)S(1)} %convolution_bitcast_fusion.3), channel_id=1, replica_groups=mesh['row'=16,'col'=16] {'row'}, use_global_device_ids=true, to_apply=%region_6.7 | all-reduce | flops 4096 | bytes 32768 | tf_op jit(solution)/shard_map/psum | solution.py:36
  755.2 163.1 %all-reduce.34.cloned.1.call-done = (f32[64,1024]{1,0:T(8,128)}, f32[64,1024]{1,0:T(8,128)}) async-done(((f32[64,1024]{1,0:T(8,128)}, f32[64,1024]{1,0:T(8,128)}), (f32[64,1024]{1,0:T(8,128)}, f32[64,1024]{1,0:T(8,128)})) %all-reduce.34.cloned.1.call-update) | async-done | bytes 524304 | tf_op jit(solution)/shard_map/psum | solution.py:9
  918.3 5.4 convolution_subtract_fusion.3
  923.8 2.0 copy-done.1
  925.8 4.9 fusion.72
  930.7 130.1 %all-reduce.22.cloned.1.call-done = f32[64,1024]{1,0:T(8,128)} async-done(((f32[64,1024]{1,0:T(8,128)}), f32[64,1024]{1,0:T(8,128)}) %all-reduce.22.cloned.1.call-update) | async-done | bytes 262160 | tf_op jit(solution)/shard_map/psum | solution.py:34
  1062.6 68.0 %psum.150 = f32[64,64]{0,1:T(8,128)S(1)} all-reduce(f32[64,64]{0,1:T(8,128)S(1)} %convolution_bitcast_fusion.2), channel_id=1, replica_groups=mesh['row'=16,'col'=16] {'row'}, use_global_device_ids=true, to_apply=%region_10.11 | all-reduce | flops 4096 | bytes 32768 | tf_op jit(solution)/shard_map/psum | solution.py:36
  1131.9 163.3 %all-reduce.32.cloned.1.call-done = (f32[64,1024]{1,0:T(8,128)}, f32[64,1024]{1,0:T(8,128)}) async-done(((f32[64,1024]{1,0:T(8,128)}, f32[64,1024]{1,0:T(8,128)}), (f32[64,1024]{1,0:T(8,128)}, f32[64,1024]{1,0:T(8,128)})) %all-reduce.32.cloned.1.call-update) | async-done | bytes 524304 | tf_op jit(solution)/shard_map/psum | solution.py:9
  1295.2 5.4 convolution_subtract_fusion.2
  1300.7 2.0 copy-done
  1302.7 4.9 fusion.73
  1307.6 130.1 %all-reduce.24.cloned.1.call-done = f32[64,1024]{1,0:T(8,128)} async-done(((f32[64,1024]{1,0:T(8,128)}), f32[64,1024]{1,0:T(8,128)}) %all-reduce.24.cloned.1.call-update) | async-done | bytes 262160 | tf_op jit(solution)/shard_map/psum | solution.py:34
  1439.5 68.0 %psum.154 = f32[64,64]{0,1:T(8,128)S(1)} all-reduce(f32[64,64]{0,1:T(8,128)S(1)} %convolution_bitcast_fusion.1), channel_id=1, replica_groups=mesh['row'=16,'col'=16] {'row'}, use_global_device_ids=true, to_apply=%region_14.15 | all-reduce | flops 4096 | bytes 32768 | tf_op jit(solution)/shard_map/psum | solution.py:36
  1508.8 163.3 %all-reduce.30.cloned.1.call-done = (f32[64,1024]{1,0:T(8,128)}, f32[64,1024]{1,0:T(8,128)}) async-done(((f32[64,1024]{1,0:T(8,128)}, f32[64,1024]{1,0:T(8,128)}), (f32[64,1024]{1,0:T(8,128)}, f32[64,1024]{1,0:T(8,128)})) %all-reduce.30.cloned.1.call-update) | async-done | bytes 524304 | tf_op jit(solution)/shard_map/psum | solution.py:9
  1672.2 5.4 convolution_subtract_fusion.1
  1677.6 2.0 copy-done.3
  1679.7 4.9 fusion.74
  1684.6 130.3 %all-reduce.26.cloned.1.call-done = f32[64,1024]{1,0:T(8,128)} async-done(((f32[64,1024]{1,0:T(8,128)}), f32[64,1024]{1,0:T(8,128)}) %all-reduce.26.cloned.1.call-update) | async-done | bytes 262160 | tf_op jit(solution)/shard_map/psum | solution.py:34
  1816.7 68.0 %psum.158 = f32[64,64]{0,1:T(8,128)S(1)} all-reduce(f32[64,64]{0,1:T(8,128)S(1)} %convolution_bitcast_fusion), channel_id=1, replica_groups=mesh['row'=16,'col'=16] {'row'}, use_global_device_ids=true, to_apply=%region_18.19 | all-reduce | flops 4096 | bytes 32768 | tf_op jit(solution)/shard_map/psum | solution.py:36
  1886.0 162.0 %all-reduce.28.cloned.1.call-done = f32[64,1024]{1,0:T(8,128)} async-done(((f32[64,1024]{1,0:T(8,128)}), f32[64,1024]{1,0:T(8,128)}) %all-reduce.28.cloned.1.call-update) | async-done | bytes 262160 | tf_op jit(solution)/shard_map/psum | solution.py:9
  2048.0 6.6 convolution_subtract_fusion
  (60 shorter events, 15.9 us)
Async XLA Ops:
  6.5 161.5 %all-reduce.16.cloned.1.call-start = ((), (), s32[]{:S(2)}) async-start(), calls=%async_computation | async-start | bytes 524288 | tf_op jit(solution)/shard_map/psum | solution.py:9
  6.5 300.2 %copy-start.4 = (f32[5,64,1024]{2,1,0:T(8,128)S(1)}, f32[5,64,1024]{2,1,0:T(8,128)}, u32[]{:S(2)}) copy-start(f32[5,64,1024]{2,1,0:T(8,128)} %param.4) | copy-start | bytes 3932164
  9.0 296.3 %all-reduce.18.cloned.1.call-start = ((), (), s32[]{:S(2)}) async-start(), calls=%async_computation.1 | async-start | bytes 524288 | tf_op jit(solution)/shard_map/psum | solution.py:34
  168.1 372.5 %copy-start.9 = (f32[64,1024]{1,0:T(8,128)S(1)}, f32[64,1024]{1,0:T(8,128)}, u32[]{:S(2)}) copy-start(f32[64,1024]{1,0:T(8,128)} %all-reduce.16.cloned.1.call-done) | copy-start | bytes 786436
  175.2 365.4 %all-reduce.36.cloned.1.call-start = ((), (), s32[]{:S(2)}) async-start(), calls=%async_computation.10 | async-start | bytes 1048576 | tf_op jit(solution)/shard_map/psum | solution.py:9
  377.2 306.0 %all-reduce.20.cloned.1.call-start = ((), (), s32[]{:S(2)}) async-start(), calls=%async_computation.2 | async-start | bytes 524288 | tf_op jit(solution)/shard_map/psum | solution.py:34
  540.6 7.5 copy-start.5
  546.0 2.0 copy-start.2
  553.0 365.4 %all-reduce.34.cloned.1.call-start = ((), (), s32[]{:S(2)}) async-start(), calls=%async_computation.9 | async-start | bytes 1048576 | tf_op jit(solution)/shard_map/psum | solution.py:9
  754.9 305.9 %all-reduce.22.cloned.1.call-start = ((), (), s32[]{:S(2)}) async-start(), calls=%async_computation.3 | async-start | bytes 524288 | tf_op jit(solution)/shard_map/psum | solution.py:34
  918.3 7.5 copy-start.7
  923.7 2.0 copy-start.1
  923.8 137.1 %copy-start.10 = (f32[5,64,64]{2,1,0:T(8,128)S(1)}, f32[5,64,64]{2,1,0:T(8,128)}, u32[]{:S(2)}) copy-start(f32[5,64,64]{2,1,0:T(8,128)} %param.5) | copy-start | bytes 245764
  930.6 364.6 %all-reduce.32.cloned.1.call-start = ((), (), s32[]{:S(2)}) async-start(), calls=%async_computation.8 | async-start | bytes 1048576 | tf_op jit(solution)/shard_map/psum | solution.py:9
  1131.9 305.9 %all-reduce.24.cloned.1.call-start = ((), (), s32[]{:S(2)}) async-start(), calls=%async_computation.4 | async-start | bytes 524288 | tf_op jit(solution)/shard_map/psum | solution.py:34
  1295.2 7.5 copy-start.6
  1300.7 2.0 copy-start
  1307.6 364.6 %all-reduce.30.cloned.1.call-start = ((), (), s32[]{:S(2)}) async-start(), calls=%async_computation.7 | async-start | bytes 1048576 | tf_op jit(solution)/shard_map/psum | solution.py:9
  1508.8 306.1 %all-reduce.26.cloned.1.call-start = ((), (), s32[]{:S(2)}) async-start(), calls=%async_computation.5 | async-start | bytes 524288 | tf_op jit(solution)/shard_map/psum | solution.py:34
  1672.2 7.5 copy-start.8
  1677.6 2.0 copy-start.3
  1684.5 363.4 %all-reduce.28.cloned.1.call-start = ((), (), s32[]{:S(2)}) async-start(), calls=%async_computation.6 | async-start | bytes 524288 | tf_op jit(solution)/shard_map/psum | solution.py:9
Sparse Core Ops, SparseCore 0:
  10.0 158.0 all-reduce.15
  175.3 130.0 all-reduce.17
  377.3 163.2 all-reduce.35
  553.1 130.0 all-reduce.19
  755.1 163.2 all-reduce.33
  930.8 130.0 all-reduce.21
  1132.0 163.1 all-reduce.31
  1307.7 130.0 all-reduce.23
  1508.9 163.2 all-reduce.29
  1684.7 130.2 all-reduce.25
  1886.1 161.8 all-reduce.27
where the time goes:
time: 2070 us; the launch traced here: 2060 us
  waiting for transfers between devices  1630 us (79%)
  blocking collectives  340 us (16%)
  matrix products  71.1 us (3%)
    psum x6, waiting for transfers between devices, spread(): return lax.psum(jnp.where(mine, x, jnp.zeros_like(x)), axis)  974 us
    psum x5, waiting for transfers between devices, body(): row_sums = lax.psum(products, 'col')  651 us
    psum x5, blocking collectives, body(): gram_matrix = lax.psum(contract(row_side, image_rows, 1, 1), 'row')  340 us
    dot_general x30, matrix products, contract(): lax.dot_general(former, latter, (((former_dim,), (latter_dim,)), ((), ())...  71.1 us
  transfers between devices with their start and end apart: 11, of which 11 were waited for; matrix products, arithmetic and copies ran while one was open for 0% of the time, Pallas kernels for 0%

commit v1 on v0

v1 whole, which is shorter than its diff:
```python
import jax
import jax.numpy as jnp
from jax import lax
from jax.experimental import pallas as pl
from jax.experimental.pallas import tpu as pltpu
from jax.sharding import PartitionSpec as P

HIGH = lax.Precision.HIGH
HIGHEST = lax.Precision.HIGHEST
F32 = jnp.float32
BF16 = jnp.bfloat16
SDS = jax.ShapeDtypeStruct

SHIFT_X = {d: [(i, (i // 4) * 4 + (i + d) % 4) for i in range(16)] for d in (1, 2, 3)}
SHIFT_Z = {d: [(i, (i + 4 * d) % 16) for i in range(16)] for d in (1, 2, 3)}
SHIFT_Y = SHIFT_Z
SWAP_ZLO = [(i, i ^ 2) for i in range(16)]
SWAP_CORE = [(i, i ^ 1) for i in range(16)]
TO_COLUMN = [(c * 16 + 4 * x + z, (z * 4 + x) * 16 + c) for c in range(16) for x in range(4) for z in range(4)]
TO_ROW = [(b, a) for a, b in TO_COLUMN]
EVERYWHERE = ("row", "col")


def flip(bit):
    return [(i, i ^ bit) for i in range(16)]


def dot(a, b, da, db, precision):
    return lax.dot_general(
        a, b, (((da,), (db,)), ((), ())), precision=precision, preferred_element_type=F32
    )


def split(a):
    high = a.astype(BF16)
    return high, (a - high.astype(F32)).astype(BF16)


def wide(a):
    high, low = split(a)
    return jnp.concatenate([high, low, high], axis=1)


def tall(a):
    high, low = split(a)
    return jnp.concatenate([high, high, low], axis=0)


def mul(a, b):
    return jnp.dot(a, b, preferred_element_type=F32)


def dot3(a, b, da, db):
    dims = (((da,), (db,)), ((), ()))
    (ah, al), (bh, bl) = a, b
    out = lax.dot_general(ah, bh, dims, preferred_element_type=F32)
    out += lax.dot_general(ah, bl, dims, preferred_element_type=F32)
    return out + lax.dot_general(al, bh, dims, preferred_element_type=F32)


def piece(a, index, size, dim):
    return lax.dynamic_slice_in_dim(a, index * size, size, dim)


def send(parts, axis, shifts):
    return [lax.ppermute(part, axis, shifts[d]) for d, part in parts]


def whole_kernel(kernel, shapes, place, *operands, scratch=(), flops=0, after=()):
    size = 4 * sum(a.size for a in operands) + sum(s.size * s.dtype.itemsize for s in shapes)
    count = len(operands)
    return pl.pallas_call(
        lambda place, *refs: kernel(place, *refs[:count], *refs[count + len(after) :]),
        out_shape=list(shapes),
        in_specs=[pl.BlockSpec(memory_space=pltpu.SMEM)]
        + [pl.BlockSpec(memory_space=pltpu.VMEM)] * len(operands)
        + [pl.BlockSpec(memory_space=pl.ANY)] * len(after),
        out_specs=[pl.BlockSpec(memory_space=pltpu.VMEM)] * len(shapes),
        scratch_shapes=list(scratch),
        compiler_params=pltpu.CompilerParams(vmem_limit_bytes=40 * 2**20),
        cost_estimate=pl.CostEstimate(flops=flops, bytes_accessed=size, transcendentals=0),
    )(place, *operands, *after)


def at(place_ref, index, size):
    return pl.ds(pl.multiple_of(place_ref[index] * size, size), size)


def quarter_product_kernel(place, vec_ref, mat_ref, *rest):
    outs, turn_ref, vec_split = rest[:4], rest[4], rest[5]
    step = pl.program_id(0)
    rank = vec_ref.shape[0]

    @pl.when(step == 0)
    def _():
        vec_split[:rank], vec_split[rank:] = split(vec_ref[...])
        size, lanes = turn_ref.shape
        turn_ref[...] = vec_ref[at(place, 4, size), at(place, 5, lanes)]

    high, low = split(mat_ref[...])
    both = mul(vec_split[...], high)
    value = both[:rank] + both[rank:] + mul(vec_split[:rank], low)
    for k in range(4):

        @pl.when(step == k)
        def _():
            outs[k][...] = value


def quarter_products(place, vectors, matrix):
    rank, rows = vectors.shape
    width = matrix.shape[1] // 4
    shapes = [SDS((rank, width), F32)] * 4 + [SDS((rank // 4, rows // 4), F32)]
    return pl.pallas_call(
        quarter_product_kernel,
        out_shape=shapes,
        grid_spec=pltpu.PrefetchScalarGridSpec(
            num_scalar_prefetch=1,
            grid=(4,),
            in_specs=[
                pl.BlockSpec((rank, rows), lambda i, place: (0, 0)),
                pl.BlockSpec((rows, width), lambda i, place: (0, place[i])),
            ],
            out_specs=[pl.BlockSpec(s.shape, lambda i, place: (0, 0)) for s in shapes],
            scratch_shapes=[pltpu.VMEM((2 * rank, rows), BF16)],
        ),
        compiler_params=pltpu.CompilerParams(vmem_limit_bytes=40 * 2**20),
        cost_estimate=pl.CostEstimate(
            flops=6 * rank * rows * width * 4,
            bytes_accessed=4 * (rank * rows + rows * width * 4 + rank * width * 4),
            transcendentals=0,
        ),
    )(place, vectors, matrix)


def sum_x_kernel(place, p0, p1, p2, p3, *rest):
    outs, prod_ref = rest[:4], rest[4]
    prod_ref[...] = p0[...] + p1[...] + p2[...] + p3[...]
    for d in range(4):
        outs[d][...] = prod_ref[at(place, d, outs[d].shape[0])]


def sum_z_kernel(place, p0, p1, p2, p3, sum_ref):
    sum_ref[...] = p0[...] + p1[...] + p2[...] + p3[...]


def join_kernel(place, *refs):
    parts, passed, prod_ref, outs = refs[:4], refs[4:6], refs[6], refs[7:]
    for d in range(4):
        prod_ref[at(place, 4 + d, parts[d].shape[0])] = parts[d][...]
    for src_ref, dst_ref in zip(passed, outs):
        dst_ref[...] = src_ref[...]


def inner_kernel(width, place, *refs):
    parts, vecs, vec_ref = refs[:4], refs[4:8], refs[8]
    out_ref, mine_ref, vec_x_ref, prod_ref = refs[9:]
    size, lanes = parts[0].shape
    for d in range(4):
        prod_ref[:, at(place, 2 + d, lanes)] = parts[d][...]
        mine_ref[d] = parts[d][...]
        vec_x_ref[at(place, 6 + d, size)] = vecs[d][...]
    mine = vec_ref[at(place, 0, size)]
    inner = dot(mine, prod_ref[...], 1, 1, HIGHEST)
    gram = dot(mine, vec_ref[at(place, 1, size)], 1, 1, HIGHEST)
    down = (place[0] * size + lax.broadcasted_iota(jnp.int32, inner.shape, 0)) // width
    over = (place[1] * size + lax.broadcasted_iota(jnp.int32, inner.shape, 1)) // width
    out_ref[...] = jnp.where(over >= down, inner, gram)


def sum_kernel(place, a, b, vec_ref, sum_ref, out_ref):
    sum_ref[...] = a[...] + b[...]
    out_ref[...] = vec_ref[...]


def pile_kernel(place, a, b, out_ref):
    out_ref[:2] = a[...]
    out_ref[2:] = b[...]


def factor_kernel(place, mine_ref, other_ref, factors_ref, *rest):
    first_ref, second_ref, factor_ref, strip_ref, both_ref = rest[-5:]
    panels, width, _ = factors_ref.shape
    rank = panels * width
    size = mine_ref.shape[2]
    for k, ref in enumerate((mine_ref, other_ref)):
        for l in range(2):
            for d in range(4):
                strip_ref[place[2 * k + l], at(place, 4 + d, size)] = ref[l, d]
    for q in range(4):
        both_ref[:, q * size : (q + 1) * size] = strip_ref[q]
    both = both_ref[...]
    turned = both.T
    down = lax.broadcasted_iota(jnp.int32, both.shape, 0) // width
    over = lax.broadcasted_iota(jnp.int32, both.shape, 1) // width
    inner = jnp.where(over >= down, both, turned)
    factor_ref[...] = jnp.zeros(factor_ref.shape, F32)
    factor_ref[:width, :width] = factors_ref[0]
    for p in range(1, panels):
        m = p * width
        across = dot(turned[:m, m : m + width], factors_ref[p], 1, 0, HIGHEST)
        factor_ref[:m, m : m + width] = -dot(factor_ref[:m, :m], across, 1, 0, HIGHEST)
        factor_ref[m : m + width, m : m + width] = factors_ref[p]
    factor = factor_ref[...]
    across = factor.T
    middle = mul(wide(across), tall(mul(wide(inner), tall(factor))))
    first_ref[...] = wide(jnp.concatenate([across, -middle], axis=1))
    second_ref[...] = wide(factor)


def left_kernel(place, vec_ref, mine_ref, other_ref, left_ref, prod_ref):
    rank = vec_ref.shape[0]
    for k, ref in enumerate((mine_ref, other_ref)):
        for l in range(2):
            for d in range(4):
                prod_ref[at(place, 2 * k + l, 80), at(place, 4 + d, 256)] = ref[l, d]
    for start, ref in ((0, vec_ref), (rank, prod_ref)):
        high, low = split(ref[...].T)
        left_ref[:, start : start + rank] = high
        left_ref[:, 2 * rank + start : 3 * rank + start] = low
        left_ref[:, 4 * rank + start : 5 * rank + start] = high


def update_kernel(place, *refs):
    prods, vecs = refs[:4], refs[4:8]
    first_ref, second_ref, left_ref, mat_ref, out_ref, new_ref, sems = refs[8:]
    width = prods[0].shape[1]
    copies = []
    for k in range(4):
        prod, vec = prods[k][...], vecs[k][...]
        one = mul(first_ref[...], tall(jnp.concatenate([prod, vec], axis=0)))
        two = mul(second_ref[...], tall(vec))
        right = tall(jnp.concatenate([one, two], axis=0))
        where = at(place, k, width)
        new_ref[:, where] = mat_ref[:, where] - mul(left_ref[...], right)
        copies.append(pltpu.make_async_copy(new_ref.at[:, where], out_ref.at[:, where], sems.at[k]))
        copies[k].start()
    for copy in copies:
        copy.wait()


def update(place, *operands):
    rows, columns = operands[-1].shape
    rank = operands[0].shape[0]
    return pl.pallas_call(
        update_kernel,
        out_shape=SDS((rows, columns), F32),
        in_specs=[pl.BlockSpec(memory_space=pltpu.SMEM)]
        + [pl.BlockSpec(memory_space=pltpu.VMEM)] * len(operands),
        out_specs=pl.BlockSpec(memory_space=pl.ANY),
        scratch_shapes=[pltpu.VMEM((rows, columns), F32), pltpu.SemaphoreType.DMA((4,))],
        compiler_params=pltpu.CompilerParams(vmem_limit_bytes=40 * 2**20),
        cost_estimate=pl.CostEstimate(
            flops=12 * rows * rank * columns, bytes_accessed=8 * rows * columns, transcendentals=0
        ),
    )(place, *operands)


def body(matrix, reflectors, factors):
    panels, width, _ = reflectors.shape
    rank = panels * width
    rows = reflectors.shape[2]
    vectors = reflectors.reshape(rank, rows)
    row, col = lax.axis_index("row"), lax.axis_index("col")
    x, z = row % 4, row // 4
    y, zlo, core = col // 4, (col // 2) % 2, col % 2
    table = lambda entries: jnp.stack(entries).astype(jnp.int32)
    order = [x, (x + 3) % 4, (x + 1) % 4, (x + 2) % 4]
    first = table([(x + 2) % 4, (x + 1) % 4, (x + 3) % 4, x, col % 4, y])
    away = table([(z + d) % 4 for d in range(4)] + [(z - d) % 4 for d in range(4)])
    lanes_at = [(y - d) % 4 for d in range(4)]
    pieces = [2 * (zlo ^ l) + (core ^ k) for k in range(2) for l in range(2)]
    pieces_flip = table(pieces + [y ^ d for d in range(4)])
    pieces_at = table(pieces + lanes_at)
    size, lanes = rank // 4, rows // 4
    slice_shape = SDS((size, lanes), F32)
    quarter_shape = SDS((rank, lanes), F32)
    inner_shape = SDS((size, size), F32)

    with jax.named_scope("products"):
        opposite, right, left, mine, turn = quarter_products(first, vectors, matrix)
    with jax.named_scope("prod_sum_x"):
        got = send([(2, opposite), (1, right), (3, left)], "row", SHIFT_X)
    with jax.named_scope("vec_turn"):
        vec_part = lax.ppermute(turn, EVERYWHERE, TO_COLUMN)
    with jax.named_scope("sum_x"):
        prods = whole_kernel(
            sum_x_kernel, [slice_shape] * 4, away, mine, *got,
            scratch=[pltpu.VMEM(quarter_shape.shape, F32)],
        )
    with jax.named_scope("prod_sum_z"):
        got = send([(d, prods[d]) for d in (2, 1, 3)], "row", SHIFT_Z)
    with jax.named_scope("sum_z"):
        (prod_part,) = whole_kernel(sum_z_kernel, [slice_shape], away, prods[0], *got)
    with jax.named_scope("prod_z"):
        got = send([(d, prod_part) for d in (1, 2, 3)], "row", SHIFT_Z)
    with jax.named_scope("prod_turn"):
        other = lax.ppermute(prod_part, EVERYWHERE, TO_ROW)
    with jax.named_scope("join"):
        prod_z, other, vec_part = whole_kernel(
            join_kernel, [quarter_shape, slice_shape, slice_shape], away, prod_part, *got, other, vec_part
        )
    with jax.named_scope("prod_x"):
        prod_two, prod_left, prod_right = send([(d, prod_z) for d in (2, 1, 3)], "row", SHIFT_X)
    with jax.named_scope("row_y"):
        others = [other] + send([(d, other) for d in (1, 2, 3)], "col", SHIFT_Y)
    with jax.named_scope("vec_z"):
        vecs = [vec_part] + send([(d, vec_part) for d in (1, 2, 3)], "row", SHIFT_Z)
    with jax.named_scope("inner"):
        inner, mine, vec_x = whole_kernel(
            lambda *refs: inner_kernel(width, *refs),
            [inner_shape, SDS((4, size, lanes), F32), quarter_shape],
            table([y, col % 4] + lanes_at + [(z - d) % 4 for d in range(4)]), *others, *vecs, vectors,
            scratch=[pltpu.VMEM((size, rows), F32)], flops=24 * size * size * rows,
            after=[prod_left, prod_right, prod_two],
        )
    with jax.named_scope("row_zlo"):
        mine = jnp.stack([mine, lax.ppermute(mine, "col", SWAP_ZLO)])
    with jax.named_scope("row_core"):
        other = lax.ppermute(mine, "col", SWAP_CORE)
    with jax.named_scope("left"):
        (left,) = whole_kernel(
            left_kernel, [SDS((rows, 6 * rank), BF16)], pieces_at, vectors, mine, other,
            scratch=[pltpu.VMEM((rank, rows), F32)],
        )
    with jax.named_scope("inner_x"):
        inner = inner + lax.ppermute(inner, "row", flip(1))
        got = lax.ppermute(inner, "row", flip(2))
        inner, vec_x = whole_kernel(sum_kernel, [inner_shape, quarter_shape], away, inner, got, vec_x)
    with jax.named_scope("vec_x"):
        vec_two, vec_left, vec_right = send([(d, vec_x) for d in (2, 1, 3)], "row", SHIFT_X)
    with jax.named_scope("inner_z"):
        for d in (4, 8):
            inner = inner + lax.ppermute(inner, "row", flip(d))
    with jax.named_scope("inner_y"):
        inner = jnp.stack([inner, lax.ppermute(inner, "col", flip(4))])
        (inner,) = whole_kernel(
            pile_kernel, [SDS((4, size, size), F32)], away, inner, lax.ppermute(inner, "col", flip(8)),
            after=[left],
        )
    with jax.named_scope("inner_zlo"):
        inner = jnp.stack([inner, lax.ppermute(inner, "col", flip(2))])
    with jax.named_scope("inner_core"):
        inner_other = lax.ppermute(inner, "col", flip(1))
    with jax.named_scope("factor"):
        sides = whole_kernel(
            factor_kernel, [SDS((rank, 6 * rank), BF16), SDS((rank, 3 * rank), BF16)],
            pieces_flip, inner, inner_other, factors,
            scratch=[
                pltpu.VMEM((rank, rank), F32), pltpu.VMEM((4, rank, size), F32), pltpu.VMEM((rank, rank), F32)
            ],
        )
    with jax.named_scope("update"):
        return update(
            table(order), prod_z, prod_left, prod_right, prod_two, vec_x, vec_left, vec_right, vec_two,
            *sides, left, matrix,
        )


def solution(mesh):
    in_specs = (P("row", "col"), P(None, None, "row"), P())
    out_specs = P("row", "col")
    return jax.shard_map(body, mesh=mesh, in_specs=in_specs, out_specs=out_specs, check_vma=False)
```

time: 2070 us -> 167 us (0.08)
  waiting for transfers between devices: 1630 us -> 58.2 us
  blocking collectives: 340 us -> 0 us
  matrix products: 71.1 us -> 0 us
  starting transfers between devices: 0.6 us -> 71.2 us
  Pallas kernels: 0 us -> 25 us
    psum x11 -> x0, waiting for transfers between devices: 1620 us -> none  [the longest x6 974 us: spread(): return lax.psum(jnp.where(mine, x, jnp.zeros_like(x)), axis)]
    psum x5 -> x0, blocking collectives: 340 us -> none  [body(): gram_matrix = lax.psum(contract(row_side, image_rows, 1, 1), 'row')]
    ppermute x0 -> x33, starting transfers between devices: none -> 71.2 us  [the longest x21 41.8 us: send(): return [lax.ppermute(part, axis, shifts[d]) for d, part in parts]]
    dot_general x30 -> x0, matrix products: 71.1 us -> none  [contract(): lax.dot_general(former, latter, (((former_dim,), (latter_dim,)), ((), ())...]
    ppermute x0 -> x33, waiting for transfers between devices: none -> 58.2 us  [the longest x21 32.7 us: send(): return [lax.ppermute(part, axis, shifts[d]) for d, part in parts]]
    pallas_call x0 -> x10, Pallas kernels: none -> 25 us  [the longest x8 10.9 us: whole_kernel(): pl.pallas_call(lambda place, *refs: kernel(place, *refs[:count], *refs[co...]
  transfers between devices with their start and end apart: 11 -> 33, of which waited for: 11 -> 19; matrix products, arithmetic and copies ran while one was open for 0% -> 0% of each run, Pallas kernels for 0% -> 5%
where the time goes in v1:
time: 167 us; the launch traced here: 165 us
  starting transfers between devices  71.2 us (43%)
  waiting for transfers between devices  58.2 us (35%)
  Pallas kernels  25 us (15%)
  local copies, waits for them, and re-layouts  10.1 us (6%)
    ppermute x21, starting transfers between devices, send(): return [lax.ppermute(part, axis, shifts[d]) for d, part in parts]  41.8 us
    ppermute x21, waiting for transfers between devices, send(): return [lax.ppermute(part, axis, shifts[d]) for d, part in parts]  32.7 us
    pallas_call x8, Pallas kernels, whole_kernel(): pl.pallas_call(lambda place, *refs: kernel(place, *refs[:count], *refs[co...  10.9 us
    unnamed x14, local copies, waits for them, and re-layouts  9.73 us
    pallas_call x1, Pallas kernels, update(): pl.pallas_call(update_kernel, out_shape=SDS((rows, columns), F32), in_spe...  9.37 us
    ppermute x2, waiting for transfers between devices, body(): inner = inner + lax.ppermute(inner, 'row', flip(d))  7.43 us
    ppermute x1, starting transfers between devices, body(): inner_other = lax.ppermute(inner, 'col', flip(1))  7.4 us
    ppermute x1, waiting for transfers between devices, body(): mine = jnp.stack([mine, lax.ppermute(mine, 'col', SWAP_ZLO)])  7.04 us
  transfers between devices with their start and end apart: 33, of which 19 were waited for; matrix products, arithmetic and copies ran while one was open for 0% of the time, Pallas kernels for 5%

profile of v1, /device:TPU:1, one launch (start us, length us, event | category | flops | bytes accessed | tf_op | source)
XLA Modules:
  0.0 165.1 jit_solution(11457178975144369421)
XLA Ops:
  1.4 2.2 %copy-done.4 = f32[1024,1024]{1,0:T(8,128)S(1)} copy-done((f32[1024,1024]{1,0:T(8,128)S(1)}, f32[1024,1024]{1,0:T(8,128)}, u32[]{:S(2)}) %copy-start.4) | copy-done | bytes 4194328
  3.6 4.7 %products.1 = (f32[320,256]{1,0:T(8,128)}, f32[320,256]{1,0:T(8,128)S(1)}, f32[320,256]{1,0:T(8,128)S(1)}, f32[320,256]{1,0:T(8,128)S(1)}, f32[80,256]{1,0:T(8,128)S(1)}) custom-call(s32[6]{0:T(128)S(1)} %stack.152.place, f32[320,1024]{1,0:T(8,128)S(1)} %bitcast.31, f32[1024,1024]{1,0:T(8,128)S(1)} %copy-done.4), custom_call_target="tpu_custom_call" | custom-call | flops 2013265920 | bytes 6815744 | tf_op jit(solution)/shard_map/products/pallas_call | solution.py:114
  8.3 3.6 %collective-permute-start = (f32[320,256]{1,0:T(8,128)}, f32[320,256]{1,0:T(8,128)S(1)}, u32[]{:S(2)}, u32[]{:S(2)}) collective-permute-start(f32[320,256]{1,0:T(8,128)} %get-tuple-element.25), channel_id=1, source_target_pairs={{0,32},{16,48},{32,0},{48,16},{64,96},{80,112},{96,64},{112,80},{1... | collective-permute-start | bytes 983048 | tf_op jit(solution)/shard_map/prod_sum_x/ppermute | solution.py:66
  12.2 2.4 %collective-permute-start.2 = (f32[320,256]{1,0:T(8,128)S(1)}, f32[320,256]{1,0:T(8,128)S(1)}, u32[]{:S(2)}, u32[]{:S(2)}) collective-permute-start(f32[320,256]{1,0:T(8,128)S(1)} %get-tuple-element.27), channel_id=1, source_target_pairs={{0,48},{16,0},{32,16},{48,32},{64,112},{80,64},{96,80},{112,96},{1... | collective-permute-start | bytes 983048 | tf_op jit(solution)/shard_map/prod_sum_x/ppermute | solution.py:66
  14.6 4.0 %collective-permute-done.refs_1_ = f32[320,256]{1,0:T(8,128)S(1)} collective-permute-done((f32[320,256]{1,0:T(8,128)}, f32[320,256]{1,0:T(8,128)S(1)}, u32[]{:S(2)}, u32[]{:S(2)}) %collective-permute-start) | collective-permute-done | bytes 327712 | tf_op jit(solution)/shard_map/prod_sum_x/ppermute | solution.py:66
  18.6 8.6 %collective-permute-done.1.refs_2_ = f32[320,256]{1,0:T(8,128)S(1)} collective-permute-done((f32[320,256]{1,0:T(8,128)S(1)}, f32[320,256]{1,0:T(8,128)S(1)}, u32[]{:S(2)}, u32[]{:S(2)}) %collective-permute-start.1) | collective-permute-done | bytes 327712 | tf_op jit(solution)/shard_map/prod_sum_x/ppermute | solution.py:66
  27.9 7.2 %collective-permute-start.3 = (f32[80,256]{1,0:T(8,128)S(1)}, f32[80,256]{1,0:T(8,128)S(1)}, u32[]{:S(2)}, u32[]{:S(2)}) collective-permute-start(f32[80,256]{1,0:T(8,128)S(1)} %get-tuple-element.29), channel_id=1, source_target_pairs={{0,128},{16,144},{32,160},{48,176},{64,192},{80,208},{96,224},{112... | collective-permute-start | bytes 245768 | tf_op jit(solution)/shard_map/prod_sum_z/ppermute | solution.py:66
  36.3 2.4 %collective-permute-start.5 = (f32[80,256]{1,0:T(8,128)S(1)}, f32[80,256]{1,0:T(8,128)S(1)}, u32[]{:S(2)}, u32[]{:S(2)}) collective-permute-start(f32[80,256]{1,0:T(8,128)S(1)} %get-tuple-element.31), channel_id=1, source_target_pairs={{0,192},{16,208},{32,224},{48,240},{64,0},{80,16},{96,32},{112,48}... | collective-permute-start | bytes 245768 | tf_op jit(solution)/shard_map/prod_sum_z/ppermute | solution.py:66
  38.7 3.2 %collective-permute-start.10 = (f32[80,256]{1,0:T(8,128)S(1)}, f32[80,256]{1,0:T(8,128)S(1)}, u32[]{:S(2)}, u32[]{:S(2)}) collective-permute-start(f32[80,256]{1,0:T(8,128)S(1)} %get-tuple-element.32), channel_id=1, source_target_pairs={{0,0},{1,64},{2,128},{3,192},{4,16},{5,80},{6,144},{7,208},{8,32},... | collective-permute-start | bytes 245768 | tf_op jit(solution)/shard_map/vec_turn/ppermute | solution.py:285
  43.8 4.2 %collective-permute-start.9 = (f32[80,256]{1,0:T(8,128)S(1)}, f32[80,256]{1,0:T(8,128)S(1)}, u32[]{:S(2)}, u32[]{:S(2)}) collective-permute-start(f32[80,256]{1,0:T(8,128)S(1)} %sum_z.1.refs_0_), channel_id=1, source_target_pairs={{0,0},{64,1},{128,2},{192,3},{16,4},{80,5},{144,6},{208,7},{32,8},... | collective-permute-start | bytes 245768 | tf_op jit(solution)/shard_map/prod_turn/ppermute | solution.py:298
  48.0 2.3 %collective-permute-start.8 = (f32[80,256]{1,0:T(8,128)S(1)}, f32[80,256]{1,0:T(8,128)S(1)}, u32[]{:S(2)}, u32[]{:S(2)}) collective-permute-start(f32[80,256]{1,0:T(8,128)S(1)} %sum_z.1.refs_0_), channel_id=1, source_target_pairs={{0,192},{16,208},{32,224},{48,240},{64,0},{80,16},{96,32},{112,48}... | collective-permute-start | bytes 245768 | tf_op jit(solution)/shard_map/prod_z/ppermute | solution.py:66
  50.3 2.1 %collective-permute-start.7 = (f32[80,256]{1,0:T(8,128)S(1)}, f32[80,256]{1,0:T(8,128)S(1)}, u32[]{:S(2)}, u32[]{:S(2)}) collective-permute-start(f32[80,256]{1,0:T(8,128)S(1)} %sum_z.1.refs_0_), channel_id=1, source_target_pairs={{0,128},{16,144},{32,160},{48,176},{64,192},{80,208},{96,224},{112... | collective-permute-start | bytes 245768 | tf_op jit(solution)/shard_map/prod_z/ppermute | solution.py:66
  52.4 2.0 %collective-permute-start.6 = (f32[80,256]{1,0:T(8,128)S(1)}, f32[80,256]{1,0:T(8,128)S(1)}, u32[]{:S(2)}, u32[]{:S(2)}) collective-permute-start(f32[80,256]{1,0:T(8,128)S(1)} %sum_z.1.refs_0_), channel_id=1, source_target_pairs={{0,64},{16,80},{32,96},{48,112},{64,128},{80,144},{96,160},{112,17... | collective-permute-start | bytes 245768 | tf_op jit(solution)/shard_map/prod_z/ppermute | solution.py:66
  59.9 10.0 %collective-permute-start.13 = (f32[320,256]{1,0:T(8,128)S(1)}, f32[320,256]{1,0:T(8,128)S(1)}, u32[]{:S(2)}, u32[]{:S(2)}) collective-permute-start(f32[320,256]{1,0:T(8,128)S(1)} %get-tuple-element.33.refs_0_), channel_id=1, source_target_pairs={{0,32},{16,48},{32,0},{48,16},{64,96},{80,112},{96,64},{112,80},{1... | collective-permute-start | bytes 983048 | tf_op jit(solution)/shard_map/prod_x/ppermute | solution.py:66
  72.9 2.4 %collective-permute-done.16.refs_3_ = f32[80,256]{1,0:T(8,128)S(1)} collective-permute-done((f32[80,256]{1,0:T(8,128)S(1)}, f32[80,256]{1,0:T(8,128)S(1)}, u32[]{:S(2)}, u32[]{:S(2)}) %collective-permute-start.16) | collective-permute-done | bytes 81952 | tf_op jit(solution)/shard_map/row_y/ppermute | solution.py:66
  75.3 2.7 %collective-permute-done.15.refs_2_ = f32[80,256]{1,0:T(8,128)S(1)} collective-permute-done((f32[80,256]{1,0:T(8,128)S(1)}, f32[80,256]{1,0:T(8,128)S(1)}, u32[]{:S(2)}, u32[]{:S(2)}) %collective-permute-start.15) | collective-permute-done | bytes 81952 | tf_op jit(solution)/shard_map/row_y/ppermute | solution.py:66
  78.0 3.0 %collective-permute-done.14.refs_1_ = f32[80,256]{1,0:T(8,128)S(1)} collective-permute-done((f32[80,256]{1,0:T(8,128)S(1)}, f32[80,256]{1,0:T(8,128)S(1)}, u32[]{:S(2)}, u32[]{:S(2)}) %collective-permute-start.14) | collective-permute-done | bytes 81952 | tf_op jit(solution)/shard_map/row_y/ppermute | solution.py:66
  83.2 5.7 %collective-permute-done.18.refs_6_ = f32[80,256]{1,0:T(8,128)S(1)} collective-permute-done((f32[80,256]{1,0:T(8,128)S(1)}, f32[80,256]{1,0:T(8,128)S(1)}, u32[]{:S(2)}, u32[]{:S(2)}) %collective-permute-start.18) | collective-permute-done | bytes 81952 | tf_op jit(solution)/shard_map/vec_z/ppermute | solution.py:66
  90.3 5.2 %collective-permute-start.29 = (f32[4,80,256]{2,1,0:T(8,128)S(1)}, f32[4,80,256]{2,1,0:T(8,128)S(1)}, u32[]{:S(2)}, u32[]{:S(2)}) collective-permute-start(f32[4,80,256]{2,1,0:T(8,128)S(1)} %get-tuple-element.40), channel_id=1, source_target_pairs={{0,2},{1,3},{2,0},{3,1},{4,6},{5,7},{6,4},{7,5},{8,10},{9,11},{10,... | collective-permute-start | bytes 983048 | tf_op jit(solution)/shard_map/row_zlo/ppermute | solution.py:318
  95.5 7.0 %collective-permute-done.29 = f32[4,80,256]{2,1,0:T(8,128)S(1)} collective-permute-done((f32[4,80,256]{2,1,0:T(8,128)S(1)}, f32[4,80,256]{2,1,0:T(8,128)S(1)}, u32[]{:S(2)}, u32[]{:S(2)}) %collective-permute-start.29) | collective-permute-done | bytes 327712 | tf_op jit(solution)/shard_map/row_zlo/ppermute | solution.py:318
  104.3 2.9 %collective-permute-done.20 = f32[80,80]{1,0:T(8,128)S(1)} collective-permute-done((f32[80,80]{1,0:T(8,128)S(1)}, f32[80,80]{1,0:T(8,128)S(1)}, u32[]{:S(2)}, u32[]{:S(2)}) %collective-permute-start.20) | collective-permute-done | bytes 25632 | tf_op jit(solution)/shard_map/inner_x/ppermute | solution.py:327
  108.8 2.7 %collective-permute-done.21.refs_1_ = f32[80,80]{1,0:T(8,128)S(1)} collective-permute-done((f32[80,80]{1,0:T(8,128)S(1)}, f32[80,80]{1,0:T(8,128)S(1)}, u32[]{:S(2)}, u32[]{:S(2)}) %collective-permute-start.21) | collective-permute-done | bytes 25632 | tf_op jit(solution)/shard_map/inner_x/ppermute | solution.py:328
  113.6 3.0 %collective-permute-done.25 = f32[80,80]{1,0:T(8,128)S(1)} collective-permute-done((f32[80,80]{1,0:T(8,128)S(1)}, f32[80,80]{1,0:T(8,128)S(1)}, u32[]{:S(2)}, u32[]{:S(2)}) %collective-permute-start.25) | collective-permute-done | bytes 25632 | tf_op jit(solution)/shard_map/inner_z/ppermute | solution.py:334
  116.6 2.3 %collective-permute-start.26 = (f32[80,80]{1,0:T(8,128)S(1)}, f32[80,80]{1,0:T(8,128)S(1)}, u32[]{:S(2)}, u32[]{:S(2)}) collective-permute-start(f32[80,80]{1,0:T(8,128)S(1)} %add.144), channel_id=1, source_target_pairs={{0,128},{16,144},{32,160},{48,176},{64,192},{80,208},{96,224},{112... | collective-permute-start | bytes 76808 | tf_op jit(solution)/shard_map/inner_z/ppermute | solution.py:334
  118.9 4.4 %collective-permute-done.26 = f32[80,80]{1,0:T(8,128)S(1)} collective-permute-done((f32[80,80]{1,0:T(8,128)S(1)}, f32[80,80]{1,0:T(8,128)S(1)}, u32[]{:S(2)}, u32[]{:S(2)}) %collective-permute-start.26) | collective-permute-done | bytes 25632 | tf_op jit(solution)/shard_map/inner_z/ppermute | solution.py:334
  123.4 3.1 %collective-permute-done.27 = f32[80,80]{1,0:T(8,128)S(1)} collective-permute-done((f32[80,80]{1,0:T(8,128)S(1)}, f32[80,80]{1,0:T(8,128)S(1)}, u32[]{:S(2)}, u32[]{:S(2)}) %collective-permute-start.27) | collective-permute-done | bytes 25632 | tf_op jit(solution)/shard_map/inner_y/ppermute | solution.py:336
  127.7 2.6 %left.1.refs_2_.refs_10_ = bf16[1024,1920]{1,0:T(8,128)(2,1)S(1)} custom-call(s32[8]{0:T(128)S(1)} %stack.169.place, f32[320,1024]{1,0:T(8,128)S(1)} %bitcast.33, f32[2,4,80,256]{3,2,1,0:T(8,128)S(1)} %pad_maximum_fusion.refs_1_, f32[2,4,80,256]{3,2,1,0:T(8,128)} %collective-permute-done.30.refs_2_), custom_call_target="tpu_custom_call" | custom-call | bytes 6553600 | tf_op jit(solution)/shard_map/left/pallas_call | solution.py:72
  139.1 7.4 %collective-permute-start.32 = (f32[2,4,80,80]{3,2,1,0:T(8,128)S(1)}, f32[2,4,80,80]{3,2,1,0:T(8,128)S(1)}, u32[]{:S(2)}, u32[]{:S(2)}) collective-permute-start(f32[2,4,80,80]{3,2,1,0:T(8,128)S(1)} %pad_maximum_fusion.1.refs_0_), channel_id=1, source_target_pairs={{0,1},{1,0},{2,3},{3,2},{4,5},{5,4},{6,7},{7,6},{8,9},{9,8},{10,11... | collective-permute-start | bytes 614408 | tf_op jit(solution)/shard_map/inner_core/ppermute | solution.py:344
  147.8 3.4 %factor.1 = (bf16[320,1920]{1,0:T(8,128)(2,1)S(1)}, bf16[320,960]{1,0:T(8,128)(2,1)S(1)}) custom-call(s32[8]{0:T(128)S(1)} %stack.165.place, f32[2,4,80,80]{3,2,1,0:T(8,128)S(1)} %pad_maximum_fusion.1.refs_0_, f32[2,4,80,80]{3,2,1,0:T(8,128)S(1)} %collective-permute-done.32.refs_1_, f32[5,64,64]{2,1,0:T(8,128)S(1)} %copy-done.6), custom_call_target="tpu_custom_call" | custom-call | bytes 2334720 | tf_op jit(solution)/shard_map/factor/pallas_call | solution.py:72
  151.2 2.1 %copy-done.1 = bf16[1024,1920]{1,0:T(8,128)(2,1)S(1)} copy-done((bf16[1024,1920]{1,0:T(8,128)(2,1)S(1)}, bf16[1024,1920]{1,0:T(8,128)(2,1)}, u32[]{:S(2)}) %copy-start.1) | copy-done | bytes 3932184
  153.4 2.2 %copy-done.5 = f32[1024,1024]{1,0:T(8,128)S(1)} copy-done((f32[1024,1024]{1,0:T(8,128)S(1)}, f32[1024,1024]{1,0:T(8,128)}, u32[]{:S(2)}) %copy-start.5) | copy-done | bytes 4194328
  155.5 9.4 %update.1 = f32[1024,1024]{1,0:T(8,128)} custom-call(s32[4]{0:T(128)S(1)} %pad_add_fusion.place, f32[320,256]{1,0:T(8,128)S(1)} %get-tuple-element.33.refs_0_, f32[320,256]{1,0:T(8,128)S(1)} %collective-permute-done.11.refs_9_.refs_1_, f32[320,256]{1,0:T(8,128)S(1)} %collective-permute-done.12.refs_10_.refs_2_, ...), custom_call_target="tpu_custom_call" | custom-call | flops 4026531840 | bytes 8388608 | tf_op jit(solution)/shard_map/update/pallas_call | solution.py:245
  (70 shorter events, 34.2 us)
Async XLA Ops:
  8.3 10.4 %collective-permute-start = (f32[320,256]{1,0:T(8,128)}, f32[320,256]{1,0:T(8,128)S(1)}, u32[]{:S(2)}, u32[]{:S(2)}) collective-permute-start(f32[320,256]{1,0:T(8,128)} %get-tuple-element.25), channel_id=1, source_target_pairs={{0,32},{16,48},{32,0},{48,16},{64,96},{80,112},{96,64},{112,80},{1... | collective-permute-start | bytes 983048 | tf_op jit(solution)/shard_map/prod_sum_x/ppermute | solution.py:66
  11.8 15.4 %collective-permute-start.1 = (f32[320,256]{1,0:T(8,128)S(1)}, f32[320,256]{1,0:T(8,128)S(1)}, u32[]{:S(2)}, u32[]{:S(2)}) collective-permute-start(f32[320,256]{1,0:T(8,128)S(1)} %get-tuple-element.26), channel_id=1, source_target_pairs={{0,16},{16,32},{32,48},{48,0},{64,80},{80,96},{96,112},{112,64},{1... | collective-permute-start | bytes 983048 | tf_op jit(solution)/shard_map/prod_sum_x/ppermute | solution.py:66
  12.2 15.1 %collective-permute-start.2 = (f32[320,256]{1,0:T(8,128)S(1)}, f32[320,256]{1,0:T(8,128)S(1)}, u32[]{:S(2)}, u32[]{:S(2)}) collective-permute-start(f32[320,256]{1,0:T(8,128)S(1)} %get-tuple-element.27), channel_id=1, source_target_pairs={{0,48},{16,0},{32,16},{48,32},{64,112},{80,64},{96,80},{112,96},{1... | collective-permute-start | bytes 983048 | tf_op jit(solution)/shard_map/prod_sum_x/ppermute | solution.py:66
  27.9 14.0 %collective-permute-start.3 = (f32[80,256]{1,0:T(8,128)S(1)}, f32[80,256]{1,0:T(8,128)S(1)}, u32[]{:S(2)}, u32[]{:S(2)}) collective-permute-start(f32[80,256]{1,0:T(8,128)S(1)} %get-tuple-element.29), channel_id=1, source_target_pairs={{0,128},{16,144},{32,160},{48,176},{64,192},{80,208},{96,224},{112... | collective-permute-start | bytes 245768 | tf_op jit(solution)/shard_map/prod_sum_z/ppermute | solution.py:66
  35.1 6.8 %collective-permute-start.4 = (f32[80,256]{1,0:T(8,128)S(1)}, f32[80,256]{1,0:T(8,128)S(1)}, u32[]{:S(2)}, u32[]{:S(2)}) collective-permute-start(f32[80,256]{1,0:T(8,128)S(1)} %get-tuple-element.30), channel_id=1, source_target_pairs={{0,64},{16,80},{32,96},{48,112},{64,128},{80,144},{96,160},{112,17... | collective-permute-start | bytes 245768 | tf_op jit(solution)/shard_map/prod_sum_z/ppermute | solution.py:66
  36.3 6.9 %collective-permute-start.5 = (f32[80,256]{1,0:T(8,128)S(1)}, f32[80,256]{1,0:T(8,128)S(1)}, u32[]{:S(2)}, u32[]{:S(2)}) collective-permute-start(f32[80,256]{1,0:T(8,128)S(1)} %get-tuple-element.31), channel_id=1, source_target_pairs={{0,192},{16,208},{32,224},{48,240},{64,0},{80,16},{96,32},{112,48}... | collective-permute-start | bytes 245768 | tf_op jit(solution)/shard_map/prod_sum_z/ppermute | solution.py:66
  38.7 15.7 %collective-permute-start.10 = (f32[80,256]{1,0:T(8,128)S(1)}, f32[80,256]{1,0:T(8,128)S(1)}, u32[]{:S(2)}, u32[]{:S(2)}) collective-permute-start(f32[80,256]{1,0:T(8,128)S(1)} %get-tuple-element.32), channel_id=1, source_target_pairs={{0,0},{1,64},{2,128},{3,192},{4,16},{5,80},{6,144},{7,208},{8,32},... | collective-permute-start | bytes 245768 | tf_op jit(solution)/shard_map/vec_turn/ppermute | solution.py:285
  43.8 10.6 %collective-permute-start.9 = (f32[80,256]{1,0:T(8,128)S(1)}, f32[80,256]{1,0:T(8,128)S(1)}, u32[]{:S(2)}, u32[]{:S(2)}) collective-permute-start(f32[80,256]{1,0:T(8,128)S(1)} %sum_z.1.refs_0_), channel_id=1, source_target_pairs={{0,0},{64,1},{128,2},{192,3},{16,4},{80,5},{144,6},{208,7},{32,8},... | collective-permute-start | bytes 245768 | tf_op jit(solution)/shard_map/prod_turn/ppermute | solution.py:298
  48.0 7.9 %collective-permute-start.8 = (f32[80,256]{1,0:T(8,128)S(1)}, f32[80,256]{1,0:T(8,128)S(1)}, u32[]{:S(2)}, u32[]{:S(2)}) collective-permute-start(f32[80,256]{1,0:T(8,128)S(1)} %sum_z.1.refs_0_), channel_id=1, source_target_pairs={{0,192},{16,208},{32,224},{48,240},{64,0},{80,16},{96,32},{112,48}... | collective-permute-start | bytes 245768 | tf_op jit(solution)/shard_map/prod_z/ppermute | solution.py:66
  50.3 7.3 %collective-permute-start.7 = (f32[80,256]{1,0:T(8,128)S(1)}, f32[80,256]{1,0:T(8,128)S(1)}, u32[]{:S(2)}, u32[]{:S(2)}) collective-permute-start(f32[80,256]{1,0:T(8,128)S(1)} %sum_z.1.refs_0_), channel_id=1, source_target_pairs={{0,128},{16,144},{32,160},{48,176},{64,192},{80,208},{96,224},{112... | collective-permute-start | bytes 245768 | tf_op jit(solution)/shard_map/prod_z/ppermute | solution.py:66
  52.4 6.9 %collective-permute-start.6 = (f32[80,256]{1,0:T(8,128)S(1)}, f32[80,256]{1,0:T(8,128)S(1)}, u32[]{:S(2)}, u32[]{:S(2)}) collective-permute-start(f32[80,256]{1,0:T(8,128)S(1)} %sum_z.1.refs_0_), channel_id=1, source_target_pairs={{0,64},{16,80},{32,96},{48,112},{64,128},{80,144},{96,160},{112,17... | collective-permute-start | bytes 245768 | tf_op jit(solution)/shard_map/prod_z/ppermute | solution.py:66
  59.9 29.1 %collective-permute-start.13 = (f32[320,256]{1,0:T(8,128)S(1)}, f32[320,256]{1,0:T(8,128)S(1)}, u32[]{:S(2)}, u32[]{:S(2)}) collective-permute-start(f32[320,256]{1,0:T(8,128)S(1)} %get-tuple-element.33.refs_0_), channel_id=1, source_target_pairs={{0,32},{16,48},{32,0},{48,16},{64,96},{80,112},{96,64},{112,80},{1... | collective-permute-start | bytes 983048 | tf_op jit(solution)/shard_map/prod_x/ppermute | solution.py:66
  69.8 19.2 %collective-permute-start.12 = (f32[320,256]{1,0:T(8,128)S(1)}, f32[320,256]{1,0:T(8,128)S(1)}, u32[]{:S(2)}, u32[]{:S(2)}) collective-permute-start(f32[320,256]{1,0:T(8,128)S(1)} %get-tuple-element.33.refs_0_), channel_id=1, source_target_pairs={{0,48},{16,0},{32,16},{48,32},{64,112},{80,64},{96,80},{112,96},{1... | collective-permute-start | bytes 983048 | tf_op jit(solution)/shard_map/prod_x/ppermute | solution.py:66
  69.9 19.1 %collective-permute-start.11 = (f32[320,256]{1,0:T(8,128)S(1)}, f32[320,256]{1,0:T(8,128)S(1)}, u32[]{:S(2)}, u32[]{:S(2)}) collective-permute-start(f32[320,256]{1,0:T(8,128)S(1)} %get-tuple-element.33.refs_0_), channel_id=1, source_target_pairs={{0,16},{16,32},{32,48},{48,0},{64,80},{80,96},{96,112},{112,64},{1... | collective-permute-start | bytes 983048 | tf_op jit(solution)/shard_map/prod_x/ppermute | solution.py:66
  71.3 4.0 %collective-permute-start.16 = (f32[80,256]{1,0:T(8,128)S(1)}, f32[80,256]{1,0:T(8,128)S(1)}, u32[]{:S(2)}, u32[]{:S(2)}) collective-permute-start(f32[80,256]{1,0:T(8,128)S(1)} %get-tuple-element.34.refs_0_), channel_id=1, source_target_pairs={{0,12},{1,13},{2,14},{3,15},{4,0},{5,1},{6,2},{7,3},{8,4},{9,5},{1... | collective-permute-start | bytes 245768 | tf_op jit(solution)/shard_map/row_y/ppermute | solution.py:66
  72.9 5.1 %collective-permute-start.15 = (f32[80,256]{1,0:T(8,128)S(1)}, f32[80,256]{1,0:T(8,128)S(1)}, u32[]{:S(2)}, u32[]{:S(2)}) collective-permute-start(f32[80,256]{1,0:T(8,128)S(1)} %get-tuple-element.34.refs_0_), channel_id=1, source_target_pairs={{0,8},{1,9},{2,10},{3,11},{4,12},{5,13},{6,14},{7,15},{8,0},{9,1},... | collective-permute-start | bytes 245768 | tf_op jit(solution)/shard_map/row_y/ppermute | solution.py:66
  75.3 5.7 %collective-permute-start.14 = (f32[80,256]{1,0:T(8,128)S(1)}, f32[80,256]{1,0:T(8,128)S(1)}, u32[]{:S(2)}, u32[]{:S(2)}) collective-permute-start(f32[80,256]{1,0:T(8,128)S(1)} %get-tuple-element.34.refs_0_), channel_id=1, source_target_pairs={{0,4},{1,5},{2,6},{3,7},{4,8},{5,9},{6,10},{7,11},{8,12},{9,13},{1... | collective-permute-start | bytes 245768 | tf_op jit(solution)/shard_map/row_y/ppermute | solution.py:66
  78.0 4.5 %collective-permute-start.19 = (f32[80,256]{1,0:T(8,128)S(1)}, f32[80,256]{1,0:T(8,128)S(1)}, u32[]{:S(2)}, u32[]{:S(2)}) collective-permute-start(f32[80,256]{1,0:T(8,128)S(1)} %get-tuple-element.35.refs_4_), channel_id=1, source_target_pairs={{0,192},{16,208},{32,224},{48,240},{64,0},{80,16},{96,32},{112,48}... | collective-permute-start | bytes 245768 | tf_op jit(solution)/shard_map/vec_z/ppermute | solution.py:66
  80.9 8.0 %collective-permute-start.18 = (f32[80,256]{1,0:T(8,128)S(1)}, f32[80,256]{1,0:T(8,128)S(1)}, u32[]{:S(2)}, u32[]{:S(2)}) collective-permute-start(f32[80,256]{1,0:T(8,128)S(1)} %get-tuple-element.35.refs_4_), channel_id=1, source_target_pairs={{0,128},{16,144},{32,160},{48,176},{64,192},{80,208},{96,224},{112... | collective-permute-start | bytes 245768 | tf_op jit(solution)/shard_map/vec_z/ppermute | solution.py:66
  82.4 6.5 %collective-permute-start.17 = (f32[80,256]{1,0:T(8,128)S(1)}, f32[80,256]{1,0:T(8,128)S(1)}, u32[]{:S(2)}, u32[]{:S(2)}) collective-permute-start(f32[80,256]{1,0:T(8,128)S(1)} %get-tuple-element.35.refs_4_), channel_id=1, source_target_pairs={{0,64},{16,80},{32,96},{48,112},{64,128},{80,144},{96,160},{112,17... | collective-permute-start | bytes 245768 | tf_op jit(solution)/shard_map/vec_z/ppermute | solution.py:66
  90.3 12.3 %collective-permute-start.29 = (f32[4,80,256]{2,1,0:T(8,128)S(1)}, f32[4,80,256]{2,1,0:T(8,128)S(1)}, u32[]{:S(2)}, u32[]{:S(2)}) collective-permute-start(f32[4,80,256]{2,1,0:T(8,128)S(1)} %get-tuple-element.40), channel_id=1, source_target_pairs={{0,2},{1,3},{2,0},{3,1},{4,6},{5,7},{6,4},{7,5},{8,10},{9,11},{10,... | collective-permute-start | bytes 983048 | tf_op jit(solution)/shard_map/row_zlo/ppermute | solution.py:318
  102.6 25.1 %collective-permute-start.30 = (f32[2,4,80,256]{3,2,1,0:T(8,128)S(1)}, f32[2,4,80,256]{3,2,1,0:T(8,128)}, u32[]{:S(2)}, u32[]{:S(2)}) collective-permute-start(f32[2,4,80,256]{3,2,1,0:T(8,128)S(1)} %pad_maximum_fusion.refs_1_), channel_id=1, source_target_pairs={{0,1},{1,0},{2,3},{3,2},{4,5},{5,4},{6,7},{7,6},{8,9},{9,8},{10,11... | collective-permute-start | bytes 1966088 | tf_op jit(solution)/shard_map/row_core/ppermute | solution.py:320
  107.2 4.4 %collective-permute-start.21 = (f32[80,80]{1,0:T(8,128)S(1)}, f32[80,80]{1,0:T(8,128)S(1)}, u32[]{:S(2)}, u32[]{:S(2)}) collective-permute-start(f32[80,80]{1,0:T(8,128)S(1)} %add.137.refs_0_), channel_id=1, source_target_pairs={{0,32},{16,48},{32,0},{48,16},{64,96},{80,112},{96,64},{112,80},{1... | collective-permute-start | bytes 76808 | tf_op jit(solution)/shard_map/inner_x/ppermute | solution.py:328
  112.9 3.8 %collective-permute-start.25 = (f32[80,80]{1,0:T(8,128)S(1)}, f32[80,80]{1,0:T(8,128)S(1)}, u32[]{:S(2)}, u32[]{:S(2)}) collective-permute-start(f32[80,80]{1,0:T(8,128)S(1)} %get-tuple-element.39), channel_id=1, source_target_pairs={{0,64},{16,80},{32,96},{48,112},{64,0},{80,16},{96,32},{112,48},{1... | collective-permute-start | bytes 76808 | tf_op jit(solution)/shard_map/inner_z/ppermute | solution.py:334
  116.6 6.8 %collective-permute-start.26 = (f32[80,80]{1,0:T(8,128)S(1)}, f32[80,80]{1,0:T(8,128)S(1)}, u32[]{:S(2)}, u32[]{:S(2)}) collective-permute-start(f32[80,80]{1,0:T(8,128)S(1)} %add.144), channel_id=1, source_target_pairs={{0,128},{16,144},{32,160},{48,176},{64,192},{80,208},{96,224},{112... | collective-permute-start | bytes 76808 | tf_op jit(solution)/shard_map/inner_z/ppermute | solution.py:334
  123.4 3.1 %collective-permute-start.27 = (f32[80,80]{1,0:T(8,128)S(1)}, f32[80,80]{1,0:T(8,128)S(1)}, u32[]{:S(2)}, u32[]{:S(2)}) collective-permute-start(f32[80,80]{1,0:T(8,128)S(1)} %add.145), channel_id=1, source_target_pairs={{0,4},{1,5},{2,6},{3,7},{4,0},{5,1},{6,2},{7,3},{8,12},{9,13},{10,... | collective-permute-start | bytes 76808 | tf_op jit(solution)/shard_map/inner_y/ppermute | solution.py:336
  126.5 5.0 %collective-permute-start.28 = (f32[2,80,80]{2,1,0:T(8,128)S(1)}, f32[2,80,80]{2,1,0:T(8,128)S(1)}, u32[]{:S(2)}, u32[]{:S(2)}) collective-permute-start(f32[2,80,80]{2,1,0:T(8,128)S(1)} %pad_maximum_fusion.2.refs_0_), channel_id=1, source_target_pairs={{0,8},{1,9},{2,10},{3,11},{4,12},{5,13},{6,14},{7,15},{8,0},{9,1},... | collective-permute-start | bytes 153608 | tf_op jit(solution)/shard_map/inner_y/ppermute | solution.py:338
  134.0 5.1 %collective-permute-start.31 = (f32[4,80,80]{2,1,0:T(8,128)S(1)}, f32[4,80,80]{2,1,0:T(8,128)S(1)}, u32[]{:S(2)}, u32[]{:S(2)}) collective-permute-start(f32[4,80,80]{2,1,0:T(8,128)S(1)} %inner_y.1), channel_id=1, source_target_pairs={{0,2},{1,3},{2,0},{3,1},{4,6},{5,7},{6,4},{7,5},{8,10},{9,11},{10,... | collective-permute-start | bytes 307208 | tf_op jit(solution)/shard_map/inner_zlo/ppermute | solution.py:342
  135.8 15.4 %collective-permute-start.24 = (f32[320,256]{1,0:T(8,128)}, f32[320,256]{1,0:T(8,128)S(1)}, u32[]{:S(2)}, u32[]{:S(2)}) collective-permute-start(f32[320,256]{1,0:T(8,128)} %get-tuple-element.38.refs_4_), channel_id=1, source_target_pairs={{0,32},{16,48},{32,0},{48,16},{64,96},{80,112},{96,64},{112,80},{1... | collective-permute-start | bytes 983048 | tf_op jit(solution)/shard_map/vec_x/ppermute | solution.py:66
  137.6 13.6 %collective-permute-start.23 = (f32[320,256]{1,0:T(8,128)}, f32[320,256]{1,0:T(8,128)S(1)}, u32[]{:S(2)}, u32[]{:S(2)}) collective-permute-start(f32[320,256]{1,0:T(8,128)} %get-tuple-element.38.refs_4_), channel_id=1, source_target_pairs={{0,48},{16,0},{32,16},{48,32},{64,112},{80,64},{96,80},{112,96},{1... | collective-permute-start | bytes 983048 | tf_op jit(solution)/shard_map/vec_x/ppermute | solution.py:66
  138.9 12.3 %collective-permute-start.22 = (f32[320,256]{1,0:T(8,128)}, f32[320,256]{1,0:T(8,128)S(1)}, u32[]{:S(2)}, u32[]{:S(2)}) collective-permute-start(f32[320,256]{1,0:T(8,128)} %get-tuple-element.38.refs_4_), channel_id=1, source_target_pairs={{0,16},{16,32},{32,48},{48,0},{64,80},{80,96},{96,112},{112,64},{1... | collective-permute-start | bytes 983048 | tf_op jit(solution)/shard_map/vec_x/ppermute | solution.py:66
  139.1 8.7 %collective-permute-start.32 = (f32[2,4,80,80]{3,2,1,0:T(8,128)S(1)}, f32[2,4,80,80]{3,2,1,0:T(8,128)S(1)}, u32[]{:S(2)}, u32[]{:S(2)}) collective-permute-start(f32[2,4,80,80]{3,2,1,0:T(8,128)S(1)} %pad_maximum_fusion.1.refs_0_), channel_id=1, source_target_pairs={{0,1},{1,0},{2,3},{3,2},{4,5},{5,4},{6,7},{7,6},{8,9},{9,8},{10,11... | collective-permute-start | bytes 614408 | tf_op jit(solution)/shard_map/inner_core/ppermute | solution.py:344
  (8 other events, 115.4 us)

commit v2 on v1

v2 whole, which is shorter than its diff:
```python
import jax
import jax.numpy as jnp
from jax import lax
from jax.experimental import pallas as pl
from jax.experimental.pallas import tpu as pltpu
from jax.sharding import PartitionSpec as P

HIGH = lax.Precision.HIGH
HIGHEST = lax.Precision.HIGHEST
F32 = jnp.float32
BF16 = jnp.bfloat16
SDS = jax.ShapeDtypeStruct

SHIFT_X = {d: [(i, (i // 4) * 4 + (i + d) % 4) for i in range(16)] for d in (1, 2, 3)}
SHIFT_Z = {d: [(i, (i + 4 * d) % 16) for i in range(16)] for d in (1, 2, 3)}
SHIFT_Y = SHIFT_Z
SWAP_ZLO = [(i, i ^ 2) for i in range(16)]
SWAP_CORE = [(i, i ^ 1) for i in range(16)]
TO_COLUMN = [(c * 16 + 4 * x + z, (z * 4 + x) * 16 + c) for c in range(16) for x in range(4) for z in range(4)]
TO_ROW = [(b, a) for a, b in TO_COLUMN]
EVERYWHERE = ("row", "col")


def flip(bit):
    return [(i, i ^ bit) for i in range(16)]


def dot(a, b, da, db, precision):
    return lax.dot_general(
        a, b, (((da,), (db,)), ((), ())), precision=precision, preferred_element_type=F32
    )


def split(a):
    high = a.astype(BF16)
    return high, (a - high.astype(F32)).astype(BF16)


def wide(a):
    high, low = split(a)
    return jnp.concatenate([high, low, high], axis=1)


def tall(a):
    high, low = split(a)
    return jnp.concatenate([high, high, low], axis=0)


def mul(a, b):
    return jnp.dot(a, b, preferred_element_type=F32)


def dot3(a, b, da, db):
    dims = (((da,), (db,)), ((), ()))
    (ah, al), (bh, bl) = a, b
    out = lax.dot_general(ah, bh, dims, preferred_element_type=F32)
    out += lax.dot_general(ah, bl, dims, preferred_element_type=F32)
    return out + lax.dot_general(al, bh, dims, preferred_element_type=F32)


def piece(a, index, size, dim):
    return lax.dynamic_slice_in_dim(a, index * size, size, dim)


def send(parts, axis, shifts):
    return [lax.ppermute(part, axis, shifts[d]) for d, part in parts]


def whole_kernel(kernel, shapes, place, *operands, scratch=(), flops=0, after=()):
    size = 4 * sum(a.size for a in operands) + sum(s.size * s.dtype.itemsize for s in shapes)
    count = len(operands)
    return pl.pallas_call(
        lambda place, *refs: kernel(place, *refs[:count], *refs[count + len(after) :]),
        out_shape=list(shapes),
        in_specs=[pl.BlockSpec(memory_space=pltpu.SMEM)]
        + [pl.BlockSpec(memory_space=pltpu.VMEM)] * len(operands)
        + [pl.BlockSpec(memory_space=pl.ANY)] * len(after),
        out_specs=[pl.BlockSpec(memory_space=pltpu.VMEM)] * len(shapes),
        scratch_shapes=list(scratch),
        compiler_params=pltpu.CompilerParams(vmem_limit_bytes=20 * 2**20),
        cost_estimate=pl.CostEstimate(flops=flops, bytes_accessed=size, transcendentals=0),
    )(place, *operands, *after)


def at(place_ref, index, size):
    return pl.ds(pl.multiple_of(place_ref[index] * size, size), size)


def quarter_product_kernel(place, vec_ref, mat_ref, *rest):
    outs, total_ref = rest[:4], rest[4]
    step = pl.program_id(0)
    rank, lanes = outs[0].shape
    vec_high, vec_low = split(vec_ref[...])
    high, low = split(mat_ref[...])
    both = mul(jnp.concatenate([vec_high, vec_low], axis=0), high)
    value = both[:rank] + both[rank:] + mul(vec_high, low)

    @pl.when(step == 0)
    def _():
        total_ref[...] = value

    @pl.when(step > 0)
    def _():
        total_ref[...] += value

    @pl.when(step == pl.num_programs(0) - 1)
    def _():
        for k in range(4):
            outs[k][...] = total_ref[:, at(place, k, lanes)]


def quarter_products(place, vectors, matrix):
    rank, rows = vectors.shape
    columns = matrix.shape[1]
    shape = SDS((rank, columns // 4), F32)
    depth = rows // 4
    return pl.pallas_call(
        quarter_product_kernel,
        out_shape=[shape] * 4,
        grid_spec=pltpu.PrefetchScalarGridSpec(
            num_scalar_prefetch=1,
            grid=(4,),
            in_specs=[
                pl.BlockSpec((rank, depth), lambda i, place: (0, i)),
                pl.BlockSpec((depth, columns), lambda i, place: (i, 0)),
            ],
            out_specs=[pl.BlockSpec(shape.shape, lambda i, place: (0, 0))] * 4,
            scratch_shapes=[pltpu.VMEM((rank, columns), F32)],
        ),
        compiler_params=pltpu.CompilerParams(vmem_limit_bytes=60 * 2**20),
        cost_estimate=pl.CostEstimate(
            flops=6 * rank * rows * rows, bytes_accessed=4 * (2 * rank * rows + rows * rows), transcendentals=0
        ),
    )(place, vectors, matrix)


def sum_x_kernel(place, p0, p1, p2, p3, *rest):
    outs, prod_ref = rest[:4], rest[4]
    prod_ref[...] = p0[...] + p1[...] + p2[...] + p3[...]
    for d in range(4):
        outs[d][...] = prod_ref[at(place, d, outs[d].shape[0])]


def sum_z_kernel(place, p0, p1, p2, p3, vec_ref, pair_ref, sum_ref):
    size = sum_ref.shape[0]
    total = p0[...] + p1[...] + p2[...] + p3[...]
    sum_ref[...] = total
    pair_ref[:size] = total
    pair_ref[size:] = vec_ref[...]


def join_kernel(width, place, *refs):
    (mine, left, right, prod_two, vec_two), other_ref, vec_ref = refs[:5], refs[5], refs[6]
    both_ref, pass_ref, pieces, inner_ref = refs[7], refs[8], refs[9:13], refs[13]
    size, lanes = other_ref.shape
    rank = vec_ref.shape[0]
    for d, (prod, vec) in enumerate(
        ((mine[:size], mine[size:]), (left[:size], left[size:]), (prod_two[...], vec_two[...]),
         (right[:size], right[size:]))
    ):
        both_ref[at(place, d, size)] = prod
        both_ref[at(place, 8 + d, size)] = vec
    pass_ref[...] = other_ref[...]
    here = at(place, 4, lanes)
    vec = split(vec_ref[:, here])
    inner = dot3(vec, split(other_ref[...]), 1, 1)
    gram = dot3(vec, split(vec_ref[at(place, 5, size), here]), 1, 1)
    down = lax.broadcasted_iota(jnp.int32, inner.shape, 0) // width
    over = (place[5] * size + lax.broadcasted_iota(jnp.int32, inner.shape, 1)) // width
    inner_ref[...] = jnp.where(over >= down, inner, gram)
    for d in range(4):
        pieces[d][...] = inner_ref[at(place, 12 + d, size)]


def sum_y_kernel(place, a, b, c, d, p0, p1, p2, p3, sum_ref, mine_ref):
    sum_ref[...] = a[...] + b[...] + c[...] + d[...]
    for d, part in enumerate((p0, p1, p2, p3)):
        mine_ref[d] = part[...]


def add_z_kernel(place, a, b, c, d, mine, other, left_ref, right_ref, sum_ref, both_ref, prod_ref, vec_ref):
    rank = prod_ref.shape[0]
    sum_ref[...] = a[...] + b[...] + c[...] + d[...]
    both_ref[0] = mine[...]
    both_ref[1] = other[...]
    prod_ref[...] = left_ref[:rank]
    vec_ref[...] = right_ref[rank:]


def add_x_kernel(place, a, b, c, d, prod_ref, vec_ref, sum_ref, prod_out, vec_out):
    sum_ref[...] = a[...] + b[...] + c[...] + d[...]
    prod_out[...] = prod_ref[...]
    vec_out[...] = vec_ref[...]


def factor_kernel(place, mine_ref, other_ref, factors_ref, *rest):
    first_ref, second_ref, factor_ref, strip_ref, both_ref = rest
    panels, width, _ = factors_ref.shape
    rank = panels * width
    size = mine_ref.shape[2]
    for k, ref in enumerate((mine_ref, other_ref)):
        for l in range(2):
            for d in range(4):
                strip_ref[place[2 * k + l], at(place, 4 + d, size)] = ref[l, d]
    for q in range(4):
        both_ref[:, q * size : (q + 1) * size] = strip_ref[q]
    both = both_ref[...]
    turned = both.T
    down = lax.broadcasted_iota(jnp.int32, both.shape, 0) // width
    over = lax.broadcasted_iota(jnp.int32, both.shape, 1) // width
    inner = jnp.where(over >= down, both, turned)
    factor_ref[...] = jnp.zeros(factor_ref.shape, F32)
    factor_ref[:width, :width] = factors_ref[0]
    for p in range(1, panels):
        m = p * width
        across = dot(turned[:m, m : m + width], factors_ref[p], 1, 0, HIGHEST)
        factor_ref[:m, m : m + width] = -dot(factor_ref[:m, :m], across, 1, 0, HIGHEST)
        factor_ref[m : m + width, m : m + width] = factors_ref[p]
    factor = factor_ref[...]
    across = factor.T
    middle = mul(wide(across), tall(mul(wide(inner), tall(factor))))
    first_ref[...] = wide(jnp.concatenate([across, -middle], axis=1))
    second_ref[...] = wide(factor)


def left_kernel(place, vec_ref, mine_ref, other_ref, left_ref, prod_ref):
    rank = vec_ref.shape[0]
    for k, ref in enumerate((mine_ref, other_ref)):
        for l in range(2):
            for d in range(4):
                prod_ref[at(place, 2 * k + l, 80), at(place, 4 + d, 256)] = ref[l, d]
    for start, ref in ((0, vec_ref), (rank, prod_ref)):
        high, low = split(ref[...].T)
        left_ref[:, start : start + rank] = high
        left_ref[:, 2 * rank + start : 3 * rank + start] = low
        left_ref[:, 4 * rank + start : 5 * rank + start] = high


def update_kernel(place, *refs):
    near, (prod_two, vec_two) = refs[:3], refs[3:5]
    first_ref, second_ref, left_ref, mat_ref, out_ref, new_ref, sems = refs[5:]
    rank, width = prod_two.shape
    copies = []
    for k in range(4):
        if k < 3:
            prod, vec = near[k][:rank], near[k][rank:]
        else:
            prod, vec = prod_two[...], vec_two[...]
        one = mul(first_ref[...], tall(jnp.concatenate([prod, vec], axis=0)))
        two = mul(second_ref[...], tall(vec))
        right = tall(jnp.concatenate([one, two], axis=0))
        where = at(place, k, width)
        new_ref[:, where] = mat_ref[:, where] - mul(left_ref[...], right)
        copies.append(pltpu.make_async_copy(new_ref.at[:, where], out_ref.at[:, where], sems.at[k]))
        copies[k].start()
    for copy in copies:
        copy.wait()


def update(place, *operands):
    rows, columns = operands[-1].shape
    rank = operands[0].shape[0] // 2
    return pl.pallas_call(
        update_kernel,
        out_shape=SDS((rows, columns), F32),
        in_specs=[pl.BlockSpec(memory_space=pltpu.SMEM)]
        + [pl.BlockSpec(memory_space=pltpu.VMEM)] * len(operands),
        out_specs=pl.BlockSpec(memory_space=pl.ANY),
        scratch_shapes=[pltpu.VMEM((rows, columns), F32), pltpu.SemaphoreType.DMA((4,))],
        compiler_params=pltpu.CompilerParams(vmem_limit_bytes=20 * 2**20),
        cost_estimate=pl.CostEstimate(
            flops=12 * rows * rank * columns, bytes_accessed=8 * rows * columns, transcendentals=0
        ),
    )(place, *operands)


def body(matrix, reflectors, factors):
    panels, width, _ = reflectors.shape
    rank = panels * width
    rows = reflectors.shape[2]
    vectors = reflectors.reshape(rank, rows)
    row, col = lax.axis_index("row"), lax.axis_index("col")
    x, z = row % 4, row // 4
    y, zlo, core = col // 4, (col // 2) % 2, col % 2
    table = lambda entries: jnp.stack(entries).astype(jnp.int32)
    order = [x, (x + 3) % 4, (x + 1) % 4, (x + 2) % 4]
    first = table([(x + 2) % 4, (x + 1) % 4, (x + 3) % 4, x, col % 4, y])
    from_z = [(z - d) % 4 for d in range(4)]
    away = table([(z + d) % 4 for d in range(4)] + from_z)
    lanes_at = [(y - d) % 4 for d in range(4)]
    pieces_at = table([2 * (zlo ^ l) + (core ^ k) for k in range(2) for l in range(2)] + lanes_at)
    size, lanes = rank // 4, rows // 4
    slice_shape = SDS((size, lanes), F32)
    quarter_shape = SDS((rank, lanes), F32)
    inner_shape = SDS((size, size), F32)

    with jax.named_scope("vec_turn"):
        turn = piece(piece(vectors, col % 4, size, 0), y, lanes, 1)
        vec_part = lax.ppermute(turn, EVERYWHERE, TO_COLUMN)
    with jax.named_scope("products"):
        opposite, right, left, mine = quarter_products(first, vectors, matrix)
    with jax.named_scope("prod_sum_x"):
        got = send([(2, opposite), (1, right), (3, left)], "row", SHIFT_X)
    with jax.named_scope("sum_x"):
        prods = whole_kernel(
            sum_x_kernel, [slice_shape] * 4, away, mine, *got,
            scratch=[pltpu.VMEM(quarter_shape.shape, F32)],
        )
    with jax.named_scope("prod_sum_z"):
        got = send([(d, prods[d]) for d in (1, 2, 3)], "row", SHIFT_Z)
    with jax.named_scope("sum_z"):
        pair, prod_part = whole_kernel(
            sum_z_kernel, [SDS((2 * size, lanes), F32), slice_shape], away, prods[0], *got, vec_part
        )
    with jax.named_scope("prod_turn"):
        other = lax.ppermute(prod_part, EVERYWHERE, TO_ROW)
    with jax.named_scope("pair_z"):
        left, right = send([(1, pair), (3, pair)], "row", SHIFT_Z)
        two = send([(1, left[:size]), (3, right[size:])], "row", SHIFT_Z)
    with jax.named_scope("join"):
        pair, other, *inners = whole_kernel(
            lambda *refs: join_kernel(width, *refs),
            [SDS((2 * rank, lanes), F32), slice_shape] + [inner_shape] * 4,
            table(
                from_z + [y, col % 4, y, y] + [4 + i for i in from_z] + [(y + d) % 4 for d in range(4)]
            ),
            pair, left, right, *two, other, vectors,
            scratch=[pltpu.VMEM((rank, size), F32)], flops=24 * rank * size * lanes,
        )
    with jax.named_scope("pair_x"):
        pair_left, pair_right = send([(1, pair), (3, pair)], "row", SHIFT_X)
    with jax.named_scope("row_y"):
        others = [other] + send([(d, other) for d in (1, 2, 3)], "col", SHIFT_Y)
    with jax.named_scope("inner_y"):
        got = send([(d, inners[d]) for d in (1, 2, 3)], "col", SHIFT_Y)
        inner, mine = whole_kernel(
            sum_y_kernel, [inner_shape, SDS((4, size, lanes), F32)], away, inners[0], *got, *others
        )
    with jax.named_scope("row_zlo"):
        other = lax.ppermute(mine, "col", SWAP_ZLO)
    with jax.named_scope("inner_z"):
        got = send([(d, inner) for d in (1, 2, 3)], "row", SHIFT_Z)
        inner, mine, *two = whole_kernel(
            add_z_kernel, [inner_shape, SDS((2, 4, size, lanes), F32), quarter_shape, quarter_shape],
            away, inner, *got, mine, other, pair_left, pair_right,
        )
    with jax.named_scope("row_core"):
        other = lax.ppermute(mine, "col", SWAP_CORE)
    with jax.named_scope("inner_x"):
        got = send([(d, inner) for d in (1, 2, 3)], "row", SHIFT_X)
        inner, *two = whole_kernel(
            add_x_kernel, [inner_shape, quarter_shape, quarter_shape], away, inner, *got, *two, after=[other]
        )
    with jax.named_scope("pair_two"):
        two = [lax.ppermute(two[0], "row", SHIFT_X[1]), lax.ppermute(two[1], "row", SHIFT_X[3])]
    with jax.named_scope("inner_gy"):
        inner = jnp.stack([inner] + send([(d, inner) for d in (1, 2, 3)], "col", SHIFT_Y))
    with jax.named_scope("inner_zlo"):
        inner = jnp.stack([inner, lax.ppermute(inner, "col", SWAP_ZLO)])
    with jax.named_scope("inner_core"):
        inner_other = lax.ppermute(inner, "col", SWAP_CORE)
    with jax.named_scope("left"):
        (left,) = whole_kernel(
            left_kernel, [SDS((rows, 6 * rank), BF16)], pieces_at, vectors, mine, other,
            scratch=[pltpu.VMEM((rank, rows), F32)], after=[inner_other],
        )
    with jax.named_scope("factor"):
        sides = whole_kernel(
            factor_kernel, [SDS((rank, 6 * rank), BF16), SDS((rank, 3 * rank), BF16)],
            pieces_at, inner, inner_other, factors,
            scratch=[
                pltpu.VMEM((rank, rank), F32), pltpu.VMEM((4, rank, size), F32), pltpu.VMEM((rank, rank), F32)
            ],
            after=two,
        )
    with jax.named_scope("update"):
        return update(table(order), pair, pair_left, pair_right, *two, *sides, left, matrix)


def solution(mesh):
    in_specs = (P("row", "col"), P(None, None, "row"), P())
    out_specs = P("row", "col")
    return jax.shard_map(body, mesh=mesh, in_specs=in_specs, out_specs=out_specs, check_vma=False)
```

time: 167 us -> 151 us (0.904); the launches traced: 165 us -> 151 us
  waiting for transfers between devices: 58.2 us -> 37.9 us
  starting transfers between devices: 71.2 us -> 79.4 us
  local copies, waits for them, and re-layouts: 10.1 us -> 4.84 us
  Pallas kernels: 25 us -> 27.4 us
    ppermute x9 -> x5, waiting for transfers between devices: 25.5 us -> 1.47 us  [the longest x1 1.43 us: body(): inner_other = lax.ppermute(inner, 'col', SWAP_CORE)]
    ppermute x9 -> x5, starting transfers between devices: 20.3 us -> 9.52 us  [the longest x1 3.65 us: body(): inner_other = lax.ppermute(inner, 'col', SWAP_CORE)]
    ppermute x1, starting transfers between devices: 1.71 us -> 9.6 us  [body(): other = lax.ppermute(mine, 'col', SWAP_CORE)]
    ppermute x21 -> x27, starting transfers between devices: 41.8 us -> 48.5 us  [send(): return [lax.ppermute(part, axis, shifts[d]) for d, part in parts]]
    ppermute x1, waiting for transfers between devices: 0.01 us -> 6.69 us  [body(): other = lax.ppermute(prod_part, EVERYWHERE, TO_ROW)]
    unnamed x14 -> x16, local copies, waits for them, and re-layouts: 9.73 us -> 3.79 us
    ppermute x1, starting transfers between devices: 3.22 us -> 6.3 us  [body(): vec_part = lax.ppermute(turn, EVERYWHERE, TO_COLUMN)]
    ppermute x21 -> x27, waiting for transfers between devices: 32.7 us -> 29.7 us  [send(): return [lax.ppermute(part, axis, shifts[d]) for d, part in parts]]
  transfers between devices with their start and end apart: 33 -> 35, of which waited for: 19 -> 20; matrix products, arithmetic and copies ran while one was open for 0% -> 1% of each run, Pallas kernels for 5% -> 2%
where the time goes in v2:
time: 151 us
  starting transfers between devices  79.4 us (53%)
  waiting for transfers between devices  37.9 us (25%)
  Pallas kernels  27.4 us (18%)
  local copies, waits for them, and re-layouts  4.84 us (3%)
    ppermute x27, starting transfers between devices, send(): return [lax.ppermute(part, axis, shifts[d]) for d, part in parts]  48.5 us
    ppermute x27, waiting for transfers between devices, send(): return [lax.ppermute(part, axis, shifts[d]) for d, part in parts]  29.7 us
    pallas_call x8, Pallas kernels, whole_kernel(): pl.pallas_call(lambda place, *refs: kernel(place, *refs[:count], *refs[co...  10.9 us
    ppermute x1, starting transfers between devices, body(): other = lax.ppermute(mine, 'col', SWAP_CORE)  9.6 us
    pallas_call x1, Pallas kernels, update(): pl.pallas_call(update_kernel, out_shape=SDS((rows, columns), F32), in_spe...  9.56 us
    pallas_call x1, Pallas kernels, quarter_products(): pl.pallas_call(quarter_product_kernel, out_shape=[shape] * 4, grid_spec=p...  6.95 us
    ppermute x1, waiting for transfers between devices, body(): other = lax.ppermute(prod_part, EVERYWHERE, TO_ROW)  6.69 us
    ppermute x1, starting transfers between devices, body(): vec_part = lax.ppermute(turn, EVERYWHERE, TO_COLUMN)  6.3 us
  transfers between devices with their start and end apart: 35, of which 20 were waited for; matrix products, arithmetic and copies ran while one was open for 1% of the time, Pallas kernels for 2%

profile of v2, /device:TPU:1, one launch (start us, length us, event | category | flops | bytes accessed | tf_op | source)
XLA Modules:
  0.0 150.9 jit_solution(3390465941603178621)
XLA Ops:
  0.7 6.9 %products.1 = (f32[320,256]{1,0:T(8,128)}, f32[320,256]{1,0:T(8,128)}, f32[320,256]{1,0:T(8,128)}, f32[320,256]{1,0:T(8,128)}) custom-call(s32[6]{0:T(128)} %stack.161.place, f32[320,1024]{1,0:T(8,128)} %bitcast.36, f32[1024,1024]{1,0:T(8,128)} %refs_8_.1), custom_call_target="tpu_custom_call" | custom-call | flops 2013265920 | bytes 6815744 | tf_op jit(solution)/shard_map/products/pallas_call | solution.py:117
  7.6 3.6 %collective-permute-start = (f32[320,256]{1,0:T(8,128)}, f32[320,256]{1,0:T(8,128)S(1)}, u32[]{:S(2)}, u32[]{:S(2)}) collective-permute-start(f32[320,256]{1,0:T(8,128)} %get-tuple-element.33), channel_id=1, source_target_pairs={{0,32},{16,48},{32,0},{48,16},{64,96},{80,112},{96,64},{112,80},{1... | collective-permute-start | bytes 983048 | tf_op jit(solution)/shard_map/prod_sum_x/ppermute | solution.py:66
  11.5 2.4 %collective-permute-start.2 = (f32[320,256]{1,0:T(8,128)}, f32[320,256]{1,0:T(8,128)S(1)}, u32[]{:S(2)}, u32[]{:S(2)}) collective-permute-start(f32[320,256]{1,0:T(8,128)} %get-tuple-element.35), channel_id=1, source_target_pairs={{0,48},{16,0},{32,16},{48,32},{64,112},{80,64},{96,80},{112,96},{1... | collective-permute-start | bytes 983048 | tf_op jit(solution)/shard_map/prod_sum_x/ppermute | solution.py:66
  14.0 6.3 %collective-permute-start.6 = (f32[80,256]{1,0:T(8,128)S(1)}, f32[80,256]{1,0:T(8,128)S(1)}, u32[]{:S(2)}, u32[]{:S(2)}) collective-permute-start(f32[80,256]{1,0:T(8,128)S(1)} %dynamic_slice.4), channel_id=1, source_target_pairs={{0,0},{1,64},{2,128},{3,192},{4,16},{5,80},{6,144},{7,208},{8,32},... | collective-permute-start | bytes 245768 | tf_op jit(solution)/shard_map/vec_turn/ppermute | solution.py:299
  20.5 6.1 %collective-permute-done.1.refs_2_ = f32[320,256]{1,0:T(8,128)S(1)} collective-permute-done((f32[320,256]{1,0:T(8,128)}, f32[320,256]{1,0:T(8,128)S(1)}, u32[]{:S(2)}, u32[]{:S(2)}) %collective-permute-start.1) | collective-permute-done | bytes 327712 | tf_op jit(solution)/shard_map/prod_sum_x/ppermute | solution.py:66
  26.6 2.0 %collective-permute-done.2.refs_3_ = f32[320,256]{1,0:T(8,128)S(1)} collective-permute-done((f32[320,256]{1,0:T(8,128)}, f32[320,256]{1,0:T(8,128)S(1)}, u32[]{:S(2)}, u32[]{:S(2)}) %collective-permute-start.2) | collective-permute-done | bytes 327712 | tf_op jit(solution)/shard_map/prod_sum_x/ppermute | solution.py:66
  30.2 3.1 %collective-permute-start.3 = (f32[80,256]{1,0:T(8,128)S(1)}, f32[80,256]{1,0:T(8,128)S(1)}, u32[]{:S(2)}, u32[]{:S(2)}) collective-permute-start(f32[80,256]{1,0:T(8,128)S(1)} %get-tuple-element.37), channel_id=1, source_target_pairs={{0,64},{16,80},{32,96},{48,112},{64,128},{80,144},{96,160},{112,17... | collective-permute-start | bytes 245768 | tf_op jit(solution)/shard_map/prod_sum_z/ppermute | solution.py:66
  33.2 6.0 %collective-permute-start.4 = (f32[80,256]{1,0:T(8,128)S(1)}, f32[80,256]{1,0:T(8,128)S(1)}, u32[]{:S(2)}, u32[]{:S(2)}) collective-permute-start(f32[80,256]{1,0:T(8,128)S(1)} %get-tuple-element.38), channel_id=1, source_target_pairs={{0,128},{16,144},{32,160},{48,176},{64,192},{80,208},{96,224},{112... | collective-permute-start | bytes 245768 | tf_op jit(solution)/shard_map/prod_sum_z/ppermute | solution.py:66
  39.2 2.4 %collective-permute-start.5 = (f32[80,256]{1,0:T(8,128)S(1)}, f32[80,256]{1,0:T(8,128)S(1)}, u32[]{:S(2)}, u32[]{:S(2)}) collective-permute-start(f32[80,256]{1,0:T(8,128)S(1)} %get-tuple-element.39), channel_id=1, source_target_pairs={{0,192},{16,208},{32,224},{48,240},{64,0},{80,16},{96,32},{112,48}... | collective-permute-start | bytes 245768 | tf_op jit(solution)/shard_map/prod_sum_z/ppermute | solution.py:66
  42.0 1.7 %collective-permute-done.5.refs_3_ = f32[80,256]{1,0:T(8,128)S(1)} collective-permute-done((f32[80,256]{1,0:T(8,128)S(1)}, f32[80,256]{1,0:T(8,128)S(1)}, u32[]{:S(2)}, u32[]{:S(2)}) %collective-permute-start.5) | collective-permute-done | bytes 81952 | tf_op jit(solution)/shard_map/prod_sum_z/ppermute | solution.py:66
  44.3 3.4 %collective-permute-start.8 = (f32[160,256]{1,0:T(8,128)S(1)}, f32[160,256]{1,0:T(8,128)S(1)}, u32[]{:S(2)}, u32[]{:S(2)}) collective-permute-start(f32[160,256]{1,0:T(8,128)S(1)} %get-tuple-element.40.refs_0_), channel_id=1, source_target_pairs={{0,192},{16,208},{32,224},{48,240},{64,0},{80,16},{96,32},{112,48}... | collective-permute-start | bytes 491528 | tf_op jit(solution)/shard_map/pair_z/ppermute | solution.py:66
  47.7 5.4 %collective-permute-start.11 = (f32[80,256]{1,0:T(8,128)S(1)}, f32[80,256]{1,0:T(8,128)S(1)}, u32[]{:S(2)}, u32[]{:S(2)}) collective-permute-start(f32[80,256]{1,0:T(8,128)S(1)} %get-tuple-element.41), channel_id=1, source_target_pairs={{0,0},{64,1},{128,2},{192,3},{16,4},{80,5},{144,6},{208,7},{32,8},... | collective-permute-start | bytes 245768 | tf_op jit(solution)/shard_map/prod_turn/ppermute | solution.py:316
  53.1 2.5 %collective-permute-start.10 = (f32[80,256]{1,0:T(8,128)S(1)}, f32[80,256]{1,0:T(8,128)S(1)}, u32[]{:S(2)}, u32[]{:S(2)}) collective-permute-start(f32[80,256]{1,0:T(8,128)S(1)} %slice.9), channel_id=1, source_target_pairs={{0,192},{16,208},{32,224},{48,240},{64,0},{80,16},{96,32},{112,48}... | collective-permute-start | bytes 245768 | tf_op jit(solution)/shard_map/pair_z/ppermute | solution.py:66
  55.9 6.7 %collective-permute-done.11.refs_5_ = f32[80,256]{1,0:T(8,128)S(1)} collective-permute-done((f32[80,256]{1,0:T(8,128)S(1)}, f32[80,256]{1,0:T(8,128)S(1)}, u32[]{:S(2)}, u32[]{:S(2)}) %collective-permute-start.11) | collective-permute-done | bytes 81952 | tf_op jit(solution)/shard_map/prod_turn/ppermute | solution.py:316
  64.8 7.5 %collective-permute-start.13 = (f32[640,256]{1,0:T(8,128)S(1)}, f32[640,256]{1,0:T(8,128)S(1)}, u32[]{:S(2)}, u32[]{:S(2)}) collective-permute-start(f32[640,256]{1,0:T(8,128)S(1)} %get-tuple-element.42.refs_0_), channel_id=1, source_target_pairs={{0,48},{16,0},{32,16},{48,32},{64,112},{80,64},{96,80},{112,96},{1... | collective-permute-start | bytes 1966088 | tf_op jit(solution)/shard_map/pair_x/ppermute | solution.py:66
  73.1 4.7 %collective-permute-start.15 = (f32[80,80]{1,0:T(8,128)S(1)}, f32[80,80]{1,0:T(8,128)S(1)}, u32[]{:S(2)}, u32[]{:S(2)}) collective-permute-start(f32[80,80]{1,0:T(8,128)S(1)} %get-tuple-element.45), channel_id=1, source_target_pairs={{0,8},{1,9},{2,10},{3,11},{4,12},{5,13},{6,14},{7,15},{8,0},{9,1},... | collective-permute-start | bytes 76808 | tf_op jit(solution)/shard_map/inner_y/ppermute | solution.py:66
  78.1 1.5 collective-permute-start.19
  79.7 2.9 %collective-permute-start.18 = (f32[80,256]{1,0:T(8,128)S(1)}, f32[80,256]{1,0:T(8,128)S(1)}, u32[]{:S(2)}, u32[]{:S(2)}) collective-permute-start(f32[80,256]{1,0:T(8,128)S(1)} %get-tuple-element.47.refs_4_), channel_id=1, source_target_pairs={{0,8},{1,9},{2,10},{3,11},{4,12},{5,13},{6,14},{7,15},{8,0},{9,1},... | collective-permute-start | bytes 245768 | tf_op jit(solution)/shard_map/row_y/ppermute | solution.py:66
  82.6 1.9 %collective-permute-done.18.refs_6_ = f32[80,256]{1,0:T(8,128)S(1)} collective-permute-done((f32[80,256]{1,0:T(8,128)S(1)}, f32[80,256]{1,0:T(8,128)S(1)}, u32[]{:S(2)}, u32[]{:S(2)}) %collective-permute-start.18) | collective-permute-done | bytes 81952 | tf_op jit(solution)/shard_map/row_y/ppermute | solution.py:66
  84.6 2.8 %collective-permute-done.17.refs_5_ = f32[80,256]{1,0:T(8,128)S(1)} collective-permute-done((f32[80,256]{1,0:T(8,128)S(1)}, f32[80,256]{1,0:T(8,128)S(1)}, u32[]{:S(2)}, u32[]{:S(2)}) %collective-permute-start.17) | collective-permute-done | bytes 81952 | tf_op jit(solution)/shard_map/row_y/ppermute | solution.py:66
  88.1 1.8 %collective-permute-start.22 = (f32[80,80]{1,0:T(8,128)S(1)}, f32[80,80]{1,0:T(8,128)S(1)}, u32[]{:S(2)}, u32[]{:S(2)}) collective-permute-start(f32[80,80]{1,0:T(8,128)S(1)} %get-tuple-element.48.refs_0_), channel_id=1, source_target_pairs={{0,192},{16,208},{32,224},{48,240},{64,0},{80,16},{96,32},{112,48}... | collective-permute-start | bytes 76808 | tf_op jit(solution)/shard_map/inner_z/ppermute | solution.py:66
  89.9 1.8 %collective-permute-start.21 = (f32[80,80]{1,0:T(8,128)S(1)}, f32[80,80]{1,0:T(8,128)S(1)}, u32[]{:S(2)}, u32[]{:S(2)}) collective-permute-start(f32[80,80]{1,0:T(8,128)S(1)} %get-tuple-element.48.refs_0_), channel_id=1, source_target_pairs={{0,128},{16,144},{32,160},{48,176},{64,192},{80,208},{96,224},{112... | collective-permute-start | bytes 76808 | tf_op jit(solution)/shard_map/inner_z/ppermute | solution.py:66
  93.5 3.4 %collective-permute-done.21.refs_2_ = f32[80,80]{1,0:T(8,128)S(1)} collective-permute-done((f32[80,80]{1,0:T(8,128)S(1)}, f32[80,80]{1,0:T(8,128)S(1)}, u32[]{:S(2)}, u32[]{:S(2)}) %collective-permute-start.21) | collective-permute-done | bytes 25632 | tf_op jit(solution)/shard_map/inner_z/ppermute | solution.py:66
  98.4 9.6 %collective-permute-start.27 = (f32[2,4,80,256]{3,2,1,0:T(8,128)S(1)}, f32[2,4,80,256]{3,2,1,0:T(8,128)S(1)}, u32[]{:S(2)}, u32[]{:S(2)}) collective-permute-start(f32[2,4,80,256]{3,2,1,0:T(8,128)S(1)} %get-tuple-element.53.refs_1_), channel_id=1, source_target_pairs={{0,1},{1,0},{2,3},{3,2},{4,5},{5,4},{6,7},{7,6},{8,9},{9,8},{10,11... | collective-permute-start | bytes 1966088 | tf_op jit(solution)/shard_map/row_core/ppermute | solution.py:348
  111.7 2.6 %collective-permute-done.25.refs_2_ = f32[80,80]{1,0:T(8,128)S(1)} collective-permute-done((f32[80,80]{1,0:T(8,128)S(1)}, f32[80,80]{1,0:T(8,128)S(1)}, u32[]{:S(2)}, u32[]{:S(2)}) %collective-permute-start.25) | collective-permute-done | bytes 25632 | tf_op jit(solution)/shard_map/inner_x/ppermute | solution.py:66
  119.7 1.5 collective-permute-done.31
  122.1 3.1 %collective-permute-start.33 = (f32[4,80,80]{2,1,0:T(8,128)S(1)}, f32[4,80,80]{2,1,0:T(8,128)S(1)}, u32[]{:S(2)}, u32[]{:S(2)}) collective-permute-start(f32[4,80,80]{2,1,0:T(8,128)S(1)} %get-tuple-element.60), channel_id=1, source_target_pairs={{0,2},{1,3},{2,0},{3,1},{4,6},{5,7},{6,4},{7,5},{8,10},{9,11},{10,... | collective-permute-start | bytes 307208 | tf_op jit(solution)/shard_map/inner_zlo/ppermute | solution.py:359
  125.2 2.7 %collective-permute-start.29 = (f32[320,256]{1,0:T(8,128)}, f32[320,256]{1,0:T(8,128)}, u32[]{:S(2)}, u32[]{:S(2)}) collective-permute-start(f32[320,256]{1,0:T(8,128)} %get-tuple-element.55), channel_id=1, source_target_pairs={{0,48},{16,0},{32,16},{48,32},{64,112},{80,64},{96,80},{112,96},{1... | collective-permute-start | bytes 983048 | tf_op jit(solution)/shard_map/pair_two/ppermute | solution.py:355
  128.7 3.7 %collective-permute-start.34 = (f32[2,4,80,80]{3,2,1,0:T(8,128)}, f32[2,4,80,80]{3,2,1,0:T(8,128)}, u32[]{:S(2)}, u32[]{:S(2)}) collective-permute-start(f32[2,4,80,80]{3,2,1,0:T(8,128)} %pad_maximum_fusion.refs_0_), channel_id=1, source_target_pairs={{0,1},{1,0},{2,3},{3,2},{4,5},{5,4},{6,7},{7,6},{8,9},{9,8},{10,11... | collective-permute-start | bytes 614408 | tf_op jit(solution)/shard_map/inner_core/ppermute | solution.py:361
  135.0 2.0 %left.1.refs_7_ = bf16[1024,1920]{1,0:T(8,128)(2,1)S(1)} custom-call(s32[8]{0:T(128)S(1)} %stack.169.place, f32[320,1024]{1,0:T(8,128)S(1)} %bitcast.39, f32[2,4,80,256]{3,2,1,0:T(8,128)S(1)} %copy-done.5, f32[2,4,80,256]{3,2,1,0:T(8,128)S(1)} %collective-permute-done.27.refs_6_.refs_2_, f32[2,4,80,80]{3,2,1,0:T(8,128)} %collective-permute-done.34.refs_1_.refs_3_), custom_call_target="tpu_custom_call" | custom-call | bytes 6553600 | tf_op jit(solution)/shard_map/left/pallas_call | solution.py:72
  137.1 4.0 %factor.1 = (bf16[320,1920]{1,0:T(8,128)(2,1)S(1)}, bf16[320,960]{1,0:T(8,128)(2,1)S(1)}) custom-call(s32[8]{0:T(128)S(1)} %stack.169.place, f32[2,4,80,80]{3,2,1,0:T(8,128)} %pad_maximum_fusion.refs_0_, f32[2,4,80,80]{3,2,1,0:T(8,128)} %collective-permute-done.34.refs_1_.refs_3_, f32[5,64,64]{2,1,0:T(8,128)S(1)} %copy-done.7, ...), custom_call_target="tpu_custom_call" | custom-call | bytes 2334720 | tf_op jit(solution)/shard_map/factor/pallas_call | solution.py:72
  141.1 9.6 %update.1 = f32[1024,1024]{1,0:T(8,128)} custom-call(s32[4]{0:T(128)S(1)} %pad_add_fusion.place, f32[640,256]{1,0:T(8,128)S(1)} %copy-done.3, f32[640,256]{1,0:T(8,128)S(1)} %collective-permute-done.12.refs_6_.refs_1_, f32[640,256]{1,0:T(8,128)S(1)} %collective-permute-done.13.refs_7_.refs_2_, f32[320,256]{1,0:T(8,128)} %collective-permute-done.28.refs_3_, ...), custom_call_target="tpu_custom_call" | custom-call | flops 4026531840 | bytes 8388608 | tf_op jit(solution)/shard_map/update/pallas_call | solution.py:263
  (74 shorter events, 24.8 us)
Async XLA Ops:
  7.6 12.9 %collective-permute-start = (f32[320,256]{1,0:T(8,128)}, f32[320,256]{1,0:T(8,128)S(1)}, u32[]{:S(2)}, u32[]{:S(2)}) collective-permute-start(f32[320,256]{1,0:T(8,128)} %get-tuple-element.33), channel_id=1, source_target_pairs={{0,32},{16,48},{32,0},{48,16},{64,96},{80,112},{96,64},{112,80},{1... | collective-permute-start | bytes 983048 | tf_op jit(solution)/shard_map/prod_sum_x/ppermute | solution.py:66
  11.2 15.4 %collective-permute-start.1 = (f32[320,256]{1,0:T(8,128)}, f32[320,256]{1,0:T(8,128)S(1)}, u32[]{:S(2)}, u32[]{:S(2)}) collective-permute-start(f32[320,256]{1,0:T(8,128)} %get-tuple-element.34), channel_id=1, source_target_pairs={{0,16},{16,32},{32,48},{48,0},{64,80},{80,96},{96,112},{112,64},{1... | collective-permute-start | bytes 983048 | tf_op jit(solution)/shard_map/prod_sum_x/ppermute | solution.py:66
  11.5 17.0 %collective-permute-start.2 = (f32[320,256]{1,0:T(8,128)}, f32[320,256]{1,0:T(8,128)S(1)}, u32[]{:S(2)}, u32[]{:S(2)}) collective-permute-start(f32[320,256]{1,0:T(8,128)} %get-tuple-element.35), channel_id=1, source_target_pairs={{0,48},{16,0},{32,16},{48,32},{64,112},{80,64},{96,80},{112,96},{1... | collective-permute-start | bytes 983048 | tf_op jit(solution)/shard_map/prod_sum_x/ppermute | solution.py:66
  14.0 27.6 %collective-permute-start.6 = (f32[80,256]{1,0:T(8,128)S(1)}, f32[80,256]{1,0:T(8,128)S(1)}, u32[]{:S(2)}, u32[]{:S(2)}) collective-permute-start(f32[80,256]{1,0:T(8,128)S(1)} %dynamic_slice.4), channel_id=1, source_target_pairs={{0,0},{1,64},{2,128},{3,192},{4,16},{5,80},{6,144},{7,208},{8,32},... | collective-permute-start | bytes 245768 | tf_op jit(solution)/shard_map/vec_turn/ppermute | solution.py:299
  30.2 11.5 %collective-permute-start.3 = (f32[80,256]{1,0:T(8,128)S(1)}, f32[80,256]{1,0:T(8,128)S(1)}, u32[]{:S(2)}, u32[]{:S(2)}) collective-permute-start(f32[80,256]{1,0:T(8,128)S(1)} %get-tuple-element.37), channel_id=1, source_target_pairs={{0,64},{16,80},{32,96},{48,112},{64,128},{80,144},{96,160},{112,17... | collective-permute-start | bytes 245768 | tf_op jit(solution)/shard_map/prod_sum_z/ppermute | solution.py:66
  33.2 8.8 %collective-permute-start.4 = (f32[80,256]{1,0:T(8,128)S(1)}, f32[80,256]{1,0:T(8,128)S(1)}, u32[]{:S(2)}, u32[]{:S(2)}) collective-permute-start(f32[80,256]{1,0:T(8,128)S(1)} %get-tuple-element.38), channel_id=1, source_target_pairs={{0,128},{16,144},{32,160},{48,176},{64,192},{80,208},{96,224},{112... | collective-permute-start | bytes 245768 | tf_op jit(solution)/shard_map/prod_sum_z/ppermute | solution.py:66
  39.2 4.5 %collective-permute-start.5 = (f32[80,256]{1,0:T(8,128)S(1)}, f32[80,256]{1,0:T(8,128)S(1)}, u32[]{:S(2)}, u32[]{:S(2)}) collective-permute-start(f32[80,256]{1,0:T(8,128)S(1)} %get-tuple-element.39), channel_id=1, source_target_pairs={{0,192},{16,208},{32,224},{48,240},{64,0},{80,16},{96,32},{112,48}... | collective-permute-start | bytes 245768 | tf_op jit(solution)/shard_map/prod_sum_z/ppermute | solution.py:66
  44.3 8.8 %collective-permute-start.8 = (f32[160,256]{1,0:T(8,128)S(1)}, f32[160,256]{1,0:T(8,128)S(1)}, u32[]{:S(2)}, u32[]{:S(2)}) collective-permute-start(f32[160,256]{1,0:T(8,128)S(1)} %get-tuple-element.40.refs_0_), channel_id=1, source_target_pairs={{0,192},{16,208},{32,224},{48,240},{64,0},{80,16},{96,32},{112,48}... | collective-permute-start | bytes 491528 | tf_op jit(solution)/shard_map/pair_z/ppermute | solution.py:66
  47.7 8.0 %collective-permute-start.7 = (f32[160,256]{1,0:T(8,128)S(1)}, f32[160,256]{1,0:T(8,128)S(1)}, u32[]{:S(2)}, u32[]{:S(2)}) collective-permute-start(f32[160,256]{1,0:T(8,128)S(1)} %get-tuple-element.40.refs_0_), channel_id=1, source_target_pairs={{0,64},{16,80},{32,96},{48,112},{64,128},{80,144},{96,160},{112,17... | collective-permute-start | bytes 491528 | tf_op jit(solution)/shard_map/pair_z/ppermute | solution.py:66
  47.7 14.9 %collective-permute-start.11 = (f32[80,256]{1,0:T(8,128)S(1)}, f32[80,256]{1,0:T(8,128)S(1)}, u32[]{:S(2)}, u32[]{:S(2)}) collective-permute-start(f32[80,256]{1,0:T(8,128)S(1)} %get-tuple-element.41), channel_id=1, source_target_pairs={{0,0},{64,1},{128,2},{192,3},{16,4},{80,5},{144,6},{208,7},{32,8},... | collective-permute-start | bytes 245768 | tf_op jit(solution)/shard_map/prod_turn/ppermute | solution.py:316
  53.1 9.5 %collective-permute-start.10 = (f32[80,256]{1,0:T(8,128)S(1)}, f32[80,256]{1,0:T(8,128)S(1)}, u32[]{:S(2)}, u32[]{:S(2)}) collective-permute-start(f32[80,256]{1,0:T(8,128)S(1)} %slice.9), channel_id=1, source_target_pairs={{0,192},{16,208},{32,224},{48,240},{64,0},{80,16},{96,32},{112,48}... | collective-permute-start | bytes 245768 | tf_op jit(solution)/shard_map/pair_z/ppermute | solution.py:66
  55.6 8.2 %collective-permute-start.9 = (f32[80,256]{1,0:T(8,128)S(1)}, f32[80,256]{1,0:T(8,128)S(1)}, u32[]{:S(2)}, u32[]{:S(2)}) collective-permute-start(f32[80,256]{1,0:T(8,128)S(1)} %slice.8), channel_id=1, source_target_pairs={{0,64},{16,80},{32,96},{48,112},{64,128},{80,144},{96,160},{112,17... | collective-permute-start | bytes 245768 | tf_op jit(solution)/shard_map/pair_z/ppermute | solution.py:66
  64.8 32.9 %collective-permute-start.13 = (f32[640,256]{1,0:T(8,128)S(1)}, f32[640,256]{1,0:T(8,128)S(1)}, u32[]{:S(2)}, u32[]{:S(2)}) collective-permute-start(f32[640,256]{1,0:T(8,128)S(1)} %get-tuple-element.42.refs_0_), channel_id=1, source_target_pairs={{0,48},{16,0},{32,16},{48,32},{64,112},{80,64},{96,80},{112,96},{1... | collective-permute-start | bytes 1966088 | tf_op jit(solution)/shard_map/pair_x/ppermute | solution.py:66
  72.3 25.5 %collective-permute-start.12 = (f32[640,256]{1,0:T(8,128)S(1)}, f32[640,256]{1,0:T(8,128)S(1)}, u32[]{:S(2)}, u32[]{:S(2)}) collective-permute-start(f32[640,256]{1,0:T(8,128)S(1)} %get-tuple-element.42.refs_0_), channel_id=1, source_target_pairs={{0,16},{16,32},{32,48},{48,0},{64,80},{80,96},{96,112},{112,64},{1... | collective-permute-start | bytes 1966088 | tf_op jit(solution)/shard_map/pair_x/ppermute | solution.py:66
  73.1 5.0 %collective-permute-start.14 = (f32[80,80]{1,0:T(8,128)S(1)}, f32[80,80]{1,0:T(8,128)S(1)}, u32[]{:S(2)}, u32[]{:S(2)}) collective-permute-start(f32[80,80]{1,0:T(8,128)S(1)} %get-tuple-element.44), channel_id=1, source_target_pairs={{0,4},{1,5},{2,6},{3,7},{4,8},{5,9},{6,10},{7,11},{8,12},{9,13},{1... | collective-permute-start | bytes 76808 | tf_op jit(solution)/shard_map/inner_y/ppermute | solution.py:66
  73.1 6.6 %collective-permute-start.15 = (f32[80,80]{1,0:T(8,128)S(1)}, f32[80,80]{1,0:T(8,128)S(1)}, u32[]{:S(2)}, u32[]{:S(2)}) collective-permute-start(f32[80,80]{1,0:T(8,128)S(1)} %get-tuple-element.45), channel_id=1, source_target_pairs={{0,8},{1,9},{2,10},{3,11},{4,12},{5,13},{6,14},{7,15},{8,0},{9,1},... | collective-permute-start | bytes 76808 | tf_op jit(solution)/shard_map/inner_y/ppermute | solution.py:66
  77.9 4.8 %collective-permute-start.16 = (f32[80,80]{1,0:T(8,128)S(1)}, f32[80,80]{1,0:T(8,128)S(1)}, u32[]{:S(2)}, u32[]{:S(2)}) collective-permute-start(f32[80,80]{1,0:T(8,128)S(1)} %get-tuple-element.46), channel_id=1, source_target_pairs={{0,12},{1,13},{2,14},{3,15},{4,0},{5,1},{6,2},{7,3},{8,4},{9,5},{1... | collective-permute-start | bytes 76808 | tf_op jit(solution)/shard_map/inner_y/ppermute | solution.py:66
  78.1 4.6 %collective-permute-start.19 = (f32[80,256]{1,0:T(8,128)S(1)}, f32[80,256]{1,0:T(8,128)S(1)}, u32[]{:S(2)}, u32[]{:S(2)}) collective-permute-start(f32[80,256]{1,0:T(8,128)S(1)} %get-tuple-element.47.refs_4_), channel_id=1, source_target_pairs={{0,12},{1,13},{2,14},{3,15},{4,0},{5,1},{6,2},{7,3},{8,4},{9,5},{1... | collective-permute-start | bytes 245768 | tf_op jit(solution)/shard_map/row_y/ppermute | solution.py:66
  79.7 4.9 %collective-permute-start.18 = (f32[80,256]{1,0:T(8,128)S(1)}, f32[80,256]{1,0:T(8,128)S(1)}, u32[]{:S(2)}, u32[]{:S(2)}) collective-permute-start(f32[80,256]{1,0:T(8,128)S(1)} %get-tuple-element.47.refs_4_), channel_id=1, source_target_pairs={{0,8},{1,9},{2,10},{3,11},{4,12},{5,13},{6,14},{7,15},{8,0},{9,1},... | collective-permute-start | bytes 245768 | tf_op jit(solution)/shard_map/row_y/ppermute | solution.py:66
  82.6 4.8 %collective-permute-start.17 = (f32[80,256]{1,0:T(8,128)S(1)}, f32[80,256]{1,0:T(8,128)S(1)}, u32[]{:S(2)}, u32[]{:S(2)}) collective-permute-start(f32[80,256]{1,0:T(8,128)S(1)} %get-tuple-element.47.refs_4_), channel_id=1, source_target_pairs={{0,4},{1,5},{2,6},{3,7},{4,8},{5,9},{6,10},{7,11},{8,12},{9,13},{1... | collective-permute-start | bytes 245768 | tf_op jit(solution)/shard_map/row_y/ppermute | solution.py:66
  88.0 9.7 %collective-permute-start.23 = (f32[4,80,256]{2,1,0:T(8,128)S(1)}, f32[4,80,256]{2,1,0:T(8,128)S(1)}, u32[]{:S(2)}, u32[]{:S(2)}) collective-permute-start(f32[4,80,256]{2,1,0:T(8,128)S(1)} %get-tuple-element.49.refs_4_), channel_id=1, source_target_pairs={{0,2},{1,3},{2,0},{3,1},{4,6},{5,7},{6,4},{7,5},{8,10},{9,11},{10,... | collective-permute-start | bytes 983048 | tf_op jit(solution)/shard_map/row_zlo/ppermute | solution.py:340
  88.1 4.1 %collective-permute-start.22 = (f32[80,80]{1,0:T(8,128)S(1)}, f32[80,80]{1,0:T(8,128)S(1)}, u32[]{:S(2)}, u32[]{:S(2)}) collective-permute-start(f32[80,80]{1,0:T(8,128)S(1)} %get-tuple-element.48.refs_0_), channel_id=1, source_target_pairs={{0,192},{16,208},{32,224},{48,240},{64,0},{80,16},{96,32},{112,48}... | collective-permute-start | bytes 76808 | tf_op jit(solution)/shard_map/inner_z/ppermute | solution.py:66
  89.9 6.9 %collective-permute-start.21 = (f32[80,80]{1,0:T(8,128)S(1)}, f32[80,80]{1,0:T(8,128)S(1)}, u32[]{:S(2)}, u32[]{:S(2)}) collective-permute-start(f32[80,80]{1,0:T(8,128)S(1)} %get-tuple-element.48.refs_0_), channel_id=1, source_target_pairs={{0,128},{16,144},{32,160},{48,176},{64,192},{80,208},{96,224},{112... | collective-permute-start | bytes 76808 | tf_op jit(solution)/shard_map/inner_z/ppermute | solution.py:66
  92.2 5.5 %collective-permute-start.20 = (f32[80,80]{1,0:T(8,128)S(1)}, f32[80,80]{1,0:T(8,128)S(1)}, u32[]{:S(2)}, u32[]{:S(2)}) collective-permute-start(f32[80,80]{1,0:T(8,128)S(1)} %get-tuple-element.48.refs_0_), channel_id=1, source_target_pairs={{0,64},{16,80},{32,96},{48,112},{64,128},{80,144},{96,160},{112,17... | collective-permute-start | bytes 76808 | tf_op jit(solution)/shard_map/inner_z/ppermute | solution.py:66
  98.4 17.0 %collective-permute-start.27 = (f32[2,4,80,256]{3,2,1,0:T(8,128)S(1)}, f32[2,4,80,256]{3,2,1,0:T(8,128)S(1)}, u32[]{:S(2)}, u32[]{:S(2)}) collective-permute-start(f32[2,4,80,256]{3,2,1,0:T(8,128)S(1)} %get-tuple-element.53.refs_1_), channel_id=1, source_target_pairs={{0,1},{1,0},{2,3},{3,2},{4,5},{5,4},{6,7},{7,6},{8,9},{9,8},{10,11... | collective-permute-start | bytes 1966088 | tf_op jit(solution)/shard_map/row_core/ppermute | solution.py:348
  109.9 4.4 %collective-permute-start.25 = (f32[80,80]{1,0:T(8,128)S(1)}, f32[80,80]{1,0:T(8,128)S(1)}, u32[]{:S(2)}, u32[]{:S(2)}) collective-permute-start(f32[80,80]{1,0:T(8,128)S(1)} %get-tuple-element.50.refs_0_), channel_id=1, source_target_pairs={{0,32},{16,48},{32,0},{48,16},{64,96},{80,112},{96,64},{112,80},{1... | collective-permute-start | bytes 76808 | tf_op jit(solution)/shard_map/inner_x/ppermute | solution.py:66
  110.7 4.7 %collective-permute-start.24 = (f32[80,80]{1,0:T(8,128)S(1)}, f32[80,80]{1,0:T(8,128)S(1)}, u32[]{:S(2)}, u32[]{:S(2)}) collective-permute-start(f32[80,80]{1,0:T(8,128)S(1)} %get-tuple-element.50.refs_0_), channel_id=1, source_target_pairs={{0,16},{16,32},{32,48},{48,0},{64,80},{80,96},{96,112},{112,64},{1... | collective-permute-start | bytes 76808 | tf_op jit(solution)/shard_map/inner_x/ppermute | solution.py:66
  116.8 4.4 %collective-permute-start.31 = (f32[80,80]{1,0:T(8,128)S(1)}, f32[80,80]{1,0:T(8,128)S(1)}, u32[]{:S(2)}, u32[]{:S(2)}) collective-permute-start(f32[80,80]{1,0:T(8,128)S(1)} %get-tuple-element.56), channel_id=1, source_target_pairs={{0,8},{1,9},{2,10},{3,11},{4,12},{5,13},{6,14},{7,15},{8,0},{9,1},... | collective-permute-start | bytes 76808 | tf_op jit(solution)/shard_map/inner_gy/ppermute | solution.py:66
  122.1 5.8 %collective-permute-start.33 = (f32[4,80,80]{2,1,0:T(8,128)S(1)}, f32[4,80,80]{2,1,0:T(8,128)S(1)}, u32[]{:S(2)}, u32[]{:S(2)}) collective-permute-start(f32[4,80,80]{2,1,0:T(8,128)S(1)} %get-tuple-element.60), channel_id=1, source_target_pairs={{0,2},{1,3},{2,0},{3,1},{4,6},{5,7},{6,4},{7,5},{8,10},{9,11},{10,... | collective-permute-start | bytes 307208 | tf_op jit(solution)/shard_map/inner_zlo/ppermute | solution.py:359
  125.2 11.9 %collective-permute-start.28 = (f32[320,256]{1,0:T(8,128)}, f32[320,256]{1,0:T(8,128)}, u32[]{:S(2)}, u32[]{:S(2)}) collective-permute-start(f32[320,256]{1,0:T(8,128)} %get-tuple-element.54), channel_id=1, source_target_pairs={{0,16},{16,32},{32,48},{48,0},{64,80},{80,96},{96,112},{112,64},{1... | collective-permute-start | bytes 983048 | tf_op jit(solution)/shard_map/pair_two/ppermute | solution.py:355
  125.2 11.9 %collective-permute-start.29 = (f32[320,256]{1,0:T(8,128)}, f32[320,256]{1,0:T(8,128)}, u32[]{:S(2)}, u32[]{:S(2)}) collective-permute-start(f32[320,256]{1,0:T(8,128)} %get-tuple-element.55), channel_id=1, source_target_pairs={{0,48},{16,0},{32,16},{48,32},{64,112},{80,64},{96,80},{112,96},{1... | collective-permute-start | bytes 983048 | tf_op jit(solution)/shard_map/pair_two/ppermute | solution.py:355
  128.7 5.2 %collective-permute-start.34 = (f32[2,4,80,80]{3,2,1,0:T(8,128)}, f32[2,4,80,80]{3,2,1,0:T(8,128)}, u32[]{:S(2)}, u32[]{:S(2)}) collective-permute-start(f32[2,4,80,80]{3,2,1,0:T(8,128)} %pad_maximum_fusion.refs_0_), channel_id=1, source_target_pairs={{0,1},{1,0},{2,3},{3,2},{4,5},{5,4},{6,7},{7,6},{8,9},{9,8},{10,11... | collective-permute-start | bytes 614408 | tf_op jit(solution)/shard_map/inner_core/ppermute | solution.py:361
  (11 other events, 59.7 us)

commit v3 on v2

--- a/solution.py
+++ b/solution.py
@@ -82,18 +82,25 @@
     )(place, *operands, *after)
 
 
+def tie(a, *after):
+    return pl.pallas_call(
+        lambda *refs: None,
+        out_shape=SDS(a.shape, a.dtype),
+        in_specs=[pl.BlockSpec(memory_space=pl.ANY)] * (1 + len(after)),
+        out_specs=pl.BlockSpec(memory_space=pl.ANY),
+        input_output_aliases={0: 0},
+    )(a, *after)
+
+
 def at(place_ref, index, size):
     return pl.ds(pl.multiple_of(place_ref[index] * size, size), size)
 
 
-def quarter_product_kernel(place, vec_ref, mat_ref, *rest):
+def quarter_product_kernel(vec_ref, mat_ref, *rest):
     outs, total_ref = rest[:4], rest[4]
     step = pl.program_id(0)
     rank, lanes = outs[0].shape
-    vec_high, vec_low = split(vec_ref[...])
-    high, low = split(mat_ref[...])
-    both = mul(jnp.concatenate([vec_high, vec_low], axis=0), high)
-    value = both[:rank] + both[rank:] + mul(vec_high, low)
+    value = mul(wide(vec_ref[...]), tall(mat_ref[...]))
 
     @pl.when(step == 0)
     def _():
@@ -105,11 +112,13 @@
 
     @pl.when(step == pl.num_programs(0) - 1)
     def _():
-        for k in range(4):
-            outs[k][...] = total_ref[:, at(place, k, lanes)]
-
-
-def quarter_products(place, vectors, matrix):
+        x = lax.rem(lax.axis_index("row"), 4)
+        for out, d in zip(outs, (2, 1, 3, 0)):
+            start = pl.multiple_of(lax.rem(x + d, 4) * lanes, lanes)
+            out[...] = total_ref[:, pl.ds(start, lanes)]
+
+
+def quarter_products(vectors, matrix):
     rank, rows = vectors.shape
     columns = matrix.shape[1]
     shape = SDS((rank, columns // 4), F32)
@@ -117,21 +126,18 @@
     return pl.pallas_call(
         quarter_product_kernel,
         out_shape=[shape] * 4,
-        grid_spec=pltpu.PrefetchScalarGridSpec(
-            num_scalar_prefetch=1,
-            grid=(4,),
-            in_specs=[
-                pl.BlockSpec((rank, depth), lambda i, place: (0, i)),
-                pl.BlockSpec((depth, columns), lambda i, place: (i, 0)),
-            ],
-            out_specs=[pl.BlockSpec(shape.shape, lambda i, place: (0, 0))] * 4,
-            scratch_shapes=[pltpu.VMEM((rank, columns), F32)],
-        ),
+        grid=(4,),
+        in_specs=[
+            pl.BlockSpec((rank, depth), lambda i: (0, i)),
+            pl.BlockSpec((depth, columns), lambda i: (i, 0)),
+        ],
+        out_specs=[pl.BlockSpec(shape.shape, lambda i: (0, 0))] * 4,
+        scratch_shapes=[pltpu.VMEM((rank, columns), F32)],
         compiler_params=pltpu.CompilerParams(vmem_limit_bytes=60 * 2**20),
         cost_estimate=pl.CostEstimate(
             flops=6 * rank * rows * rows, bytes_accessed=4 * (2 * rank * rows + rows * rows), transcendentals=0
         ),
-    )(place, vectors, matrix)
+    )(vectors, matrix)
 
 
 def sum_x_kernel(place, p0, p1, p2, p3, *rest):
@@ -238,21 +244,30 @@
 
 def update_kernel(place, *refs):
     near, (prod_two, vec_two) = refs[:3], refs[3:5]
-    first_ref, second_ref, left_ref, mat_ref, out_ref, new_ref, sems = refs[5:]
+    first_ref, second_ref, left_ref, mat_ref, out_ref, new_ref, right_ref, sems = refs[5:]
     rank, width = prod_two.shape
+    step = 256
     copies = []
-    for k in range(4):
-        if k < 3:
-            prod, vec = near[k][:rank], near[k][rank:]
+    for half in range(2):
+        if half == 0:
+            pair = jnp.concatenate([near[0][...], near[1][...]], axis=1)
         else:
-            prod, vec = prod_two[...], vec_two[...]
-        one = mul(first_ref[...], tall(jnp.concatenate([prod, vec], axis=0)))
-        two = mul(second_ref[...], tall(vec))
-        right = tall(jnp.concatenate([one, two], axis=0))
-        where = at(place, k, width)
-        new_ref[:, where] = mat_ref[:, where] - mul(left_ref[...], right)
-        copies.append(pltpu.make_async_copy(new_ref.at[:, where], out_ref.at[:, where], sems.at[k]))
-        copies[k].start()
+            far = jnp.concatenate([prod_two[...], vec_two[...]], axis=0)
+            pair = jnp.concatenate([near[2][...], far], axis=1)
+        one = mul(first_ref[...], tall(pair))
+        two = mul(second_ref[...], tall(pair[rank:]))
+        right_ref[...] = tall(jnp.concatenate([one, two], axis=0))
+        for m in range(mat_ref.shape[0] // step):
+            rows = pl.ds(m * step, step)
+            change = mul(left_ref[rows], right_ref[...])
+            for j in range(2):
+                where = at(place, 2 * half + j, width)
+                new_ref[rows, where] = mat_ref[rows, where] - change[:, j * width : (j + 1) * width]
+                copy = pltpu.make_async_copy(
+                    new_ref.at[rows, where], out_ref.at[rows, where], sems.at[len(copies)]
+                )
+                copy.start()
+                copies.append(copy)
     for copy in copies:
         copy.wait()
 
@@ -266,7 +281,11 @@
         in_specs=[pl.BlockSpec(memory_space=pltpu.SMEM)]
         + [pl.BlockSpec(memory_space=pltpu.VMEM)] * len(operands),
         out_specs=pl.BlockSpec(memory_space=pl.ANY),
-        scratch_shapes=[pltpu.VMEM((rows, columns), F32), pltpu.SemaphoreType.DMA((4,))],
+        scratch_shapes=[
+            pltpu.VMEM((rows, columns), F32),
+            pltpu.VMEM((6 * rank, columns // 2), BF16),
+            pltpu.SemaphoreType.DMA((16,)),
+        ],
         compiler_params=pltpu.CompilerParams(vmem_limit_bytes=20 * 2**20),
         cost_estimate=pl.CostEstimate(
             flops=12 * rows * rank * columns, bytes_accessed=8 * rows * columns, transcendentals=0
@@ -284,7 +303,6 @@
     y, zlo, core = col // 4, (col // 2) % 2, col % 2
     table = lambda entries: jnp.stack(entries).astype(jnp.int32)
     order = [x, (x + 3) % 4, (x + 1) % 4, (x + 2) % 4]
-    first = table([(x + 2) % 4, (x + 1) % 4, (x + 3) % 4, x, col % 4, y])
     from_z = [(z - d) % 4 for d in range(4)]
     away = table([(z + d) % 4 for d in range(4)] + from_z)
     lanes_at = [(y - d) % 4 for d in range(4)]
@@ -294,13 +312,13 @@
     quarter_shape = SDS((rank, lanes), F32)
     inner_shape = SDS((size, size), F32)
 
+    with jax.named_scope("products"):
+        opposite, right, left, mine = quarter_products(vectors, matrix)
+    with jax.named_scope("prod_sum_x"):
+        got = send([(2, opposite), (1, right), (3, left)], "row", SHIFT_X)
     with jax.named_scope("vec_turn"):
         turn = piece(piece(vectors, col % 4, size, 0), y, lanes, 1)
-        vec_part = lax.ppermute(turn, EVERYWHERE, TO_COLUMN)
-    with jax.named_scope("products"):
-        opposite, right, left, mine = quarter_products(first, vectors, matrix)
-    with jax.named_scope("prod_sum_x"):
-        got = send([(2, opposite), (1, right), (3, left)], "row", SHIFT_X)
+        vec_part = lax.ppermute(tie(turn, got[0][:8, :128]), EVERYWHERE, TO_COLUMN)
     with jax.named_scope("sum_x"):
         prods = whole_kernel(
             sum_x_kernel, [slice_shape] * 4, away, mine, *got,

time: 151 us -> 147 us (0.974)
  starting transfers between devices: 79.4 us -> 75.3 us
    ppermute x27, waiting for transfers between devices: 29.7 us -> 33.3 us  [send(): return [lax.ppermute(part, axis, shifts[d]) for d, part in parts]]
    ppermute x1, waiting for transfers between devices: 6.69 us -> 3.83 us  [body(): other = lax.ppermute(prod_part, EVERYWHERE, TO_ROW)]
    ppermute x1, starting transfers between devices: 9.6 us -> 7.46 us  [body(): other = lax.ppermute(mine, 'col', SWAP_CORE)]
    ppermute x1, starting transfers between devices: 5.42 us -> 3.33 us  [body(): other = lax.ppermute(prod_part, EVERYWHERE, TO_ROW)]
    ppermute x1, starting transfers between devices: 6.3 us -> 8.27 us  [body(): vec_part = lax.ppermute(tie(turn, got[0][:8, :128]), EVERYWHERE, TO_COLUMN)]
    pallas_call x1 -> x2, Pallas kernels: 6.95 us -> 6.46 us  [the longest x1 6.46 us: quarter_products(): pl.pallas_call(quarter_product_kernel, out_shape=[shape] * 4, grid=(4,),...]
  transfers between devices with their start and end apart: 35 -> 35, of which waited for: 20 -> 19; matrix products, arithmetic and copies ran while one was open for 1% -> 2% of each run, Pallas kernels for 2% -> 2%
where the time goes in v3:
time: 147 us
  starting transfers between devices  75.3 us (51%)
  waiting for transfers between devices  38.6 us (26%)
  Pallas kernels  26.4 us (18%)
  local copies, waits for them, and re-layouts  5.37 us (4%)
    ppermute x27, starting transfers between devices, send(): return [lax.ppermute(part, axis, shifts[d]) for d, part in parts]  47.8 us
    ppermute x27, waiting for transfers between devices, send(): return [lax.ppermute(part, axis, shifts[d]) for d, part in parts]  33.3 us
    pallas_call x8, Pallas kernels, whole_kernel(): pl.pallas_call(lambda place, *refs: kernel(place, *refs[:count], *refs[co...  10.9 us
    pallas_call x1, Pallas kernels, update(): pl.pallas_call(update_kernel, out_shape=SDS((rows, columns), F32), in_spe...  9.01 us
    ppermute x1, starting transfers between devices, body(): vec_part = lax.ppermute(tie(turn, got[0][:8, :128]), EVERYWHERE, TO_COLUMN)  8.27 us
    ppermute x1, starting transfers between devices, body(): other = lax.ppermute(mine, 'col', SWAP_CORE)  7.46 us
    pallas_call x1, Pallas kernels, quarter_products(): pl.pallas_call(quarter_product_kernel, out_shape=[shape] * 4, grid=(4,),...  6.46 us
    ppermute x1, waiting for transfers between devices, body(): other = lax.ppermute(prod_part, EVERYWHERE, TO_ROW)  3.83 us
  transfers between devices with their start and end apart: 35, of which 19 were waited for; matrix products, arithmetic and copies ran while one was open for 2% of the time, Pallas kernels for 2%

profile of v3, /device:TPU:1, one launch (start us, length us, event | category | flops | bytes accessed | tf_op | source)
XLA Modules:
  0.0 146.9 jit_solution(7350102742160923383)
XLA Ops:
  0.0 6.5 %products.1 = (f32[320,256]{1,0:T(8,128)}, f32[320,256]{1,0:T(8,128)}, f32[320,256]{1,0:T(8,128)}, f32[320,256]{1,0:T(8,128)}) custom-call(f32[320,1024]{1,0:T(8,128)} %bitcast.36, f32[1024,1024]{1,0:T(8,128)} %refs_8_.1), custom_call_target="tpu_custom_call" | custom-call | flops 2013265920 | bytes 6815744 | tf_op jit(solution)/shard_map/products/pallas_call | solution.py:126
  6.5 3.6 %collective-permute-start = (f32[320,256]{1,0:T(8,128)}, f32[320,256]{1,0:T(8,128)S(1)}, u32[]{:S(2)}, u32[]{:S(2)}) collective-permute-start(f32[320,256]{1,0:T(8,128)} %get-tuple-element.33), channel_id=1, source_target_pairs={{0,32},{16,48},{32,0},{48,16},{64,96},{80,112},{96,64},{112,80},{1... | collective-permute-start | bytes 983048 | tf_op jit(solution)/shard_map/prod_sum_x/ppermute | solution.py:66
  10.3 2.4 %collective-permute-start.2 = (f32[320,256]{1,0:T(8,128)}, f32[320,256]{1,0:T(8,128)S(1)}, u32[]{:S(2)}, u32[]{:S(2)}) collective-permute-start(f32[320,256]{1,0:T(8,128)} %get-tuple-element.35), channel_id=1, source_target_pairs={{0,48},{16,0},{32,16},{48,32},{64,112},{80,64},{96,80},{112,96},{1... | collective-permute-start | bytes 983048 | tf_op jit(solution)/shard_map/prod_sum_x/ppermute | solution.py:66
  13.5 3.3 %collective-permute-done.refs_1_ = f32[320,256]{1,0:T(8,128)S(1)} collective-permute-done((f32[320,256]{1,0:T(8,128)}, f32[320,256]{1,0:T(8,128)S(1)}, u32[]{:S(2)}, u32[]{:S(2)}) %collective-permute-start) | collective-permute-done | bytes 327712 | tf_op jit(solution)/shard_map/prod_sum_x/ppermute | solution.py:66
  17.4 8.3 %collective-permute-start.6 = (f32[80,256]{1,0:T(8,128)}, f32[80,256]{1,0:T(8,128)S(1)}, u32[]{:S(2)}, u32[]{:S(2)}) collective-permute-start(f32[80,256]{1,0:T(8,128)} %vec_turn.1), channel_id=1, source_target_pairs={{0,0},{1,64},{2,128},{3,192},{4,16},{5,80},{6,144},{7,208},{8,32},... | collective-permute-start | bytes 245768 | tf_op jit(solution)/shard_map/vec_turn/ppermute | solution.py:321
  27.3 3.0 %collective-permute-start.3 = (f32[80,256]{1,0:T(8,128)S(1)}, f32[80,256]{1,0:T(8,128)S(1)}, u32[]{:S(2)}, u32[]{:S(2)}) collective-permute-start(f32[80,256]{1,0:T(8,128)S(1)} %get-tuple-element.37), channel_id=1, source_target_pairs={{0,64},{16,80},{32,96},{48,112},{64,128},{80,144},{96,160},{112,17... | collective-permute-start | bytes 245768 | tf_op jit(solution)/shard_map/prod_sum_z/ppermute | solution.py:66
  30.4 5.1 %collective-permute-start.4 = (f32[80,256]{1,0:T(8,128)S(1)}, f32[80,256]{1,0:T(8,128)S(1)}, u32[]{:S(2)}, u32[]{:S(2)}) collective-permute-start(f32[80,256]{1,0:T(8,128)S(1)} %get-tuple-element.38), channel_id=1, source_target_pairs={{0,128},{16,144},{32,160},{48,176},{64,192},{80,208},{96,224},{112... | collective-permute-start | bytes 245768 | tf_op jit(solution)/shard_map/prod_sum_z/ppermute | solution.py:66
  35.5 2.4 %collective-permute-start.5 = (f32[80,256]{1,0:T(8,128)S(1)}, f32[80,256]{1,0:T(8,128)S(1)}, u32[]{:S(2)}, u32[]{:S(2)}) collective-permute-start(f32[80,256]{1,0:T(8,128)S(1)} %get-tuple-element.39), channel_id=1, source_target_pairs={{0,192},{16,208},{32,224},{48,240},{64,0},{80,16},{96,32},{112,48}... | collective-permute-start | bytes 245768 | tf_op jit(solution)/shard_map/prod_sum_z/ppermute | solution.py:66
  37.9 4.4 %collective-permute-done.4.refs_2_ = f32[80,256]{1,0:T(8,128)S(1)} collective-permute-done((f32[80,256]{1,0:T(8,128)S(1)}, f32[80,256]{1,0:T(8,128)S(1)}, u32[]{:S(2)}, u32[]{:S(2)}) %collective-permute-start.4) | collective-permute-done | bytes 81952 | tf_op jit(solution)/shard_map/prod_sum_z/ppermute | solution.py:66
  42.3 2.2 %collective-permute-done.5.refs_3_ = f32[80,256]{1,0:T(8,128)S(1)} collective-permute-done((f32[80,256]{1,0:T(8,128)S(1)}, f32[80,256]{1,0:T(8,128)S(1)}, u32[]{:S(2)}, u32[]{:S(2)}) %collective-permute-start.5) | collective-permute-done | bytes 81952 | tf_op jit(solution)/shard_map/prod_sum_z/ppermute | solution.py:66
  45.0 3.6 %collective-permute-start.8 = (f32[160,256]{1,0:T(8,128)S(1)}, f32[160,256]{1,0:T(8,128)S(1)}, u32[]{:S(2)}, u32[]{:S(2)}) collective-permute-start(f32[160,256]{1,0:T(8,128)S(1)} %get-tuple-element.40.refs_0_), channel_id=1, source_target_pairs={{0,192},{16,208},{32,224},{48,240},{64,0},{80,16},{96,32},{112,48}... | collective-permute-start | bytes 491528 | tf_op jit(solution)/shard_map/pair_z/ppermute | solution.py:66
  48.6 3.3 %collective-permute-start.11 = (f32[80,256]{1,0:T(8,128)S(1)}, f32[80,256]{1,0:T(8,128)S(1)}, u32[]{:S(2)}, u32[]{:S(2)}) collective-permute-start(f32[80,256]{1,0:T(8,128)S(1)} %get-tuple-element.41), channel_id=1, source_target_pairs={{0,0},{64,1},{128,2},{192,3},{16,4},{80,5},{144,6},{208,7},{32,8},... | collective-permute-start | bytes 245768 | tf_op jit(solution)/shard_map/prod_turn/ppermute | solution.py:334
  51.9 3.2 %collective-permute-done.8.refs_2_ = f32[160,256]{1,0:T(8,128)S(1)} collective-permute-done((f32[160,256]{1,0:T(8,128)S(1)}, f32[160,256]{1,0:T(8,128)S(1)}, u32[]{:S(2)}, u32[]{:S(2)}) %collective-permute-start.8) | collective-permute-done | bytes 163872 | tf_op jit(solution)/shard_map/pair_z/ppermute | solution.py:66
  55.2 4.1 %collective-permute-start.10 = (f32[80,256]{1,0:T(8,128)S(1)}, f32[80,256]{1,0:T(8,128)S(1)}, u32[]{:S(2)}, u32[]{:S(2)}) collective-permute-start(f32[80,256]{1,0:T(8,128)S(1)} %slice.14), channel_id=1, source_target_pairs={{0,192},{16,208},{32,224},{48,240},{64,0},{80,16},{96,32},{112,48}... | collective-permute-start | bytes 245768 | tf_op jit(solution)/shard_map/pair_z/ppermute | solution.py:66
  59.6 3.8 %collective-permute-done.11.refs_5_ = f32[80,256]{1,0:T(8,128)S(1)} collective-permute-done((f32[80,256]{1,0:T(8,128)S(1)}, f32[80,256]{1,0:T(8,128)S(1)}, u32[]{:S(2)}, u32[]{:S(2)}) %collective-permute-start.11) | collective-permute-done | bytes 81952 | tf_op jit(solution)/shard_map/prod_turn/ppermute | solution.py:334
  63.4 2.3 %collective-permute-done.10.refs_4_ = f32[80,256]{1,0:T(8,128)S(1)} collective-permute-done((f32[80,256]{1,0:T(8,128)S(1)}, f32[80,256]{1,0:T(8,128)S(1)}, u32[]{:S(2)}, u32[]{:S(2)}) %collective-permute-start.10) | collective-permute-done | bytes 81952 | tf_op jit(solution)/shard_map/pair_z/ppermute | solution.py:66
  66.7 3.2 %collective-permute-start.13 = (f32[640,256]{1,0:T(8,128)S(1)}, f32[640,256]{1,0:T(8,128)S(1)}, u32[]{:S(2)}, u32[]{:S(2)}) collective-permute-start(f32[640,256]{1,0:T(8,128)S(1)} %get-tuple-element.42.refs_0_), channel_id=1, source_target_pairs={{0,48},{16,0},{32,16},{48,32},{64,112},{80,64},{96,80},{112,96},{1... | collective-permute-start | bytes 1966088 | tf_op jit(solution)/shard_map/pair_x/ppermute | solution.py:66
  70.8 4.0 %collective-permute-start.15 = (f32[80,80]{1,0:T(8,128)S(1)}, f32[80,80]{1,0:T(8,128)S(1)}, u32[]{:S(2)}, u32[]{:S(2)}) collective-permute-start(f32[80,80]{1,0:T(8,128)S(1)} %get-tuple-element.45), channel_id=1, source_target_pairs={{0,8},{1,9},{2,10},{3,11},{4,12},{5,13},{6,14},{7,15},{8,0},{9,1},... | collective-permute-start | bytes 76808 | tf_op jit(solution)/shard_map/inner_y/ppermute | solution.py:66
  76.6 2.8 %collective-permute-start.18 = (f32[80,256]{1,0:T(8,128)S(1)}, f32[80,256]{1,0:T(8,128)S(1)}, u32[]{:S(2)}, u32[]{:S(2)}) collective-permute-start(f32[80,256]{1,0:T(8,128)S(1)} %get-tuple-element.47.refs_4_), channel_id=1, source_target_pairs={{0,8},{1,9},{2,10},{3,11},{4,12},{5,13},{6,14},{7,15},{8,0},{9,1},... | collective-permute-start | bytes 245768 | tf_op jit(solution)/shard_map/row_y/ppermute | solution.py:66
  79.5 2.6 %collective-permute-done.18.refs_6_ = f32[80,256]{1,0:T(8,128)S(1)} collective-permute-done((f32[80,256]{1,0:T(8,128)S(1)}, f32[80,256]{1,0:T(8,128)S(1)}, u32[]{:S(2)}, u32[]{:S(2)}) %collective-permute-start.18) | collective-permute-done | bytes 81952 | tf_op jit(solution)/shard_map/row_y/ppermute | solution.py:66
  82.1 2.2 %collective-permute-done.17.refs_5_ = f32[80,256]{1,0:T(8,128)S(1)} collective-permute-done((f32[80,256]{1,0:T(8,128)S(1)}, f32[80,256]{1,0:T(8,128)S(1)}, u32[]{:S(2)}, u32[]{:S(2)}) %collective-permute-start.17) | collective-permute-done | bytes 81952 | tf_op jit(solution)/shard_map/row_y/ppermute | solution.py:66
  85.0 2.8 %collective-permute-start.22 = (f32[80,80]{1,0:T(8,128)S(1)}, f32[80,80]{1,0:T(8,128)S(1)}, u32[]{:S(2)}, u32[]{:S(2)}) collective-permute-start(f32[80,80]{1,0:T(8,128)S(1)} %get-tuple-element.48.refs_0_), channel_id=1, source_target_pairs={{0,192},{16,208},{32,224},{48,240},{64,0},{80,16},{96,32},{112,48}... | collective-permute-start | bytes 76808 | tf_op jit(solution)/shard_map/inner_z/ppermute | solution.py:66
  87.7 2.2 %collective-permute-start.21 = (f32[80,80]{1,0:T(8,128)S(1)}, f32[80,80]{1,0:T(8,128)S(1)}, u32[]{:S(2)}, u32[]{:S(2)}) collective-permute-start(f32[80,80]{1,0:T(8,128)S(1)} %get-tuple-element.48.refs_0_), channel_id=1, source_target_pairs={{0,128},{16,144},{32,160},{48,176},{64,192},{80,208},{96,224},{112... | collective-permute-start | bytes 76808 | tf_op jit(solution)/shard_map/inner_z/ppermute | solution.py:66
  91.7 3.2 %collective-permute-done.21.refs_2_ = f32[80,80]{1,0:T(8,128)S(1)} collective-permute-done((f32[80,80]{1,0:T(8,128)S(1)}, f32[80,80]{1,0:T(8,128)S(1)}, u32[]{:S(2)}, u32[]{:S(2)}) %collective-permute-start.21) | collective-permute-done | bytes 25632 | tf_op jit(solution)/shard_map/inner_z/ppermute | solution.py:66
  96.2 7.5 %collective-permute-start.27 = (f32[2,4,80,256]{3,2,1,0:T(8,128)S(1)}, f32[2,4,80,256]{3,2,1,0:T(8,128)S(1)}, u32[]{:S(2)}, u32[]{:S(2)}) collective-permute-start(f32[2,4,80,256]{3,2,1,0:T(8,128)S(1)} %get-tuple-element.53.refs_1_), channel_id=1, source_target_pairs={{0,1},{1,0},{2,3},{3,2},{4,5},{5,4},{6,7},{7,6},{8,9},{9,8},{10,11... | collective-permute-start | bytes 1966088 | tf_op jit(solution)/shard_map/row_core/ppermute | solution.py:366
  104.5 2.9 %collective-permute-start.26 = (f32[80,80]{1,0:T(8,128)S(1)}, f32[80,80]{1,0:T(8,128)S(1)}, u32[]{:S(2)}, u32[]{:S(2)}) collective-permute-start(f32[80,80]{1,0:T(8,128)S(1)} %get-tuple-element.50.refs_0_), channel_id=1, source_target_pairs={{0,48},{16,0},{32,16},{48,32},{64,112},{80,64},{96,80},{112,96},{1... | collective-permute-start | bytes 76808 | tf_op jit(solution)/shard_map/inner_x/ppermute | solution.py:66
  108.5 3.4 %collective-permute-done.25.refs_2_ = f32[80,80]{1,0:T(8,128)S(1)} collective-permute-done((f32[80,80]{1,0:T(8,128)S(1)}, f32[80,80]{1,0:T(8,128)S(1)}, u32[]{:S(2)}, u32[]{:S(2)}) %collective-permute-start.25) | collective-permute-done | bytes 25632 | tf_op jit(solution)/shard_map/inner_x/ppermute | solution.py:66
  116.6 2.7 %collective-permute-done.31 = f32[80,80]{1,0:T(8,128)S(1)} collective-permute-done((f32[80,80]{1,0:T(8,128)S(1)}, f32[80,80]{1,0:T(8,128)S(1)}, u32[]{:S(2)}, u32[]{:S(2)}) %collective-permute-start.31) | collective-permute-done | bytes 25632 | tf_op jit(solution)/shard_map/inner_gy/ppermute | solution.py:66
  121.8 2.7 %collective-permute-start.29 = (f32[320,256]{1,0:T(8,128)}, f32[320,256]{1,0:T(8,128)}, u32[]{:S(2)}, u32[]{:S(2)}) collective-permute-start(f32[320,256]{1,0:T(8,128)} %get-tuple-element.55), channel_id=1, source_target_pairs={{0,48},{16,0},{32,16},{48,32},{64,112},{80,64},{96,80},{112,96},{1... | collective-permute-start | bytes 983048 | tf_op jit(solution)/shard_map/pair_two/ppermute | solution.py:373
  125.3 3.7 %collective-permute-start.34 = (f32[2,4,80,80]{3,2,1,0:T(8,128)}, f32[2,4,80,80]{3,2,1,0:T(8,128)}, u32[]{:S(2)}, u32[]{:S(2)}) collective-permute-start(f32[2,4,80,80]{3,2,1,0:T(8,128)} %pad_maximum_fusion.refs_0_), channel_id=1, source_target_pairs={{0,1},{1,0},{2,3},{3,2},{4,5},{5,4},{6,7},{7,6},{8,9},{9,8},{10,11... | collective-permute-start | bytes 614408 | tf_op jit(solution)/shard_map/inner_core/ppermute | solution.py:379
  133.7 4.0 %factor.1 = (bf16[320,1920]{1,0:T(8,128)(2,1)S(1)}, bf16[320,960]{1,0:T(8,128)(2,1)S(1)}) custom-call(s32[8]{0:T(128)S(1)} %stack.159.place, f32[2,4,80,80]{3,2,1,0:T(8,128)} %pad_maximum_fusion.refs_0_, f32[2,4,80,80]{3,2,1,0:T(8,128)} %collective-permute-done.34.refs_1_.refs_3_, f32[5,64,64]{2,1,0:T(8,128)S(1)} %copy-done.7, ...), custom_call_target="tpu_custom_call" | custom-call | bytes 2334720 | tf_op jit(solution)/shard_map/factor/pallas_call | solution.py:72
  137.7 9.0 %update.1 = f32[1024,1024]{1,0:T(8,128)} custom-call(s32[4]{0:T(128)S(1)} %pad_add_fusion.place, f32[640,256]{1,0:T(8,128)S(1)} %copy-done.3, f32[640,256]{1,0:T(8,128)S(1)} %collective-permute-done.12.refs_6_.refs_1_, f32[640,256]{1,0:T(8,128)S(1)} %collective-permute-done.13.refs_7_.refs_2_, f32[320,256]{1,0:T(8,128)} %collective-permute-done.28.refs_3_, ...), custom_call_target="tpu_custom_call" | custom-call | flops 4026531840 | bytes 8388608 | tf_op jit(solution)/shard_map/update/pallas_call | solution.py:278
  (75 shorter events, 26.2 us)
Async XLA Ops:
  6.5 10.4 %collective-permute-start = (f32[320,256]{1,0:T(8,128)}, f32[320,256]{1,0:T(8,128)S(1)}, u32[]{:S(2)}, u32[]{:S(2)}) collective-permute-start(f32[320,256]{1,0:T(8,128)} %get-tuple-element.33), channel_id=1, source_target_pairs={{0,32},{16,48},{32,0},{48,16},{64,96},{80,112},{96,64},{112,80},{1... | collective-permute-start | bytes 983048 | tf_op jit(solution)/shard_map/prod_sum_x/ppermute | solution.py:66
  10.0 15.7 %collective-permute-start.1 = (f32[320,256]{1,0:T(8,128)}, f32[320,256]{1,0:T(8,128)S(1)}, u32[]{:S(2)}, u32[]{:S(2)}) collective-permute-start(f32[320,256]{1,0:T(8,128)} %get-tuple-element.34), channel_id=1, source_target_pairs={{0,16},{16,32},{32,48},{48,0},{64,80},{80,96},{96,112},{112,64},{1... | collective-permute-start | bytes 983048 | tf_op jit(solution)/shard_map/prod_sum_x/ppermute | solution.py:66
  10.3 15.4 %collective-permute-start.2 = (f32[320,256]{1,0:T(8,128)}, f32[320,256]{1,0:T(8,128)S(1)}, u32[]{:S(2)}, u32[]{:S(2)}) collective-permute-start(f32[320,256]{1,0:T(8,128)} %get-tuple-element.35), channel_id=1, source_target_pairs={{0,48},{16,0},{32,16},{48,32},{64,112},{80,64},{96,80},{112,96},{1... | collective-permute-start | bytes 983048 | tf_op jit(solution)/shard_map/prod_sum_x/ppermute | solution.py:66
  17.4 20.4 %collective-permute-start.6 = (f32[80,256]{1,0:T(8,128)}, f32[80,256]{1,0:T(8,128)S(1)}, u32[]{:S(2)}, u32[]{:S(2)}) collective-permute-start(f32[80,256]{1,0:T(8,128)} %vec_turn.1), channel_id=1, source_target_pairs={{0,0},{1,64},{2,128},{3,192},{4,16},{5,80},{6,144},{7,208},{8,32},... | collective-permute-start | bytes 245768 | tf_op jit(solution)/shard_map/vec_turn/ppermute | solution.py:321
  27.3 10.5 %collective-permute-start.3 = (f32[80,256]{1,0:T(8,128)S(1)}, f32[80,256]{1,0:T(8,128)S(1)}, u32[]{:S(2)}, u32[]{:S(2)}) collective-permute-start(f32[80,256]{1,0:T(8,128)S(1)} %get-tuple-element.37), channel_id=1, source_target_pairs={{0,64},{16,80},{32,96},{48,112},{64,128},{80,144},{96,160},{112,17... | collective-permute-start | bytes 245768 | tf_op jit(solution)/shard_map/prod_sum_z/ppermute | solution.py:66
  30.4 11.9 %collective-permute-start.4 = (f32[80,256]{1,0:T(8,128)S(1)}, f32[80,256]{1,0:T(8,128)S(1)}, u32[]{:S(2)}, u32[]{:S(2)}) collective-permute-start(f32[80,256]{1,0:T(8,128)S(1)} %get-tuple-element.38), channel_id=1, source_target_pairs={{0,128},{16,144},{32,160},{48,176},{64,192},{80,208},{96,224},{112... | collective-permute-start | bytes 245768 | tf_op jit(solution)/shard_map/prod_sum_z/ppermute | solution.py:66
  35.5 9.0 %collective-permute-start.5 = (f32[80,256]{1,0:T(8,128)S(1)}, f32[80,256]{1,0:T(8,128)S(1)}, u32[]{:S(2)}, u32[]{:S(2)}) collective-permute-start(f32[80,256]{1,0:T(8,128)S(1)} %get-tuple-element.39), channel_id=1, source_target_pairs={{0,192},{16,208},{32,224},{48,240},{64,0},{80,16},{96,32},{112,48}... | collective-permute-start | bytes 245768 | tf_op jit(solution)/shard_map/prod_sum_z/ppermute | solution.py:66
  45.0 10.1 %collective-permute-start.8 = (f32[160,256]{1,0:T(8,128)S(1)}, f32[160,256]{1,0:T(8,128)S(1)}, u32[]{:S(2)}, u32[]{:S(2)}) collective-permute-start(f32[160,256]{1,0:T(8,128)S(1)} %get-tuple-element.40.refs_0_), channel_id=1, source_target_pairs={{0,192},{16,208},{32,224},{48,240},{64,0},{80,16},{96,32},{112,48}... | collective-permute-start | bytes 491528 | tf_op jit(solution)/shard_map/pair_z/ppermute | solution.py:66
  48.6 10.7 %collective-permute-start.7 = (f32[160,256]{1,0:T(8,128)S(1)}, f32[160,256]{1,0:T(8,128)S(1)}, u32[]{:S(2)}, u32[]{:S(2)}) collective-permute-start(f32[160,256]{1,0:T(8,128)S(1)} %get-tuple-element.40.refs_0_), channel_id=1, source_target_pairs={{0,64},{16,80},{32,96},{48,112},{64,128},{80,144},{96,160},{112,17... | collective-permute-start | bytes 491528 | tf_op jit(solution)/shard_map/pair_z/ppermute | solution.py:66
  48.6 14.8 %collective-permute-start.11 = (f32[80,256]{1,0:T(8,128)S(1)}, f32[80,256]{1,0:T(8,128)S(1)}, u32[]{:S(2)}, u32[]{:S(2)}) collective-permute-start(f32[80,256]{1,0:T(8,128)S(1)} %get-tuple-element.41), channel_id=1, source_target_pairs={{0,0},{64,1},{128,2},{192,3},{16,4},{80,5},{144,6},{208,7},{32,8},... | collective-permute-start | bytes 245768 | tf_op jit(solution)/shard_map/prod_turn/ppermute | solution.py:334
  55.2 10.6 %collective-permute-start.10 = (f32[80,256]{1,0:T(8,128)S(1)}, f32[80,256]{1,0:T(8,128)S(1)}, u32[]{:S(2)}, u32[]{:S(2)}) collective-permute-start(f32[80,256]{1,0:T(8,128)S(1)} %slice.14), channel_id=1, source_target_pairs={{0,192},{16,208},{32,224},{48,240},{64,0},{80,16},{96,32},{112,48}... | collective-permute-start | bytes 245768 | tf_op jit(solution)/shard_map/pair_z/ppermute | solution.py:66
  59.3 6.4 %collective-permute-start.9 = (f32[80,256]{1,0:T(8,128)S(1)}, f32[80,256]{1,0:T(8,128)S(1)}, u32[]{:S(2)}, u32[]{:S(2)}) collective-permute-start(f32[80,256]{1,0:T(8,128)S(1)} %slice.13), channel_id=1, source_target_pairs={{0,64},{16,80},{32,96},{48,112},{64,128},{80,144},{96,160},{112,17... | collective-permute-start | bytes 245768 | tf_op jit(solution)/shard_map/pair_z/ppermute | solution.py:66
  66.7 28.8 %collective-permute-start.13 = (f32[640,256]{1,0:T(8,128)S(1)}, f32[640,256]{1,0:T(8,128)S(1)}, u32[]{:S(2)}, u32[]{:S(2)}) collective-permute-start(f32[640,256]{1,0:T(8,128)S(1)} %get-tuple-element.42.refs_0_), channel_id=1, source_target_pairs={{0,48},{16,0},{32,16},{48,32},{64,112},{80,64},{96,80},{112,96},{1... | collective-permute-start | bytes 1966088 | tf_op jit(solution)/shard_map/pair_x/ppermute | solution.py:66
  70.0 25.6 %collective-permute-start.12 = (f32[640,256]{1,0:T(8,128)S(1)}, f32[640,256]{1,0:T(8,128)S(1)}, u32[]{:S(2)}, u32[]{:S(2)}) collective-permute-start(f32[640,256]{1,0:T(8,128)S(1)} %get-tuple-element.42.refs_0_), channel_id=1, source_target_pairs={{0,16},{16,32},{32,48},{48,0},{64,80},{80,96},{96,112},{112,64},{1... | collective-permute-start | bytes 1966088 | tf_op jit(solution)/shard_map/pair_x/ppermute | solution.py:66
  70.8 4.5 %collective-permute-start.14 = (f32[80,80]{1,0:T(8,128)S(1)}, f32[80,80]{1,0:T(8,128)S(1)}, u32[]{:S(2)}, u32[]{:S(2)}) collective-permute-start(f32[80,80]{1,0:T(8,128)S(1)} %get-tuple-element.44), channel_id=1, source_target_pairs={{0,4},{1,5},{2,6},{3,7},{4,8},{5,9},{6,10},{7,11},{8,12},{9,13},{1... | collective-permute-start | bytes 76808 | tf_op jit(solution)/shard_map/inner_y/ppermute | solution.py:66
  70.8 5.8 %collective-permute-start.15 = (f32[80,80]{1,0:T(8,128)S(1)}, f32[80,80]{1,0:T(8,128)S(1)}, u32[]{:S(2)}, u32[]{:S(2)}) collective-permute-start(f32[80,80]{1,0:T(8,128)S(1)} %get-tuple-element.45), channel_id=1, source_target_pairs={{0,8},{1,9},{2,10},{3,11},{4,12},{5,13},{6,14},{7,15},{8,0},{9,1},... | collective-permute-start | bytes 76808 | tf_op jit(solution)/shard_map/inner_y/ppermute | solution.py:66
  74.8 4.7 %collective-permute-start.16 = (f32[80,80]{1,0:T(8,128)S(1)}, f32[80,80]{1,0:T(8,128)S(1)}, u32[]{:S(2)}, u32[]{:S(2)}) collective-permute-start(f32[80,80]{1,0:T(8,128)S(1)} %get-tuple-element.46), channel_id=1, source_target_pairs={{0,12},{1,13},{2,14},{3,15},{4,0},{5,1},{6,2},{7,3},{8,4},{9,5},{1... | collective-permute-start | bytes 76808 | tf_op jit(solution)/shard_map/inner_y/ppermute | solution.py:66
  76.6 5.4 %collective-permute-start.18 = (f32[80,256]{1,0:T(8,128)S(1)}, f32[80,256]{1,0:T(8,128)S(1)}, u32[]{:S(2)}, u32[]{:S(2)}) collective-permute-start(f32[80,256]{1,0:T(8,128)S(1)} %get-tuple-element.47.refs_4_), channel_id=1, source_target_pairs={{0,8},{1,9},{2,10},{3,11},{4,12},{5,13},{6,14},{7,15},{8,0},{9,1},... | collective-permute-start | bytes 245768 | tf_op jit(solution)/shard_map/row_y/ppermute | solution.py:66
  79.5 4.8 %collective-permute-start.17 = (f32[80,256]{1,0:T(8,128)S(1)}, f32[80,256]{1,0:T(8,128)S(1)}, u32[]{:S(2)}, u32[]{:S(2)}) collective-permute-start(f32[80,256]{1,0:T(8,128)S(1)} %get-tuple-element.47.refs_4_), channel_id=1, source_target_pairs={{0,4},{1,5},{2,6},{3,7},{4,8},{5,9},{6,10},{7,11},{8,12},{9,13},{1... | collective-permute-start | bytes 245768 | tf_op jit(solution)/shard_map/row_y/ppermute | solution.py:66
  84.8 10.7 %collective-permute-start.23 = (f32[4,80,256]{2,1,0:T(8,128)S(1)}, f32[4,80,256]{2,1,0:T(8,128)S(1)}, u32[]{:S(2)}, u32[]{:S(2)}) collective-permute-start(f32[4,80,256]{2,1,0:T(8,128)S(1)} %get-tuple-element.49.refs_4_), channel_id=1, source_target_pairs={{0,2},{1,3},{2,0},{3,1},{4,6},{5,7},{6,4},{7,5},{8,10},{9,11},{10,... | collective-permute-start | bytes 983048 | tf_op jit(solution)/shard_map/row_zlo/ppermute | solution.py:358
  85.0 5.0 %collective-permute-start.22 = (f32[80,80]{1,0:T(8,128)S(1)}, f32[80,80]{1,0:T(8,128)S(1)}, u32[]{:S(2)}, u32[]{:S(2)}) collective-permute-start(f32[80,80]{1,0:T(8,128)S(1)} %get-tuple-element.48.refs_0_), channel_id=1, source_target_pairs={{0,192},{16,208},{32,224},{48,240},{64,0},{80,16},{96,32},{112,48}... | collective-permute-start | bytes 76808 | tf_op jit(solution)/shard_map/inner_z/ppermute | solution.py:66
  87.7 7.2 %collective-permute-start.21 = (f32[80,80]{1,0:T(8,128)S(1)}, f32[80,80]{1,0:T(8,128)S(1)}, u32[]{:S(2)}, u32[]{:S(2)}) collective-permute-start(f32[80,80]{1,0:T(8,128)S(1)} %get-tuple-element.48.refs_0_), channel_id=1, source_target_pairs={{0,128},{16,144},{32,160},{48,176},{64,192},{80,208},{96,224},{112... | collective-permute-start | bytes 76808 | tf_op jit(solution)/shard_map/inner_z/ppermute | solution.py:66
  89.9 5.6 %collective-permute-start.20 = (f32[80,80]{1,0:T(8,128)S(1)}, f32[80,80]{1,0:T(8,128)S(1)}, u32[]{:S(2)}, u32[]{:S(2)}) collective-permute-start(f32[80,80]{1,0:T(8,128)S(1)} %get-tuple-element.48.refs_0_), channel_id=1, source_target_pairs={{0,64},{16,80},{32,96},{48,112},{64,128},{80,144},{96,160},{112,17... | collective-permute-start | bytes 76808 | tf_op jit(solution)/shard_map/inner_z/ppermute | solution.py:66
  96.2 16.1 %collective-permute-start.27 = (f32[2,4,80,256]{3,2,1,0:T(8,128)S(1)}, f32[2,4,80,256]{3,2,1,0:T(8,128)S(1)}, u32[]{:S(2)}, u32[]{:S(2)}) collective-permute-start(f32[2,4,80,256]{3,2,1,0:T(8,128)S(1)} %get-tuple-element.53.refs_1_), channel_id=1, source_target_pairs={{0,1},{1,0},{2,3},{3,2},{4,5},{5,4},{6,7},{7,6},{8,9},{9,8},{10,11... | collective-permute-start | bytes 1966088 | tf_op jit(solution)/shard_map/row_core/ppermute | solution.py:366
  107.4 4.5 %collective-permute-start.25 = (f32[80,80]{1,0:T(8,128)S(1)}, f32[80,80]{1,0:T(8,128)S(1)}, u32[]{:S(2)}, u32[]{:S(2)}) collective-permute-start(f32[80,80]{1,0:T(8,128)S(1)} %get-tuple-element.50.refs_0_), channel_id=1, source_target_pairs={{0,32},{16,48},{32,0},{48,16},{64,96},{80,112},{96,64},{112,80},{1... | collective-permute-start | bytes 76808 | tf_op jit(solution)/shard_map/inner_x/ppermute | solution.py:66
  107.4 4.9 %collective-permute-start.24 = (f32[80,80]{1,0:T(8,128)S(1)}, f32[80,80]{1,0:T(8,128)S(1)}, u32[]{:S(2)}, u32[]{:S(2)}) collective-permute-start(f32[80,80]{1,0:T(8,128)S(1)} %get-tuple-element.50.refs_0_), channel_id=1, source_target_pairs={{0,16},{16,32},{32,48},{48,0},{64,80},{80,96},{96,112},{112,64},{1... | collective-permute-start | bytes 76808 | tf_op jit(solution)/shard_map/inner_x/ppermute | solution.py:66
  114.9 4.4 %collective-permute-start.31 = (f32[80,80]{1,0:T(8,128)S(1)}, f32[80,80]{1,0:T(8,128)S(1)}, u32[]{:S(2)}, u32[]{:S(2)}) collective-permute-start(f32[80,80]{1,0:T(8,128)S(1)} %get-tuple-element.56), channel_id=1, source_target_pairs={{0,8},{1,9},{2,10},{3,11},{4,12},{5,13},{6,14},{7,15},{8,0},{9,1},... | collective-permute-start | bytes 76808 | tf_op jit(solution)/shard_map/inner_gy/ppermute | solution.py:66
  115.4 4.3 %collective-permute-start.30 = (f32[80,80]{1,0:T(8,128)S(1)}, f32[80,80]{1,0:T(8,128)S(1)}, u32[]{:S(2)}, u32[]{:S(2)}) collective-permute-start(f32[80,80]{1,0:T(8,128)S(1)} %get-tuple-element.56), channel_id=1, source_target_pairs={{0,4},{1,5},{2,6},{3,7},{4,8},{5,9},{6,10},{7,11},{8,12},{9,13},{1... | collective-permute-start | bytes 76808 | tf_op jit(solution)/shard_map/inner_gy/ppermute | solution.py:66
  119.8 4.8 %collective-permute-start.33 = (f32[4,80,80]{2,1,0:T(8,128)S(1)}, f32[4,80,80]{2,1,0:T(8,128)S(1)}, u32[]{:S(2)}, u32[]{:S(2)}) collective-permute-start(f32[4,80,80]{2,1,0:T(8,128)S(1)} %get-tuple-element.60), channel_id=1, source_target_pairs={{0,2},{1,3},{2,0},{3,1},{4,6},{5,7},{6,4},{7,5},{8,10},{9,11},{10,... | collective-permute-start | bytes 307208 | tf_op jit(solution)/shard_map/inner_zlo/ppermute | solution.py:377
  121.8 11.9 %collective-permute-start.28 = (f32[320,256]{1,0:T(8,128)}, f32[320,256]{1,0:T(8,128)}, u32[]{:S(2)}, u32[]{:S(2)}) collective-permute-start(f32[320,256]{1,0:T(8,128)} %get-tuple-element.54), channel_id=1, source_target_pairs={{0,16},{16,32},{32,48},{48,0},{64,80},{80,96},{96,112},{112,64},{1... | collective-permute-start | bytes 983048 | tf_op jit(solution)/shard_map/pair_two/ppermute | solution.py:373
  121.8 11.9 %collective-permute-start.29 = (f32[320,256]{1,0:T(8,128)}, f32[320,256]{1,0:T(8,128)}, u32[]{:S(2)}, u32[]{:S(2)}) collective-permute-start(f32[320,256]{1,0:T(8,128)} %get-tuple-element.55), channel_id=1, source_target_pairs={{0,48},{16,0},{32,16},{48,32},{64,112},{80,64},{96,80},{112,96},{1... | collective-permute-start | bytes 983048 | tf_op jit(solution)/shard_map/pair_two/ppermute | solution.py:373
  125.3 5.2 %collective-permute-start.34 = (f32[2,4,80,80]{3,2,1,0:T(8,128)}, f32[2,4,80,80]{3,2,1,0:T(8,128)}, u32[]{:S(2)}, u32[]{:S(2)}) collective-permute-start(f32[2,4,80,80]{3,2,1,0:T(8,128)} %pad_maximum_fusion.refs_0_), channel_id=1, source_target_pairs={{0,1},{1,0},{2,3},{3,2},{4,5},{5,4},{6,7},{7,6},{8,9},{9,8},{10,11... | collective-permute-start | bytes 614408 | tf_op jit(solution)/shard_map/inner_core/ppermute | solution.py:379
  (11 other events, 58.7 us)

commit v4 on v3

--- a/solution.py
+++ b/solution.py
@@ -184,17 +184,18 @@
         mine_ref[d] = part[...]
 
 
-def add_z_kernel(place, a, b, c, d, mine, other, left_ref, right_ref, sum_ref, both_ref, prod_ref, vec_ref):
+def add_z_kernel(place, a, b, c, d, mine, left_ref, right_ref, sum_ref, pass_ref, prod_ref, vec_ref):
     rank = prod_ref.shape[0]
+    sum_ref[...] = a[...] + b[...] + c[...] + d[...]
+    pass_ref[...] = mine[...]
+    prod_ref[...] = left_ref[:rank]
+    vec_ref[...] = right_ref[rank:]
+
+
+def add_x_kernel(place, a, b, c, d, mine, other, prod_ref, vec_ref, sum_ref, both_ref, prod_out, vec_out):
     sum_ref[...] = a[...] + b[...] + c[...] + d[...]
     both_ref[0] = mine[...]
     both_ref[1] = other[...]
-    prod_ref[...] = left_ref[:rank]
-    vec_ref[...] = right_ref[rank:]
-
-
-def add_x_kernel(place, a, b, c, d, prod_ref, vec_ref, sum_ref, prod_out, vec_out):
-    sum_ref[...] = a[...] + b[...] + c[...] + d[...]
     prod_out[...] = prod_ref[...]
     vec_out[...] = vec_ref[...]
 
@@ -354,21 +355,22 @@
         inner, mine = whole_kernel(
             sum_y_kernel, [inner_shape, SDS((4, size, lanes), F32)], away, inners[0], *got, *others
         )
-    with jax.named_scope("row_zlo"):
-        other = lax.ppermute(mine, "col", SWAP_ZLO)
     with jax.named_scope("inner_z"):
         got = send([(d, inner) for d in (1, 2, 3)], "row", SHIFT_Z)
         inner, mine, *two = whole_kernel(
-            add_z_kernel, [inner_shape, SDS((2, 4, size, lanes), F32), quarter_shape, quarter_shape],
-            away, inner, *got, mine, other, pair_left, pair_right,
+            add_z_kernel, [inner_shape, SDS((4, size, lanes), F32), quarter_shape, quarter_shape],
+            away, inner, *got, mine, pair_left, pair_right,
+        )
+    with jax.named_scope("row_zlo"):
+        other = lax.ppermute(mine, "col", SWAP_ZLO)
+    with jax.named_scope("inner_x"):
+        got = send([(d, inner) for d in (1, 2, 3)], "row", SHIFT_X)
+        inner, mine, *two = whole_kernel(
+            add_x_kernel, [inner_shape, SDS((2, 4, size, lanes), F32), quarter_shape, quarter_shape],
+            away, inner, *got, mine, other, *two,
         )
     with jax.named_scope("row_core"):
         other = lax.ppermute(mine, "col", SWAP_CORE)
-    with jax.named_scope("inner_x"):
-        got = send([(d, inner) for d in (1, 2, 3)], "row", SHIFT_X)
-        inner, *two = whole_kernel(
-            add_x_kernel, [inner_shape, quarter_shape, quarter_shape], away, inner, *got, *two, after=[other]
-        )
     with jax.named_scope("pair_two"):
         two = [lax.ppermute(two[0], "row", SHIFT_X[1]), lax.ppermute(two[1], "row", SHIFT_X[3])]
     with jax.named_scope("inner_gy"):
@@ -380,7 +382,7 @@
     with jax.named_scope("left"):
         (left,) = whole_kernel(
             left_kernel, [SDS((rows, 6 * rank), BF16)], pieces_at, vectors, mine, other,
-            scratch=[pltpu.VMEM((rank, rows), F32)], after=[inner_other],
+            scratch=[pltpu.VMEM((rank, rows), F32)], after=[inner],
         )
     with jax.named_scope("factor"):
         sides = whole_kernel(
@@ -389,7 +391,7 @@
             scratch=[
                 pltpu.VMEM((rank, rank), F32), pltpu.VMEM((4, rank, size), F32), pltpu.VMEM((rank, rank), F32)
             ],
-            after=two,
+            after=[*two, left],
         )
     with jax.named_scope("update"):
         return update(table(order), pair, pair_left, pair_right, *two, *sides, left, matrix)

time: 147 us -> 144 us (0.980)
  starting transfers between devices: 75.3 us -> 71.9 us
  waiting for transfers between devices: 38.6 us -> 40.6 us
  local copies, waits for them, and re-layouts: 5.37 us -> 3.42 us
    ppermute x27, starting transfers between devices: 47.8 us -> 43.6 us  [send(): return [lax.ppermute(part, axis, shifts[d]) for d, part in parts]]
    ppermute x1, starting transfers between devices: 7.46 us -> 10.4 us  [body(): other = lax.ppermute(mine, 'col', SWAP_CORE)]
    ppermute x1, waiting for transfers between devices: 0.03 us -> 2 us  [body(): inner = jnp.stack([inner, lax.ppermute(inner, 'col', SWAP_ZLO)])]
    unnamed x16 -> x12, local copies, waits for them, and re-layouts: 3.79 us -> 1.82 us
    ppermute x1, starting transfers between devices: 2.04 us -> 0.09 us  [body(): inner = jnp.stack([inner, lax.ppermute(inner, 'col', SWAP_ZLO)])]
    ppermute x1, starting transfers between devices: 3.65 us -> 2.16 us  [body(): inner_other = lax.ppermute(inner, 'col', SWAP_CORE)]
  transfers between devices with their start and end apart: 35 -> 35, of which waited for: 19 -> 19; matrix products, arithmetic and copies ran while one was open for 2% -> 1% of each run, Pallas kernels for 2% -> 3%
where the time goes in v4:
time: 144 us
  starting transfers between devices  71.9 us (50%)
  waiting for transfers between devices  40.6 us (28%)
  Pallas kernels  27.3 us (19%)
  local copies, waits for them, and re-layouts  3.42 us (2%)
    ppermute x27, starting transfers between devices, send(): return [lax.ppermute(part, axis, shifts[d]) for d, part in parts]  43.6 us
    ppermute x27, waiting for transfers between devices, send(): return [lax.ppermute(part, axis, shifts[d]) for d, part in parts]  34.7 us
    pallas_call x8, Pallas kernels, whole_kernel(): pl.pallas_call(lambda place, *refs: kernel(place, *refs[:count], *refs[co...  11.9 us
    ppermute x1, starting transfers between devices, body(): other = lax.ppermute(mine, 'col', SWAP_CORE)  10.4 us
    pallas_call x1, Pallas kernels, update(): pl.pallas_call(update_kernel, out_shape=SDS((rows, columns), F32), in_spe...  8.88 us
    ppermute x1, starting transfers between devices, body(): vec_part = lax.ppermute(tie(turn, got[0][:8, :128]), EVERYWHERE, TO_COLUMN)  8.27 us
    pallas_call x1, Pallas kernels, quarter_products(): pl.pallas_call(quarter_product_kernel, out_shape=[shape] * 4, grid=(4,),...  6.46 us
    ppermute x1, waiting for transfers between devices, body(): other = lax.ppermute(prod_part, EVERYWHERE, TO_ROW)  3.83 us
  transfers between devices with their start and end apart: 35, of which 19 were waited for; matrix products, arithmetic and copies ran while one was open for 1% of the time, Pallas kernels for 3%

profile of v4, /device:TPU:1, one launch (start us, length us, event | category | flops | bytes accessed | tf_op | source)
XLA Modules:
  0.0 143.8 jit_solution(11514197596410405290)
XLA Ops:
  0.0 6.5 %products.1 = (f32[320,256]{1,0:T(8,128)}, f32[320,256]{1,0:T(8,128)}, f32[320,256]{1,0:T(8,128)}, f32[320,256]{1,0:T(8,128)}) custom-call(f32[320,1024]{1,0:T(8,128)} %bitcast.36, f32[1024,1024]{1,0:T(8,128)} %refs_8_.1), custom_call_target="tpu_custom_call" | custom-call | flops 2013265920 | bytes 6815744 | tf_op jit(solution)/shard_map/products/pallas_call | solution.py:126
  6.5 3.6 %collective-permute-start = (f32[320,256]{1,0:T(8,128)}, f32[320,256]{1,0:T(8,128)S(1)}, u32[]{:S(2)}, u32[]{:S(2)}) collective-permute-start(f32[320,256]{1,0:T(8,128)} %get-tuple-element.34), channel_id=1, source_target_pairs={{0,32},{16,48},{32,0},{48,16},{64,96},{80,112},{96,64},{112,80},{1... | collective-permute-start | bytes 983048 | tf_op jit(solution)/shard_map/prod_sum_x/ppermute | solution.py:66
  10.3 2.4 %collective-permute-start.2 = (f32[320,256]{1,0:T(8,128)}, f32[320,256]{1,0:T(8,128)S(1)}, u32[]{:S(2)}, u32[]{:S(2)}) collective-permute-start(f32[320,256]{1,0:T(8,128)} %get-tuple-element.36), channel_id=1, source_target_pairs={{0,48},{16,0},{32,16},{48,32},{64,112},{80,64},{96,80},{112,96},{1... | collective-permute-start | bytes 983048 | tf_op jit(solution)/shard_map/prod_sum_x/ppermute | solution.py:66
  13.5 3.3 %collective-permute-done.refs_1_ = f32[320,256]{1,0:T(8,128)S(1)} collective-permute-done((f32[320,256]{1,0:T(8,128)}, f32[320,256]{1,0:T(8,128)S(1)}, u32[]{:S(2)}, u32[]{:S(2)}) %collective-permute-start) | collective-permute-done | bytes 327712 | tf_op jit(solution)/shard_map/prod_sum_x/ppermute | solution.py:66
  17.4 8.3 %collective-permute-start.6 = (f32[80,256]{1,0:T(8,128)}, f32[80,256]{1,0:T(8,128)S(1)}, u32[]{:S(2)}, u32[]{:S(2)}) collective-permute-start(f32[80,256]{1,0:T(8,128)} %vec_turn.1), channel_id=1, source_target_pairs={{0,0},{1,64},{2,128},{3,192},{4,16},{5,80},{6,144},{7,208},{8,32},... | collective-permute-start | bytes 245768 | tf_op jit(solution)/shard_map/vec_turn/ppermute | solution.py:322
  27.4 3.0 %collective-permute-start.3 = (f32[80,256]{1,0:T(8,128)S(1)}, f32[80,256]{1,0:T(8,128)S(1)}, u32[]{:S(2)}, u32[]{:S(2)}) collective-permute-start(f32[80,256]{1,0:T(8,128)S(1)} %get-tuple-element.38), channel_id=1, source_target_pairs={{0,64},{16,80},{32,96},{48,112},{64,128},{80,144},{96,160},{112,17... | collective-permute-start | bytes 245768 | tf_op jit(solution)/shard_map/prod_sum_z/ppermute | solution.py:66
  30.4 5.1 %collective-permute-start.4 = (f32[80,256]{1,0:T(8,128)S(1)}, f32[80,256]{1,0:T(8,128)S(1)}, u32[]{:S(2)}, u32[]{:S(2)}) collective-permute-start(f32[80,256]{1,0:T(8,128)S(1)} %get-tuple-element.39), channel_id=1, source_target_pairs={{0,128},{16,144},{32,160},{48,176},{64,192},{80,208},{96,224},{112... | collective-permute-start | bytes 245768 | tf_op jit(solution)/shard_map/prod_sum_z/ppermute | solution.py:66
  35.5 2.4 %collective-permute-start.5 = (f32[80,256]{1,0:T(8,128)S(1)}, f32[80,256]{1,0:T(8,128)S(1)}, u32[]{:S(2)}, u32[]{:S(2)}) collective-permute-start(f32[80,256]{1,0:T(8,128)S(1)} %get-tuple-element.40), channel_id=1, source_target_pairs={{0,192},{16,208},{32,224},{48,240},{64,0},{80,16},{96,32},{112,48}... | collective-permute-start | bytes 245768 | tf_op jit(solution)/shard_map/prod_sum_z/ppermute | solution.py:66
  37.9 4.4 %collective-permute-done.4.refs_2_ = f32[80,256]{1,0:T(8,128)S(1)} collective-permute-done((f32[80,256]{1,0:T(8,128)S(1)}, f32[80,256]{1,0:T(8,128)S(1)}, u32[]{:S(2)}, u32[]{:S(2)}) %collective-permute-start.4) | collective-permute-done | bytes 81952 | tf_op jit(solution)/shard_map/prod_sum_z/ppermute | solution.py:66
  42.3 2.2 %collective-permute-done.5.refs_3_ = f32[80,256]{1,0:T(8,128)S(1)} collective-permute-done((f32[80,256]{1,0:T(8,128)S(1)}, f32[80,256]{1,0:T(8,128)S(1)}, u32[]{:S(2)}, u32[]{:S(2)}) %collective-permute-start.5) | collective-permute-done | bytes 81952 | tf_op jit(solution)/shard_map/prod_sum_z/ppermute | solution.py:66
  45.0 3.6 %collective-permute-start.8 = (f32[160,256]{1,0:T(8,128)S(1)}, f32[160,256]{1,0:T(8,128)S(1)}, u32[]{:S(2)}, u32[]{:S(2)}) collective-permute-start(f32[160,256]{1,0:T(8,128)S(1)} %get-tuple-element.41.refs_0_), channel_id=1, source_target_pairs={{0,192},{16,208},{32,224},{48,240},{64,0},{80,16},{96,32},{112,48}... | collective-permute-start | bytes 491528 | tf_op jit(solution)/shard_map/pair_z/ppermute | solution.py:66
  48.6 3.3 %collective-permute-start.11 = (f32[80,256]{1,0:T(8,128)S(1)}, f32[80,256]{1,0:T(8,128)S(1)}, u32[]{:S(2)}, u32[]{:S(2)}) collective-permute-start(f32[80,256]{1,0:T(8,128)S(1)} %get-tuple-element.42), channel_id=1, source_target_pairs={{0,0},{64,1},{128,2},{192,3},{16,4},{80,5},{144,6},{208,7},{32,8},... | collective-permute-start | bytes 245768 | tf_op jit(solution)/shard_map/prod_turn/ppermute | solution.py:335
  51.9 3.2 %collective-permute-done.8.refs_2_ = f32[160,256]{1,0:T(8,128)S(1)} collective-permute-done((f32[160,256]{1,0:T(8,128)S(1)}, f32[160,256]{1,0:T(8,128)S(1)}, u32[]{:S(2)}, u32[]{:S(2)}) %collective-permute-start.8) | collective-permute-done | bytes 163872 | tf_op jit(solution)/shard_map/pair_z/ppermute | solution.py:66
  55.2 4.1 %collective-permute-start.10 = (f32[80,256]{1,0:T(8,128)S(1)}, f32[80,256]{1,0:T(8,128)S(1)}, u32[]{:S(2)}, u32[]{:S(2)}) collective-permute-start(f32[80,256]{1,0:T(8,128)S(1)} %slice.14), channel_id=1, source_target_pairs={{0,192},{16,208},{32,224},{48,240},{64,0},{80,16},{96,32},{112,48}... | collective-permute-start | bytes 245768 | tf_op jit(solution)/shard_map/pair_z/ppermute | solution.py:66
  59.6 3.8 %collective-permute-done.11.refs_5_ = f32[80,256]{1,0:T(8,128)S(1)} collective-permute-done((f32[80,256]{1,0:T(8,128)S(1)}, f32[80,256]{1,0:T(8,128)S(1)}, u32[]{:S(2)}, u32[]{:S(2)}) %collective-permute-start.11) | collective-permute-done | bytes 81952 | tf_op jit(solution)/shard_map/prod_turn/ppermute | solution.py:335
  63.4 2.3 %collective-permute-done.10.refs_4_ = f32[80,256]{1,0:T(8,128)S(1)} collective-permute-done((f32[80,256]{1,0:T(8,128)S(1)}, f32[80,256]{1,0:T(8,128)S(1)}, u32[]{:S(2)}, u32[]{:S(2)}) %collective-permute-start.10) | collective-permute-done | bytes 81952 | tf_op jit(solution)/shard_map/pair_z/ppermute | solution.py:66
  66.7 3.2 %collective-permute-start.13 = (f32[640,256]{1,0:T(8,128)S(1)}, f32[640,256]{1,0:T(8,128)S(1)}, u32[]{:S(2)}, u32[]{:S(2)}) collective-permute-start(f32[640,256]{1,0:T(8,128)S(1)} %get-tuple-element.43.refs_0_), channel_id=1, source_target_pairs={{0,48},{16,0},{32,16},{48,32},{64,112},{80,64},{96,80},{112,96},{1... | collective-permute-start | bytes 1966088 | tf_op jit(solution)/shard_map/pair_x/ppermute | solution.py:66
  70.8 4.0 %collective-permute-start.15 = (f32[80,80]{1,0:T(8,128)S(1)}, f32[80,80]{1,0:T(8,128)S(1)}, u32[]{:S(2)}, u32[]{:S(2)}) collective-permute-start(f32[80,80]{1,0:T(8,128)S(1)} %get-tuple-element.46), channel_id=1, source_target_pairs={{0,8},{1,9},{2,10},{3,11},{4,12},{5,13},{6,14},{7,15},{8,0},{9,1},... | collective-permute-start | bytes 76808 | tf_op jit(solution)/shard_map/inner_y/ppermute | solution.py:66
  76.6 2.8 %collective-permute-start.18 = (f32[80,256]{1,0:T(8,128)S(1)}, f32[80,256]{1,0:T(8,128)S(1)}, u32[]{:S(2)}, u32[]{:S(2)}) collective-permute-start(f32[80,256]{1,0:T(8,128)S(1)} %get-tuple-element.48.refs_4_), channel_id=1, source_target_pairs={{0,8},{1,9},{2,10},{3,11},{4,12},{5,13},{6,14},{7,15},{8,0},{9,1},... | collective-permute-start | bytes 245768 | tf_op jit(solution)/shard_map/row_y/ppermute | solution.py:66
  79.5 2.6 %collective-permute-done.18.refs_6_ = f32[80,256]{1,0:T(8,128)S(1)} collective-permute-done((f32[80,256]{1,0:T(8,128)S(1)}, f32[80,256]{1,0:T(8,128)S(1)}, u32[]{:S(2)}, u32[]{:S(2)}) %collective-permute-start.18) | collective-permute-done | bytes 81952 | tf_op jit(solution)/shard_map/row_y/ppermute | solution.py:66
  82.1 2.2 %collective-permute-done.17.refs_5_ = f32[80,256]{1,0:T(8,128)S(1)} collective-permute-done((f32[80,256]{1,0:T(8,128)S(1)}, f32[80,256]{1,0:T(8,128)S(1)}, u32[]{:S(2)}, u32[]{:S(2)}) %collective-permute-start.17) | collective-permute-done | bytes 81952 | tf_op jit(solution)/shard_map/row_y/ppermute | solution.py:66
  85.7 3.1 %collective-permute-start.21 = (f32[80,80]{1,0:T(8,128)S(1)}, f32[80,80]{1,0:T(8,128)S(1)}, u32[]{:S(2)}, u32[]{:S(2)}) collective-permute-start(f32[80,80]{1,0:T(8,128)S(1)} %get-tuple-element.49.refs_0_), channel_id=1, source_target_pairs={{0,128},{16,144},{32,160},{48,176},{64,192},{80,208},{96,224},{112... | collective-permute-start | bytes 76808 | tf_op jit(solution)/shard_map/inner_z/ppermute | solution.py:66
  88.8 3.6 %collective-permute-done.21.refs_2_ = f32[80,80]{1,0:T(8,128)S(1)} collective-permute-done((f32[80,80]{1,0:T(8,128)S(1)}, f32[80,80]{1,0:T(8,128)S(1)}, u32[]{:S(2)}, u32[]{:S(2)}) %collective-permute-start.21) | collective-permute-done | bytes 25632 | tf_op jit(solution)/shard_map/inner_z/ppermute | solution.py:66
  99.2 2.6 %collective-permute-done.24.refs_2_ = f32[80,80]{1,0:T(8,128)S(1)} collective-permute-done((f32[80,80]{1,0:T(8,128)S(1)}, f32[80,80]{1,0:T(8,128)S(1)}, u32[]{:S(2)}, u32[]{:S(2)}) %collective-permute-start.24) | collective-permute-done | bytes 25632 | tf_op jit(solution)/shard_map/inner_x/ppermute | solution.py:66
  103.6 10.4 %collective-permute-start.34 = (f32[2,4,80,256]{3,2,1,0:T(8,128)}, f32[2,4,80,256]{3,2,1,0:T(8,128)}, u32[]{:S(2)}, u32[]{:S(2)}) collective-permute-start(f32[2,4,80,256]{3,2,1,0:T(8,128)} %get-tuple-element.58.refs_1_), channel_id=1, source_target_pairs={{0,1},{1,0},{2,3},{3,2},{4,5},{5,4},{6,7},{7,6},{8,9},{9,8},{10,11... | collective-permute-start | bytes 1966088 | tf_op jit(solution)/shard_map/row_core/ppermute | solution.py:373
  116.9 2.7 %collective-permute-done.30 = f32[80,80]{1,0:T(8,128)S(1)} collective-permute-done((f32[80,80]{1,0:T(8,128)S(1)}, f32[80,80]{1,0:T(8,128)S(1)}, u32[]{:S(2)}, u32[]{:S(2)}) %collective-permute-start.30) | collective-permute-done | bytes 25632 | tf_op jit(solution)/shard_map/inner_gy/ppermute | solution.py:66
  120.8 2.7 %collective-permute-start.28 = (f32[320,256]{1,0:T(8,128)}, f32[320,256]{1,0:T(8,128)}, u32[]{:S(2)}, u32[]{:S(2)}) collective-permute-start(f32[320,256]{1,0:T(8,128)} %get-tuple-element.56), channel_id=1, source_target_pairs={{0,48},{16,0},{32,16},{48,32},{64,112},{80,64},{96,80},{112,96},{1... | collective-permute-start | bytes 983048 | tf_op jit(solution)/shard_map/pair_two/ppermute | solution.py:375
  123.5 2.0 %collective-permute-done.32 = f32[4,80,80]{2,1,0:T(8,128)S(1)} collective-permute-done((f32[4,80,80]{2,1,0:T(8,128)S(1)}, f32[4,80,80]{2,1,0:T(8,128)S(1)}, u32[]{:S(2)}, u32[]{:S(2)}) %collective-permute-start.32) | collective-permute-done | bytes 102432 | tf_op jit(solution)/shard_map/inner_zlo/ppermute | solution.py:379
  125.5 2.2 %collective-permute-start.33 = (f32[2,4,80,80]{3,2,1,0:T(8,128)S(1)}, f32[2,4,80,80]{3,2,1,0:T(8,128)}, u32[]{:S(2)}, u32[]{:S(2)}) collective-permute-start(f32[2,4,80,80]{3,2,1,0:T(8,128)S(1)} %pad_maximum_fusion.refs_3_.refs_0_), channel_id=1, source_target_pairs={{0,1},{1,0},{2,3},{3,2},{4,5},{5,4},{6,7},{7,6},{8,9},{9,8},{10,11... | collective-permute-start | bytes 614408 | tf_op jit(solution)/shard_map/inner_core/ppermute | solution.py:381
  127.8 2.8 %left.1.refs_5_.refs_7_ = bf16[1024,1920]{1,0:T(8,128)(2,1)S(1)} custom-call(s32[8]{0:T(128)S(1)} %stack.159.place, f32[320,1024]{1,0:T(8,128)S(1)} %bitcast.39, f32[2,4,80,256]{3,2,1,0:T(8,128)} %get-tuple-element.58.refs_1_, f32[2,4,80,256]{3,2,1,0:T(8,128)} %collective-permute-done.34.refs_2_, f32[2,4,80,80]{3,2,1,0:T(8,128)S(1)} %pad_maximum_fusion.refs_3_.refs_0_), custom_call_target="tpu_custom_call" | custom-call | bytes 6553600 | tf_op jit(solution)/shard_map/left/pallas_call | solution.py:72
  130.7 4.0 %factor.1 = (bf16[320,1920]{1,0:T(8,128)(2,1)S(1)}, bf16[320,960]{1,0:T(8,128)(2,1)S(1)}) custom-call(s32[8]{0:T(128)S(1)} %stack.159.place, f32[2,4,80,80]{3,2,1,0:T(8,128)S(1)} %pad_maximum_fusion.refs_3_.refs_0_, f32[2,4,80,80]{3,2,1,0:T(8,128)} %collective-permute-done.33.refs_1_, f32[5,64,64]{2,1,0:T(8,128)S(1)} %copy-done.5, ...), custom_call_target="tpu_custom_call" | custom-call | bytes 2334720 | tf_op jit(solution)/shard_map/factor/pallas_call | solution.py:72
  134.8 8.9 %update.1 = f32[1024,1024]{1,0:T(8,128)} custom-call(s32[4]{0:T(128)S(1)} %pad_add_fusion.place, f32[640,256]{1,0:T(8,128)S(1)} %copy-done.3, f32[640,256]{1,0:T(8,128)S(1)} %collective-permute-done.12.refs_5_.refs_1_, f32[640,256]{1,0:T(8,128)S(1)} %collective-permute-done.13.refs_6_.refs_2_, f32[320,256]{1,0:T(8,128)S(1)} %collective-permute-done.27.refs_3_, ...), custom_call_target="tpu_custom_call" | custom-call | flops 4026531840 | bytes 8388608 | tf_op jit(solution)/shard_map/update/pallas_call | solution.py:279
  (71 shorter events, 22.0 us)
Async XLA Ops:
  6.5 10.4 %collective-permute-start = (f32[320,256]{1,0:T(8,128)}, f32[320,256]{1,0:T(8,128)S(1)}, u32[]{:S(2)}, u32[]{:S(2)}) collective-permute-start(f32[320,256]{1,0:T(8,128)} %get-tuple-element.34), channel_id=1, source_target_pairs={{0,32},{16,48},{32,0},{48,16},{64,96},{80,112},{96,64},{112,80},{1... | collective-permute-start | bytes 983048 | tf_op jit(solution)/shard_map/prod_sum_x/ppermute | solution.py:66
  10.0 15.7 %collective-permute-start.1 = (f32[320,256]{1,0:T(8,128)}, f32[320,256]{1,0:T(8,128)S(1)}, u32[]{:S(2)}, u32[]{:S(2)}) collective-permute-start(f32[320,256]{1,0:T(8,128)} %get-tuple-element.35), channel_id=1, source_target_pairs={{0,16},{16,32},{32,48},{48,0},{64,80},{80,96},{96,112},{112,64},{1... | collective-permute-start | bytes 983048 | tf_op jit(solution)/shard_map/prod_sum_x/ppermute | solution.py:66
  10.3 15.4 %collective-permute-start.2 = (f32[320,256]{1,0:T(8,128)}, f32[320,256]{1,0:T(8,128)S(1)}, u32[]{:S(2)}, u32[]{:S(2)}) collective-permute-start(f32[320,256]{1,0:T(8,128)} %get-tuple-element.36), channel_id=1, source_target_pairs={{0,48},{16,0},{32,16},{48,32},{64,112},{80,64},{96,80},{112,96},{1... | collective-permute-start | bytes 983048 | tf_op jit(solution)/shard_map/prod_sum_x/ppermute | solution.py:66
  17.4 20.4 %collective-permute-start.6 = (f32[80,256]{1,0:T(8,128)}, f32[80,256]{1,0:T(8,128)S(1)}, u32[]{:S(2)}, u32[]{:S(2)}) collective-permute-start(f32[80,256]{1,0:T(8,128)} %vec_turn.1), channel_id=1, source_target_pairs={{0,0},{1,64},{2,128},{3,192},{4,16},{5,80},{6,144},{7,208},{8,32},... | collective-permute-start | bytes 245768 | tf_op jit(solution)/shard_map/vec_turn/ppermute | solution.py:322
  27.4 10.5 %collective-permute-start.3 = (f32[80,256]{1,0:T(8,128)S(1)}, f32[80,256]{1,0:T(8,128)S(1)}, u32[]{:S(2)}, u32[]{:S(2)}) collective-permute-start(f32[80,256]{1,0:T(8,128)S(1)} %get-tuple-element.38), channel_id=1, source_target_pairs={{0,64},{16,80},{32,96},{48,112},{64,128},{80,144},{96,160},{112,17... | collective-permute-start | bytes 245768 | tf_op jit(solution)/shard_map/prod_sum_z/ppermute | solution.py:66
  30.4 11.9 %collective-permute-start.4 = (f32[80,256]{1,0:T(8,128)S(1)}, f32[80,256]{1,0:T(8,128)S(1)}, u32[]{:S(2)}, u32[]{:S(2)}) collective-permute-start(f32[80,256]{1,0:T(8,128)S(1)} %get-tuple-element.39), channel_id=1, source_target_pairs={{0,128},{16,144},{32,160},{48,176},{64,192},{80,208},{96,224},{112... | collective-permute-start | bytes 245768 | tf_op jit(solution)/shard_map/prod_sum_z/ppermute | solution.py:66
  35.5 9.0 %collective-permute-start.5 = (f32[80,256]{1,0:T(8,128)S(1)}, f32[80,256]{1,0:T(8,128)S(1)}, u32[]{:S(2)}, u32[]{:S(2)}) collective-permute-start(f32[80,256]{1,0:T(8,128)S(1)} %get-tuple-element.40), channel_id=1, source_target_pairs={{0,192},{16,208},{32,224},{48,240},{64,0},{80,16},{96,32},{112,48}... | collective-permute-start | bytes 245768 | tf_op jit(solution)/shard_map/prod_sum_z/ppermute | solution.py:66
  45.0 10.1 %collective-permute-start.8 = (f32[160,256]{1,0:T(8,128)S(1)}, f32[160,256]{1,0:T(8,128)S(1)}, u32[]{:S(2)}, u32[]{:S(2)}) collective-permute-start(f32[160,256]{1,0:T(8,128)S(1)} %get-tuple-element.41.refs_0_), channel_id=1, source_target_pairs={{0,192},{16,208},{32,224},{48,240},{64,0},{80,16},{96,32},{112,48}... | collective-permute-start | bytes 491528 | tf_op jit(solution)/shard_map/pair_z/ppermute | solution.py:66
  48.6 10.7 %collective-permute-start.7 = (f32[160,256]{1,0:T(8,128)S(1)}, f32[160,256]{1,0:T(8,128)S(1)}, u32[]{:S(2)}, u32[]{:S(2)}) collective-permute-start(f32[160,256]{1,0:T(8,128)S(1)} %get-tuple-element.41.refs_0_), channel_id=1, source_target_pairs={{0,64},{16,80},{32,96},{48,112},{64,128},{80,144},{96,160},{112,17... | collective-permute-start | bytes 491528 | tf_op jit(solution)/shard_map/pair_z/ppermute | solution.py:66
  48.6 14.8 %collective-permute-start.11 = (f32[80,256]{1,0:T(8,128)S(1)}, f32[80,256]{1,0:T(8,128)S(1)}, u32[]{:S(2)}, u32[]{:S(2)}) collective-permute-start(f32[80,256]{1,0:T(8,128)S(1)} %get-tuple-element.42), channel_id=1, source_target_pairs={{0,0},{64,1},{128,2},{192,3},{16,4},{80,5},{144,6},{208,7},{32,8},... | collective-permute-start | bytes 245768 | tf_op jit(solution)/shard_map/prod_turn/ppermute | solution.py:335
  55.2 10.6 %collective-permute-start.10 = (f32[80,256]{1,0:T(8,128)S(1)}, f32[80,256]{1,0:T(8,128)S(1)}, u32[]{:S(2)}, u32[]{:S(2)}) collective-permute-start(f32[80,256]{1,0:T(8,128)S(1)} %slice.14), channel_id=1, source_target_pairs={{0,192},{16,208},{32,224},{48,240},{64,0},{80,16},{96,32},{112,48}... | collective-permute-start | bytes 245768 | tf_op jit(solution)/shard_map/pair_z/ppermute | solution.py:66
  59.3 6.4 %collective-permute-start.9 = (f32[80,256]{1,0:T(8,128)S(1)}, f32[80,256]{1,0:T(8,128)S(1)}, u32[]{:S(2)}, u32[]{:S(2)}) collective-permute-start(f32[80,256]{1,0:T(8,128)S(1)} %slice.13), channel_id=1, source_target_pairs={{0,64},{16,80},{32,96},{48,112},{64,128},{80,144},{96,160},{112,17... | collective-permute-start | bytes 245768 | tf_op jit(solution)/shard_map/pair_z/ppermute | solution.py:66
  66.7 27.4 %collective-permute-start.13 = (f32[640,256]{1,0:T(8,128)S(1)}, f32[640,256]{1,0:T(8,128)S(1)}, u32[]{:S(2)}, u32[]{:S(2)}) collective-permute-start(f32[640,256]{1,0:T(8,128)S(1)} %get-tuple-element.43.refs_0_), channel_id=1, source_target_pairs={{0,48},{16,0},{32,16},{48,32},{64,112},{80,64},{96,80},{112,96},{1... | collective-permute-start | bytes 1966088 | tf_op jit(solution)/shard_map/pair_x/ppermute | solution.py:66
  70.0 24.1 %collective-permute-start.12 = (f32[640,256]{1,0:T(8,128)S(1)}, f32[640,256]{1,0:T(8,128)S(1)}, u32[]{:S(2)}, u32[]{:S(2)}) collective-permute-start(f32[640,256]{1,0:T(8,128)S(1)} %get-tuple-element.43.refs_0_), channel_id=1, source_target_pairs={{0,16},{16,32},{32,48},{48,0},{64,80},{80,96},{96,112},{112,64},{1... | collective-permute-start | bytes 1966088 | tf_op jit(solution)/shard_map/pair_x/ppermute | solution.py:66
  70.8 4.5 %collective-permute-start.14 = (f32[80,80]{1,0:T(8,128)S(1)}, f32[80,80]{1,0:T(8,128)S(1)}, u32[]{:S(2)}, u32[]{:S(2)}) collective-permute-start(f32[80,80]{1,0:T(8,128)S(1)} %get-tuple-element.45), channel_id=1, source_target_pairs={{0,4},{1,5},{2,6},{3,7},{4,8},{5,9},{6,10},{7,11},{8,12},{9,13},{1... | collective-permute-start | bytes 76808 | tf_op jit(solution)/shard_map/inner_y/ppermute | solution.py:66
  70.8 5.8 %collective-permute-start.15 = (f32[80,80]{1,0:T(8,128)S(1)}, f32[80,80]{1,0:T(8,128)S(1)}, u32[]{:S(2)}, u32[]{:S(2)}) collective-permute-start(f32[80,80]{1,0:T(8,128)S(1)} %get-tuple-element.46), channel_id=1, source_target_pairs={{0,8},{1,9},{2,10},{3,11},{4,12},{5,13},{6,14},{7,15},{8,0},{9,1},... | collective-permute-start | bytes 76808 | tf_op jit(solution)/shard_map/inner_y/ppermute | solution.py:66
  74.8 4.7 %collective-permute-start.16 = (f32[80,80]{1,0:T(8,128)S(1)}, f32[80,80]{1,0:T(8,128)S(1)}, u32[]{:S(2)}, u32[]{:S(2)}) collective-permute-start(f32[80,80]{1,0:T(8,128)S(1)} %get-tuple-element.47), channel_id=1, source_target_pairs={{0,12},{1,13},{2,14},{3,15},{4,0},{5,1},{6,2},{7,3},{8,4},{9,5},{1... | collective-permute-start | bytes 76808 | tf_op jit(solution)/shard_map/inner_y/ppermute | solution.py:66
  75.3 4.2 %collective-permute-start.19 = (f32[80,256]{1,0:T(8,128)S(1)}, f32[80,256]{1,0:T(8,128)S(1)}, u32[]{:S(2)}, u32[]{:S(2)}) collective-permute-start(f32[80,256]{1,0:T(8,128)S(1)} %get-tuple-element.48.refs_4_), channel_id=1, source_target_pairs={{0,12},{1,13},{2,14},{3,15},{4,0},{5,1},{6,2},{7,3},{8,4},{9,5},{1... | collective-permute-start | bytes 245768 | tf_op jit(solution)/shard_map/row_y/ppermute | solution.py:66
  76.6 5.4 %collective-permute-start.18 = (f32[80,256]{1,0:T(8,128)S(1)}, f32[80,256]{1,0:T(8,128)S(1)}, u32[]{:S(2)}, u32[]{:S(2)}) collective-permute-start(f32[80,256]{1,0:T(8,128)S(1)} %get-tuple-element.48.refs_4_), channel_id=1, source_target_pairs={{0,8},{1,9},{2,10},{3,11},{4,12},{5,13},{6,14},{7,15},{8,0},{9,1},... | collective-permute-start | bytes 245768 | tf_op jit(solution)/shard_map/row_y/ppermute | solution.py:66
  79.5 4.8 %collective-permute-start.17 = (f32[80,256]{1,0:T(8,128)S(1)}, f32[80,256]{1,0:T(8,128)S(1)}, u32[]{:S(2)}, u32[]{:S(2)}) collective-permute-start(f32[80,256]{1,0:T(8,128)S(1)} %get-tuple-element.48.refs_4_), channel_id=1, source_target_pairs={{0,4},{1,5},{2,6},{3,7},{4,8},{5,9},{6,10},{7,11},{8,12},{9,13},{1... | collective-permute-start | bytes 245768 | tf_op jit(solution)/shard_map/row_y/ppermute | solution.py:66
  85.7 6.8 %collective-permute-start.21 = (f32[80,80]{1,0:T(8,128)S(1)}, f32[80,80]{1,0:T(8,128)S(1)}, u32[]{:S(2)}, u32[]{:S(2)}) collective-permute-start(f32[80,80]{1,0:T(8,128)S(1)} %get-tuple-element.49.refs_0_), channel_id=1, source_target_pairs={{0,128},{16,144},{32,160},{48,176},{64,192},{80,208},{96,224},{112... | collective-permute-start | bytes 76808 | tf_op jit(solution)/shard_map/inner_z/ppermute | solution.py:66
  88.8 5.3 %collective-permute-start.20 = (f32[80,80]{1,0:T(8,128)S(1)}, f32[80,80]{1,0:T(8,128)S(1)}, u32[]{:S(2)}, u32[]{:S(2)}) collective-permute-start(f32[80,80]{1,0:T(8,128)S(1)} %get-tuple-element.49.refs_0_), channel_id=1, source_target_pairs={{0,64},{16,80},{32,96},{48,112},{64,128},{80,144},{96,160},{112,17... | collective-permute-start | bytes 76808 | tf_op jit(solution)/shard_map/inner_z/ppermute | solution.py:66
  94.7 7.2 %collective-permute-start.26 = (f32[4,80,256]{2,1,0:T(8,128)S(1)}, f32[4,80,256]{2,1,0:T(8,128)S(1)}, u32[]{:S(2)}, u32[]{:S(2)}) collective-permute-start(f32[4,80,256]{2,1,0:T(8,128)S(1)} %get-tuple-element.52.refs_4_), channel_id=1, source_target_pairs={{0,2},{1,3},{2,0},{3,1},{4,6},{5,7},{6,4},{7,5},{8,10},{9,11},{10,... | collective-permute-start | bytes 983048 | tf_op jit(solution)/shard_map/row_zlo/ppermute | solution.py:365
  97.2 4.6 %collective-permute-start.24 = (f32[80,80]{1,0:T(8,128)S(1)}, f32[80,80]{1,0:T(8,128)S(1)}, u32[]{:S(2)}, u32[]{:S(2)}) collective-permute-start(f32[80,80]{1,0:T(8,128)S(1)} %get-tuple-element.51.refs_0_), channel_id=1, source_target_pairs={{0,32},{16,48},{32,0},{48,16},{64,96},{80,112},{96,64},{112,80},{1... | collective-permute-start | bytes 76808 | tf_op jit(solution)/shard_map/inner_x/ppermute | solution.py:66
  97.4 4.5 %collective-permute-start.23 = (f32[80,80]{1,0:T(8,128)S(1)}, f32[80,80]{1,0:T(8,128)S(1)}, u32[]{:S(2)}, u32[]{:S(2)}) collective-permute-start(f32[80,80]{1,0:T(8,128)S(1)} %get-tuple-element.51.refs_0_), channel_id=1, source_target_pairs={{0,16},{16,32},{32,48},{48,0},{64,80},{80,96},{96,112},{112,64},{1... | collective-permute-start | bytes 76808 | tf_op jit(solution)/shard_map/inner_x/ppermute | solution.py:66
  103.6 24.2 %collective-permute-start.34 = (f32[2,4,80,256]{3,2,1,0:T(8,128)}, f32[2,4,80,256]{3,2,1,0:T(8,128)}, u32[]{:S(2)}, u32[]{:S(2)}) collective-permute-start(f32[2,4,80,256]{3,2,1,0:T(8,128)} %get-tuple-element.58.refs_1_), channel_id=1, source_target_pairs={{0,1},{1,0},{2,3},{3,2},{4,5},{5,4},{6,7},{7,6},{8,9},{9,8},{10,11... | collective-permute-start | bytes 1966088 | tf_op jit(solution)/shard_map/row_core/ppermute | solution.py:373
  115.2 4.4 %collective-permute-start.30 = (f32[80,80]{1,0:T(8,128)S(1)}, f32[80,80]{1,0:T(8,128)S(1)}, u32[]{:S(2)}, u32[]{:S(2)}) collective-permute-start(f32[80,80]{1,0:T(8,128)S(1)} %get-tuple-element.57), channel_id=1, source_target_pairs={{0,8},{1,9},{2,10},{3,11},{4,12},{5,13},{6,14},{7,15},{8,0},{9,1},... | collective-permute-start | bytes 76808 | tf_op jit(solution)/shard_map/inner_gy/ppermute | solution.py:66
  115.8 4.8 %collective-permute-start.29 = (f32[80,80]{1,0:T(8,128)S(1)}, f32[80,80]{1,0:T(8,128)S(1)}, u32[]{:S(2)}, u32[]{:S(2)}) collective-permute-start(f32[80,80]{1,0:T(8,128)S(1)} %get-tuple-element.57), channel_id=1, source_target_pairs={{0,4},{1,5},{2,6},{3,7},{4,8},{5,9},{6,10},{7,11},{8,12},{9,13},{1... | collective-permute-start | bytes 76808 | tf_op jit(solution)/shard_map/inner_gy/ppermute | solution.py:66
  120.6 4.9 %collective-permute-start.32 = (f32[4,80,80]{2,1,0:T(8,128)S(1)}, f32[4,80,80]{2,1,0:T(8,128)S(1)}, u32[]{:S(2)}, u32[]{:S(2)}) collective-permute-start(f32[4,80,80]{2,1,0:T(8,128)S(1)} %get-tuple-element.62), channel_id=1, source_target_pairs={{0,2},{1,3},{2,0},{3,1},{4,6},{5,7},{6,4},{7,5},{8,10},{9,11},{10,... | collective-permute-start | bytes 307208 | tf_op jit(solution)/shard_map/inner_zlo/ppermute | solution.py:379
  120.7 9.9 %collective-permute-start.27 = (f32[320,256]{1,0:T(8,128)}, f32[320,256]{1,0:T(8,128)S(1)}, u32[]{:S(2)}, u32[]{:S(2)}) collective-permute-start(f32[320,256]{1,0:T(8,128)} %get-tuple-element.55), channel_id=1, source_target_pairs={{0,16},{16,32},{32,48},{48,0},{64,80},{80,96},{96,112},{112,64},{1... | collective-permute-start | bytes 983048 | tf_op jit(solution)/shard_map/pair_two/ppermute | solution.py:375
  120.8 9.8 %collective-permute-start.28 = (f32[320,256]{1,0:T(8,128)}, f32[320,256]{1,0:T(8,128)}, u32[]{:S(2)}, u32[]{:S(2)}) collective-permute-start(f32[320,256]{1,0:T(8,128)} %get-tuple-element.56), channel_id=1, source_target_pairs={{0,48},{16,0},{32,16},{48,32},{64,112},{80,64},{96,80},{112,96},{1... | collective-permute-start | bytes 983048 | tf_op jit(solution)/shard_map/pair_two/ppermute | solution.py:375
  125.5 5.2 %collective-permute-start.33 = (f32[2,4,80,80]{3,2,1,0:T(8,128)S(1)}, f32[2,4,80,80]{3,2,1,0:T(8,128)}, u32[]{:S(2)}, u32[]{:S(2)}) collective-permute-start(f32[2,4,80,80]{3,2,1,0:T(8,128)S(1)} %pad_maximum_fusion.refs_3_.refs_0_), channel_id=1, source_target_pairs={{0,1},{1,0},{2,3},{3,2},{4,5},{5,4},{6,7},{7,6},{8,9},{9,8},{10,11... | collective-permute-start | bytes 614408 | tf_op jit(solution)/shard_map/inner_core/ppermute | solution.py:381
  (9 other events, 42.7 us)

commit v5 on v4

--- a/solution.py
+++ b/solution.py
@@ -369,12 +369,14 @@
             add_x_kernel, [inner_shape, SDS((2, 4, size, lanes), F32), quarter_shape, quarter_shape],
             away, inner, *got, mine, other, *two,
         )
-    with jax.named_scope("row_core"):
-        other = lax.ppermute(mine, "col", SWAP_CORE)
     with jax.named_scope("pair_two"):
         two = [lax.ppermute(two[0], "row", SHIFT_X[1]), lax.ppermute(two[1], "row", SHIFT_X[3])]
     with jax.named_scope("inner_gy"):
-        inner = jnp.stack([inner] + send([(d, inner) for d in (1, 2, 3)], "col", SHIFT_Y))
+        got = send([(d, inner) for d in (1, 2, 3)], "col", SHIFT_Y)
+        inner = jnp.stack([inner] + got)
+    with jax.named_scope("row_core"):
+        mine = tie(mine, *got)
+        other = lax.ppermute(mine, "col", SWAP_CORE)
     with jax.named_scope("inner_zlo"):
         inner = jnp.stack([inner, lax.ppermute(inner, "col", SWAP_ZLO)])
     with jax.named_scope("inner_core"):

time: 144 us -> 147 us (1.021)
  local copies, waits for them, and re-layouts: 3.42 us -> 5.14 us
    unnamed x12 -> x22, local copies, waits for them, and re-layouts: 1.82 us -> 3.55 us
    ppermute x1, starting transfers between devices: 10.4 us -> 12.1 us  [body(): other = lax.ppermute(mine, 'col', SWAP_CORE)]
  transfers between devices with their start and end apart: 35 -> 35, of which waited for: 19 -> 19; matrix products, arithmetic and copies ran while one was open for 1% -> 2% of each run, Pallas kernels for 3% -> 3%
where the time goes in v5:
time: 147 us
  starting transfers between devices  73 us (50%)
  waiting for transfers between devices  40.5 us (28%)
  Pallas kernels  26.9 us (18%)
  local copies, waits for them, and re-layouts  5.14 us (3%)
    ppermute x27, starting transfers between devices, send(): return [lax.ppermute(part, axis, shifts[d]) for d, part in parts]  44.1 us
    ppermute x27, waiting for transfers between devices, send(): return [lax.ppermute(part, axis, shifts[d]) for d, part in parts]  33.4 us
    ppermute x1, starting transfers between devices, body(): other = lax.ppermute(mine, 'col', SWAP_CORE)  12.1 us
    pallas_call x8, Pallas kernels, whole_kernel(): pl.pallas_call(lambda place, *refs: kernel(place, *refs[:count], *refs[co...  11.5 us
    pallas_call x1, Pallas kernels, update(): pl.pallas_call(update_kernel, out_shape=SDS((rows, columns), F32), in_spe...  8.89 us
    ppermute x1, starting transfers between devices, body(): vec_part = lax.ppermute(tie(turn, got[0][:8, :128]), EVERYWHERE, TO_COLUMN)  8.27 us
    pallas_call x1, Pallas kernels, quarter_products(): pl.pallas_call(quarter_product_kernel, out_shape=[shape] * 4, grid=(4,),...  6.45 us
    ppermute x1, waiting for transfers between devices, body(): other = lax.ppermute(prod_part, EVERYWHERE, TO_ROW)  3.83 us
  transfers between devices with their start and end apart: 35, of which 19 were waited for; matrix products, arithmetic and copies ran while one was open for 2% of the time, Pallas kernels for 3%

profile of v5, /device:TPU:1, one launch (start us, length us, event | category | flops | bytes accessed | tf_op | source)
XLA Modules:
  0.0 146.9 jit_solution(16512361710284977925)
XLA Ops:
  0.0 6.4 %products.1 = (f32[320,256]{1,0:T(8,128)}, f32[320,256]{1,0:T(8,128)}, f32[320,256]{1,0:T(8,128)}, f32[320,256]{1,0:T(8,128)}) custom-call(f32[320,1024]{1,0:T(8,128)} %bitcast.36, f32[1024,1024]{1,0:T(8,128)} %refs_8_.1), custom_call_target="tpu_custom_call" | custom-call | flops 2013265920 | bytes 6815744 | tf_op jit(solution)/shard_map/products/pallas_call | solution.py:126
  6.5 3.6 %collective-permute-start = (f32[320,256]{1,0:T(8,128)}, f32[320,256]{1,0:T(8,128)S(1)}, u32[]{:S(2)}, u32[]{:S(2)}) collective-permute-start(f32[320,256]{1,0:T(8,128)} %get-tuple-element.34), channel_id=1, source_target_pairs={{0,32},{16,48},{32,0},{48,16},{64,96},{80,112},{96,64},{112,80},{1... | collective-permute-start | bytes 983048 | tf_op jit(solution)/shard_map/prod_sum_x/ppermute | solution.py:66
  10.3 2.4 %collective-permute-start.2 = (f32[320,256]{1,0:T(8,128)}, f32[320,256]{1,0:T(8,128)S(1)}, u32[]{:S(2)}, u32[]{:S(2)}) collective-permute-start(f32[320,256]{1,0:T(8,128)} %get-tuple-element.36), channel_id=1, source_target_pairs={{0,48},{16,0},{32,16},{48,32},{64,112},{80,64},{96,80},{112,96},{1... | collective-permute-start | bytes 983048 | tf_op jit(solution)/shard_map/prod_sum_x/ppermute | solution.py:66
  13.5 3.3 %collective-permute-done.refs_1_ = f32[320,256]{1,0:T(8,128)S(1)} collective-permute-done((f32[320,256]{1,0:T(8,128)}, f32[320,256]{1,0:T(8,128)S(1)}, u32[]{:S(2)}, u32[]{:S(2)}) %collective-permute-start) | collective-permute-done | bytes 327712 | tf_op jit(solution)/shard_map/prod_sum_x/ppermute | solution.py:66
  17.4 8.3 %collective-permute-start.6 = (f32[80,256]{1,0:T(8,128)}, f32[80,256]{1,0:T(8,128)S(1)}, u32[]{:S(2)}, u32[]{:S(2)}) collective-permute-start(f32[80,256]{1,0:T(8,128)} %vec_turn.1), channel_id=1, source_target_pairs={{0,0},{1,64},{2,128},{3,192},{4,16},{5,80},{6,144},{7,208},{8,32},... | collective-permute-start | bytes 245768 | tf_op jit(solution)/shard_map/vec_turn/ppermute | solution.py:322
  27.3 3.0 %collective-permute-start.3 = (f32[80,256]{1,0:T(8,128)S(1)}, f32[80,256]{1,0:T(8,128)S(1)}, u32[]{:S(2)}, u32[]{:S(2)}) collective-permute-start(f32[80,256]{1,0:T(8,128)S(1)} %get-tuple-element.38), channel_id=1, source_target_pairs={{0,64},{16,80},{32,96},{48,112},{64,128},{80,144},{96,160},{112,17... | collective-permute-start | bytes 245768 | tf_op jit(solution)/shard_map/prod_sum_z/ppermute | solution.py:66
  30.3 5.1 %collective-permute-start.4 = (f32[80,256]{1,0:T(8,128)S(1)}, f32[80,256]{1,0:T(8,128)S(1)}, u32[]{:S(2)}, u32[]{:S(2)}) collective-permute-start(f32[80,256]{1,0:T(8,128)S(1)} %get-tuple-element.39), channel_id=1, source_target_pairs={{0,128},{16,144},{32,160},{48,176},{64,192},{80,208},{96,224},{112... | collective-permute-start | bytes 245768 | tf_op jit(solution)/shard_map/prod_sum_z/ppermute | solution.py:66
  35.5 2.4 %collective-permute-start.5 = (f32[80,256]{1,0:T(8,128)S(1)}, f32[80,256]{1,0:T(8,128)S(1)}, u32[]{:S(2)}, u32[]{:S(2)}) collective-permute-start(f32[80,256]{1,0:T(8,128)S(1)} %get-tuple-element.40), channel_id=1, source_target_pairs={{0,192},{16,208},{32,224},{48,240},{64,0},{80,16},{96,32},{112,48}... | collective-permute-start | bytes 245768 | tf_op jit(solution)/shard_map/prod_sum_z/ppermute | solution.py:66
  37.8 4.4 %collective-permute-done.4.refs_2_ = f32[80,256]{1,0:T(8,128)S(1)} collective-permute-done((f32[80,256]{1,0:T(8,128)S(1)}, f32[80,256]{1,0:T(8,128)S(1)}, u32[]{:S(2)}, u32[]{:S(2)}) %collective-permute-start.4) | collective-permute-done | bytes 81952 | tf_op jit(solution)/shard_map/prod_sum_z/ppermute | solution.py:66
  42.3 2.2 %collective-permute-done.5.refs_3_ = f32[80,256]{1,0:T(8,128)S(1)} collective-permute-done((f32[80,256]{1,0:T(8,128)S(1)}, f32[80,256]{1,0:T(8,128)S(1)}, u32[]{:S(2)}, u32[]{:S(2)}) %collective-permute-start.5) | collective-permute-done | bytes 81952 | tf_op jit(solution)/shard_map/prod_sum_z/ppermute | solution.py:66
  45.0 3.6 %collective-permute-start.8 = (f32[160,256]{1,0:T(8,128)S(1)}, f32[160,256]{1,0:T(8,128)S(1)}, u32[]{:S(2)}, u32[]{:S(2)}) collective-permute-start(f32[160,256]{1,0:T(8,128)S(1)} %get-tuple-element.41.refs_0_), channel_id=1, source_target_pairs={{0,192},{16,208},{32,224},{48,240},{64,0},{80,16},{96,32},{112,48}... | collective-permute-start | bytes 491528 | tf_op jit(solution)/shard_map/pair_z/ppermute | solution.py:66
  48.6 3.3 %collective-permute-start.11 = (f32[80,256]{1,0:T(8,128)S(1)}, f32[80,256]{1,0:T(8,128)S(1)}, u32[]{:S(2)}, u32[]{:S(2)}) collective-permute-start(f32[80,256]{1,0:T(8,128)S(1)} %get-tuple-element.42), channel_id=1, source_target_pairs={{0,0},{64,1},{128,2},{192,3},{16,4},{80,5},{144,6},{208,7},{32,8},... | collective-permute-start | bytes 245768 | tf_op jit(solution)/shard_map/prod_turn/ppermute | solution.py:335
  51.9 3.2 %collective-permute-done.8.refs_2_ = f32[160,256]{1,0:T(8,128)S(1)} collective-permute-done((f32[160,256]{1,0:T(8,128)S(1)}, f32[160,256]{1,0:T(8,128)S(1)}, u32[]{:S(2)}, u32[]{:S(2)}) %collective-permute-start.8) | collective-permute-done | bytes 163872 | tf_op jit(solution)/shard_map/pair_z/ppermute | solution.py:66
  55.1 4.1 %collective-permute-start.10 = (f32[80,256]{1,0:T(8,128)S(1)}, f32[80,256]{1,0:T(8,128)S(1)}, u32[]{:S(2)}, u32[]{:S(2)}) collective-permute-start(f32[80,256]{1,0:T(8,128)S(1)} %slice.14), channel_id=1, source_target_pairs={{0,192},{16,208},{32,224},{48,240},{64,0},{80,16},{96,32},{112,48}... | collective-permute-start | bytes 245768 | tf_op jit(solution)/shard_map/pair_z/ppermute | solution.py:66
  59.6 3.8 %collective-permute-done.11.refs_5_ = f32[80,256]{1,0:T(8,128)S(1)} collective-permute-done((f32[80,256]{1,0:T(8,128)S(1)}, f32[80,256]{1,0:T(8,128)S(1)}, u32[]{:S(2)}, u32[]{:S(2)}) %collective-permute-start.11) | collective-permute-done | bytes 81952 | tf_op jit(solution)/shard_map/prod_turn/ppermute | solution.py:335
  63.4 2.3 %collective-permute-done.10.refs_4_ = f32[80,256]{1,0:T(8,128)S(1)} collective-permute-done((f32[80,256]{1,0:T(8,128)S(1)}, f32[80,256]{1,0:T(8,128)S(1)}, u32[]{:S(2)}, u32[]{:S(2)}) %collective-permute-start.10) | collective-permute-done | bytes 81952 | tf_op jit(solution)/shard_map/pair_z/ppermute | solution.py:66
  66.7 3.2 %collective-permute-start.13 = (f32[640,256]{1,0:T(8,128)S(1)}, f32[640,256]{1,0:T(8,128)S(1)}, u32[]{:S(2)}, u32[]{:S(2)}) collective-permute-start(f32[640,256]{1,0:T(8,128)S(1)} %get-tuple-element.43.refs_0_), channel_id=1, source_target_pairs={{0,48},{16,0},{32,16},{48,32},{64,112},{80,64},{96,80},{112,96},{1... | collective-permute-start | bytes 1966088 | tf_op jit(solution)/shard_map/pair_x/ppermute | solution.py:66
  70.0 4.0 %collective-permute-start.15 = (f32[80,80]{1,0:T(8,128)S(1)}, f32[80,80]{1,0:T(8,128)S(1)}, u32[]{:S(2)}, u32[]{:S(2)}) collective-permute-start(f32[80,80]{1,0:T(8,128)S(1)} %get-tuple-element.46), channel_id=1, source_target_pairs={{0,8},{1,9},{2,10},{3,11},{4,12},{5,13},{6,14},{7,15},{8,0},{9,1},... | collective-permute-start | bytes 76808 | tf_op jit(solution)/shard_map/inner_y/ppermute | solution.py:66
  75.8 2.8 %collective-permute-start.18 = (f32[80,256]{1,0:T(8,128)S(1)}, f32[80,256]{1,0:T(8,128)S(1)}, u32[]{:S(2)}, u32[]{:S(2)}) collective-permute-start(f32[80,256]{1,0:T(8,128)S(1)} %get-tuple-element.48.refs_4_), channel_id=1, source_target_pairs={{0,8},{1,9},{2,10},{3,11},{4,12},{5,13},{6,14},{7,15},{8,0},{9,1},... | collective-permute-start | bytes 245768 | tf_op jit(solution)/shard_map/row_y/ppermute | solution.py:66
  78.6 2.6 %collective-permute-done.18.refs_6_ = f32[80,256]{1,0:T(8,128)S(1)} collective-permute-done((f32[80,256]{1,0:T(8,128)S(1)}, f32[80,256]{1,0:T(8,128)S(1)}, u32[]{:S(2)}, u32[]{:S(2)}) %collective-permute-start.18) | collective-permute-done | bytes 81952 | tf_op jit(solution)/shard_map/row_y/ppermute | solution.py:66
  81.3 2.2 %collective-permute-done.17.refs_5_ = f32[80,256]{1,0:T(8,128)S(1)} collective-permute-done((f32[80,256]{1,0:T(8,128)S(1)}, f32[80,256]{1,0:T(8,128)S(1)}, u32[]{:S(2)}, u32[]{:S(2)}) %collective-permute-start.17) | collective-permute-done | bytes 81952 | tf_op jit(solution)/shard_map/row_y/ppermute | solution.py:66
  84.8 3.1 %collective-permute-start.21 = (f32[80,80]{1,0:T(8,128)S(1)}, f32[80,80]{1,0:T(8,128)S(1)}, u32[]{:S(2)}, u32[]{:S(2)}) collective-permute-start(f32[80,80]{1,0:T(8,128)S(1)} %get-tuple-element.49.refs_0_), channel_id=1, source_target_pairs={{0,128},{16,144},{32,160},{48,176},{64,192},{80,208},{96,224},{112... | collective-permute-start | bytes 76808 | tf_op jit(solution)/shard_map/inner_z/ppermute | solution.py:66
  87.9 3.6 %collective-permute-done.21.refs_2_ = f32[80,80]{1,0:T(8,128)S(1)} collective-permute-done((f32[80,80]{1,0:T(8,128)S(1)}, f32[80,80]{1,0:T(8,128)S(1)}, u32[]{:S(2)}, u32[]{:S(2)}) %collective-permute-start.21) | collective-permute-done | bytes 25632 | tf_op jit(solution)/shard_map/inner_z/ppermute | solution.py:66
  91.6 1.7 %collective-permute-done.20.refs_1_ = f32[80,80]{1,0:T(8,128)S(1)} collective-permute-done((f32[80,80]{1,0:T(8,128)S(1)}, f32[80,80]{1,0:T(8,128)S(1)}, u32[]{:S(2)}, u32[]{:S(2)}) %collective-permute-start.20) | collective-permute-done | bytes 25632 | tf_op jit(solution)/shard_map/inner_z/ppermute | solution.py:66
  98.5 2.5 %collective-permute-done.24.refs_2_ = f32[80,80]{1,0:T(8,128)S(1)} collective-permute-done((f32[80,80]{1,0:T(8,128)S(1)}, f32[80,80]{1,0:T(8,128)S(1)}, u32[]{:S(2)}, u32[]{:S(2)}) %collective-permute-start.24) | collective-permute-done | bytes 25632 | tf_op jit(solution)/shard_map/inner_x/ppermute | solution.py:66
  106.6 1.7 %collective-permute-done.30.refs_2_ = f32[80,80]{1,0:T(8,128)S(1)} collective-permute-done((f32[80,80]{1,0:T(8,128)S(1)}, f32[80,80]{1,0:T(8,128)S(1)}, u32[]{:S(2)}, u32[]{:S(2)}) %collective-permute-start.30) | collective-permute-done | bytes 25632 | tf_op jit(solution)/shard_map/inner_gy/ppermute | solution.py:66
  109.9 12.1 %collective-permute-start.34 = (f32[2,4,80,256]{3,2,1,0:T(8,128)}, f32[2,4,80,256]{3,2,1,0:T(8,128)}, u32[]{:S(2)}, u32[]{:S(2)}) collective-permute-start(f32[2,4,80,256]{3,2,1,0:T(8,128)} %row_core.1.refs_1_), channel_id=1, source_target_pairs={{0,1},{1,0},{2,3},{3,2},{4,5},{5,4},{6,7},{7,6},{8,9},{9,8},{10,11... | collective-permute-start | bytes 1966088 | tf_op jit(solution)/shard_map/row_core/ppermute | solution.py:379
  123.0 2.7 %collective-permute-start.28 = (f32[320,256]{1,0:T(8,128)}, f32[320,256]{1,0:T(8,128)}, u32[]{:S(2)}, u32[]{:S(2)}) collective-permute-start(f32[320,256]{1,0:T(8,128)} %get-tuple-element.56), channel_id=1, source_target_pairs={{0,48},{16,0},{32,16},{48,32},{64,112},{80,64},{96,80},{112,96},{1... | collective-permute-start | bytes 983048 | tf_op jit(solution)/shard_map/pair_two/ppermute | solution.py:373
  125.7 3.2 %collective-permute-done.32 = f32[4,80,80]{2,1,0:T(8,128)S(1)} collective-permute-done((f32[4,80,80]{2,1,0:T(8,128)S(1)}, f32[4,80,80]{2,1,0:T(8,128)S(1)}, u32[]{:S(2)}, u32[]{:S(2)}) %collective-permute-start.32) | collective-permute-done | bytes 102432 | tf_op jit(solution)/shard_map/inner_zlo/ppermute | solution.py:381
  131.1 2.6 %left.1.refs_5_.refs_7_ = bf16[1024,1920]{1,0:T(8,128)(2,1)S(1)} custom-call(s32[8]{0:T(128)S(1)} %stack.159.place, f32[320,1024]{1,0:T(8,128)S(1)} %bitcast.39, f32[2,4,80,256]{3,2,1,0:T(8,128)S(1)} %copy-done.3, f32[2,4,80,256]{3,2,1,0:T(8,128)} %collective-permute-done.34.refs_2_, f32[2,4,80,80]{3,2,1,0:T(8,128)S(1)} %pad_maximum_fusion.refs_3_.refs_0_), custom_call_target="tpu_custom_call" | custom-call | bytes 6553600 | tf_op jit(solution)/shard_map/left/pallas_call | solution.py:72
  133.8 4.0 %factor.1 = (bf16[320,1920]{1,0:T(8,128)(2,1)S(1)}, bf16[320,960]{1,0:T(8,128)(2,1)S(1)}) custom-call(s32[8]{0:T(128)S(1)} %stack.159.place, f32[2,4,80,80]{3,2,1,0:T(8,128)S(1)} %pad_maximum_fusion.refs_3_.refs_0_, f32[2,4,80,80]{3,2,1,0:T(8,128)} %collective-permute-done.33.refs_1_, f32[5,64,64]{2,1,0:T(8,128)S(1)} %copy-done.7, ...), custom_call_target="tpu_custom_call" | custom-call | bytes 2334720 | tf_op jit(solution)/shard_map/factor/pallas_call | solution.py:72
  137.9 8.9 %update.1 = f32[1024,1024]{1,0:T(8,128)} custom-call(s32[4]{0:T(128)S(1)} %pad_add_fusion.place, f32[640,256]{1,0:T(8,128)S(1)} %copy-done.5, f32[640,256]{1,0:T(8,128)S(1)} %collective-permute-done.12.refs_5_.refs_1_, f32[640,256]{1,0:T(8,128)S(1)} %collective-permute-done.13.refs_6_.refs_2_, f32[320,256]{1,0:T(8,128)S(1)} %collective-permute-done.27.refs_3_, ...), custom_call_target="tpu_custom_call" | custom-call | flops 4026531840 | bytes 8388608 | tf_op jit(solution)/shard_map/update/pallas_call | solution.py:279
  (82 shorter events, 24.1 us)
Async XLA Ops:
  6.5 10.4 %collective-permute-start = (f32[320,256]{1,0:T(8,128)}, f32[320,256]{1,0:T(8,128)S(1)}, u32[]{:S(2)}, u32[]{:S(2)}) collective-permute-start(f32[320,256]{1,0:T(8,128)} %get-tuple-element.34), channel_id=1, source_target_pairs={{0,32},{16,48},{32,0},{48,16},{64,96},{80,112},{96,64},{112,80},{1... | collective-permute-start | bytes 983048 | tf_op jit(solution)/shard_map/prod_sum_x/ppermute | solution.py:66
  10.0 15.7 %collective-permute-start.1 = (f32[320,256]{1,0:T(8,128)}, f32[320,256]{1,0:T(8,128)S(1)}, u32[]{:S(2)}, u32[]{:S(2)}) collective-permute-start(f32[320,256]{1,0:T(8,128)} %get-tuple-element.35), channel_id=1, source_target_pairs={{0,16},{16,32},{32,48},{48,0},{64,80},{80,96},{96,112},{112,64},{1... | collective-permute-start | bytes 983048 | tf_op jit(solution)/shard_map/prod_sum_x/ppermute | solution.py:66
  10.3 15.4 %collective-permute-start.2 = (f32[320,256]{1,0:T(8,128)}, f32[320,256]{1,0:T(8,128)S(1)}, u32[]{:S(2)}, u32[]{:S(2)}) collective-permute-start(f32[320,256]{1,0:T(8,128)} %get-tuple-element.36), channel_id=1, source_target_pairs={{0,48},{16,0},{32,16},{48,32},{64,112},{80,64},{96,80},{112,96},{1... | collective-permute-start | bytes 983048 | tf_op jit(solution)/shard_map/prod_sum_x/ppermute | solution.py:66
  17.4 20.4 %collective-permute-start.6 = (f32[80,256]{1,0:T(8,128)}, f32[80,256]{1,0:T(8,128)S(1)}, u32[]{:S(2)}, u32[]{:S(2)}) collective-permute-start(f32[80,256]{1,0:T(8,128)} %vec_turn.1), channel_id=1, source_target_pairs={{0,0},{1,64},{2,128},{3,192},{4,16},{5,80},{6,144},{7,208},{8,32},... | collective-permute-start | bytes 245768 | tf_op jit(solution)/shard_map/vec_turn/ppermute | solution.py:322
  27.3 10.5 %collective-permute-start.3 = (f32[80,256]{1,0:T(8,128)S(1)}, f32[80,256]{1,0:T(8,128)S(1)}, u32[]{:S(2)}, u32[]{:S(2)}) collective-permute-start(f32[80,256]{1,0:T(8,128)S(1)} %get-tuple-element.38), channel_id=1, source_target_pairs={{0,64},{16,80},{32,96},{48,112},{64,128},{80,144},{96,160},{112,17... | collective-permute-start | bytes 245768 | tf_op jit(solution)/shard_map/prod_sum_z/ppermute | solution.py:66
  30.3 11.9 %collective-permute-start.4 = (f32[80,256]{1,0:T(8,128)S(1)}, f32[80,256]{1,0:T(8,128)S(1)}, u32[]{:S(2)}, u32[]{:S(2)}) collective-permute-start(f32[80,256]{1,0:T(8,128)S(1)} %get-tuple-element.39), channel_id=1, source_target_pairs={{0,128},{16,144},{32,160},{48,176},{64,192},{80,208},{96,224},{112... | collective-permute-start | bytes 245768 | tf_op jit(solution)/shard_map/prod_sum_z/ppermute | solution.py:66
  35.5 9.0 %collective-permute-start.5 = (f32[80,256]{1,0:T(8,128)S(1)}, f32[80,256]{1,0:T(8,128)S(1)}, u32[]{:S(2)}, u32[]{:S(2)}) collective-permute-start(f32[80,256]{1,0:T(8,128)S(1)} %get-tuple-element.40), channel_id=1, source_target_pairs={{0,192},{16,208},{32,224},{48,240},{64,0},{80,16},{96,32},{112,48}... | collective-permute-start | bytes 245768 | tf_op jit(solution)/shard_map/prod_sum_z/ppermute | solution.py:66
  45.0 10.1 %collective-permute-start.8 = (f32[160,256]{1,0:T(8,128)S(1)}, f32[160,256]{1,0:T(8,128)S(1)}, u32[]{:S(2)}, u32[]{:S(2)}) collective-permute-start(f32[160,256]{1,0:T(8,128)S(1)} %get-tuple-element.41.refs_0_), channel_id=1, source_target_pairs={{0,192},{16,208},{32,224},{48,240},{64,0},{80,16},{96,32},{112,48}... | collective-permute-start | bytes 491528 | tf_op jit(solution)/shard_map/pair_z/ppermute | solution.py:66
  48.6 10.7 %collective-permute-start.7 = (f32[160,256]{1,0:T(8,128)S(1)}, f32[160,256]{1,0:T(8,128)S(1)}, u32[]{:S(2)}, u32[]{:S(2)}) collective-permute-start(f32[160,256]{1,0:T(8,128)S(1)} %get-tuple-element.41.refs_0_), channel_id=1, source_target_pairs={{0,64},{16,80},{32,96},{48,112},{64,128},{80,144},{96,160},{112,17... | collective-permute-start | bytes 491528 | tf_op jit(solution)/shard_map/pair_z/ppermute | solution.py:66
  48.6 14.8 %collective-permute-start.11 = (f32[80,256]{1,0:T(8,128)S(1)}, f32[80,256]{1,0:T(8,128)S(1)}, u32[]{:S(2)}, u32[]{:S(2)}) collective-permute-start(f32[80,256]{1,0:T(8,128)S(1)} %get-tuple-element.42), channel_id=1, source_target_pairs={{0,0},{64,1},{128,2},{192,3},{16,4},{80,5},{144,6},{208,7},{32,8},... | collective-permute-start | bytes 245768 | tf_op jit(solution)/shard_map/prod_turn/ppermute | solution.py:335
  55.1 10.6 %collective-permute-start.10 = (f32[80,256]{1,0:T(8,128)S(1)}, f32[80,256]{1,0:T(8,128)S(1)}, u32[]{:S(2)}, u32[]{:S(2)}) collective-permute-start(f32[80,256]{1,0:T(8,128)S(1)} %slice.14), channel_id=1, source_target_pairs={{0,192},{16,208},{32,224},{48,240},{64,0},{80,16},{96,32},{112,48}... | collective-permute-start | bytes 245768 | tf_op jit(solution)/shard_map/pair_z/ppermute | solution.py:66
  59.3 6.4 %collective-permute-start.9 = (f32[80,256]{1,0:T(8,128)S(1)}, f32[80,256]{1,0:T(8,128)S(1)}, u32[]{:S(2)}, u32[]{:S(2)}) collective-permute-start(f32[80,256]{1,0:T(8,128)S(1)} %slice.13), channel_id=1, source_target_pairs={{0,64},{16,80},{32,96},{48,112},{64,128},{80,144},{96,160},{112,17... | collective-permute-start | bytes 245768 | tf_op jit(solution)/shard_map/pair_z/ppermute | solution.py:66
  66.7 26.5 %collective-permute-start.13 = (f32[640,256]{1,0:T(8,128)S(1)}, f32[640,256]{1,0:T(8,128)S(1)}, u32[]{:S(2)}, u32[]{:S(2)}) collective-permute-start(f32[640,256]{1,0:T(8,128)S(1)} %get-tuple-element.43.refs_0_), channel_id=1, source_target_pairs={{0,48},{16,0},{32,16},{48,32},{64,112},{80,64},{96,80},{112,96},{1... | collective-permute-start | bytes 1966088 | tf_op jit(solution)/shard_map/pair_x/ppermute | solution.py:66
  70.0 23.3 %collective-permute-start.12 = (f32[640,256]{1,0:T(8,128)S(1)}, f32[640,256]{1,0:T(8,128)S(1)}, u32[]{:S(2)}, u32[]{:S(2)}) collective-permute-start(f32[640,256]{1,0:T(8,128)S(1)} %get-tuple-element.43.refs_0_), channel_id=1, source_target_pairs={{0,16},{16,32},{32,48},{48,0},{64,80},{80,96},{96,112},{112,64},{1... | collective-permute-start | bytes 1966088 | tf_op jit(solution)/shard_map/pair_x/ppermute | solution.py:66
  70.0 4.2 %collective-permute-start.14 = (f32[80,80]{1,0:T(8,128)S(1)}, f32[80,80]{1,0:T(8,128)S(1)}, u32[]{:S(2)}, u32[]{:S(2)}) collective-permute-start(f32[80,80]{1,0:T(8,128)S(1)} %get-tuple-element.45), channel_id=1, source_target_pairs={{0,4},{1,5},{2,6},{3,7},{4,8},{5,9},{6,10},{7,11},{8,12},{9,13},{1... | collective-permute-start | bytes 76808 | tf_op jit(solution)/shard_map/inner_y/ppermute | solution.py:66
  70.0 5.8 %collective-permute-start.15 = (f32[80,80]{1,0:T(8,128)S(1)}, f32[80,80]{1,0:T(8,128)S(1)}, u32[]{:S(2)}, u32[]{:S(2)}) collective-permute-start(f32[80,80]{1,0:T(8,128)S(1)} %get-tuple-element.46), channel_id=1, source_target_pairs={{0,8},{1,9},{2,10},{3,11},{4,12},{5,13},{6,14},{7,15},{8,0},{9,1},... | collective-permute-start | bytes 76808 | tf_op jit(solution)/shard_map/inner_y/ppermute | solution.py:66
  74.0 4.7 %collective-permute-start.16 = (f32[80,80]{1,0:T(8,128)S(1)}, f32[80,80]{1,0:T(8,128)S(1)}, u32[]{:S(2)}, u32[]{:S(2)}) collective-permute-start(f32[80,80]{1,0:T(8,128)S(1)} %get-tuple-element.47), channel_id=1, source_target_pairs={{0,12},{1,13},{2,14},{3,15},{4,0},{5,1},{6,2},{7,3},{8,4},{9,5},{1... | collective-permute-start | bytes 76808 | tf_op jit(solution)/shard_map/inner_y/ppermute | solution.py:66
  74.2 4.5 %collective-permute-start.19 = (f32[80,256]{1,0:T(8,128)S(1)}, f32[80,256]{1,0:T(8,128)S(1)}, u32[]{:S(2)}, u32[]{:S(2)}) collective-permute-start(f32[80,256]{1,0:T(8,128)S(1)} %get-tuple-element.48.refs_4_), channel_id=1, source_target_pairs={{0,12},{1,13},{2,14},{3,15},{4,0},{5,1},{6,2},{7,3},{8,4},{9,5},{1... | collective-permute-start | bytes 245768 | tf_op jit(solution)/shard_map/row_y/ppermute | solution.py:66
  75.8 5.4 %collective-permute-start.18 = (f32[80,256]{1,0:T(8,128)S(1)}, f32[80,256]{1,0:T(8,128)S(1)}, u32[]{:S(2)}, u32[]{:S(2)}) collective-permute-start(f32[80,256]{1,0:T(8,128)S(1)} %get-tuple-element.48.refs_4_), channel_id=1, source_target_pairs={{0,8},{1,9},{2,10},{3,11},{4,12},{5,13},{6,14},{7,15},{8,0},{9,1},... | collective-permute-start | bytes 245768 | tf_op jit(solution)/shard_map/row_y/ppermute | solution.py:66
  78.6 4.8 %collective-permute-start.17 = (f32[80,256]{1,0:T(8,128)S(1)}, f32[80,256]{1,0:T(8,128)S(1)}, u32[]{:S(2)}, u32[]{:S(2)}) collective-permute-start(f32[80,256]{1,0:T(8,128)S(1)} %get-tuple-element.48.refs_4_), channel_id=1, source_target_pairs={{0,4},{1,5},{2,6},{3,7},{4,8},{5,9},{6,10},{7,11},{8,12},{9,13},{1... | collective-permute-start | bytes 245768 | tf_op jit(solution)/shard_map/row_y/ppermute | solution.py:66
  84.8 6.8 %collective-permute-start.21 = (f32[80,80]{1,0:T(8,128)S(1)}, f32[80,80]{1,0:T(8,128)S(1)}, u32[]{:S(2)}, u32[]{:S(2)}) collective-permute-start(f32[80,80]{1,0:T(8,128)S(1)} %get-tuple-element.49.refs_0_), channel_id=1, source_target_pairs={{0,128},{16,144},{32,160},{48,176},{64,192},{80,208},{96,224},{112... | collective-permute-start | bytes 76808 | tf_op jit(solution)/shard_map/inner_z/ppermute | solution.py:66
  87.9 5.3 %collective-permute-start.20 = (f32[80,80]{1,0:T(8,128)S(1)}, f32[80,80]{1,0:T(8,128)S(1)}, u32[]{:S(2)}, u32[]{:S(2)}) collective-permute-start(f32[80,80]{1,0:T(8,128)S(1)} %get-tuple-element.49.refs_0_), channel_id=1, source_target_pairs={{0,64},{16,80},{32,96},{48,112},{64,128},{80,144},{96,160},{112,17... | collective-permute-start | bytes 76808 | tf_op jit(solution)/shard_map/inner_z/ppermute | solution.py:66
  93.9 7.2 %collective-permute-start.26 = (f32[4,80,256]{2,1,0:T(8,128)S(1)}, f32[4,80,256]{2,1,0:T(8,128)S(1)}, u32[]{:S(2)}, u32[]{:S(2)}) collective-permute-start(f32[4,80,256]{2,1,0:T(8,128)S(1)} %get-tuple-element.52.refs_4_), channel_id=1, source_target_pairs={{0,2},{1,3},{2,0},{3,1},{4,6},{5,7},{6,4},{7,5},{8,10},{9,11},{10,... | collective-permute-start | bytes 983048 | tf_op jit(solution)/shard_map/row_zlo/ppermute | solution.py:365
  96.3 4.6 %collective-permute-start.24 = (f32[80,80]{1,0:T(8,128)S(1)}, f32[80,80]{1,0:T(8,128)S(1)}, u32[]{:S(2)}, u32[]{:S(2)}) collective-permute-start(f32[80,80]{1,0:T(8,128)S(1)} %get-tuple-element.51.refs_0_), channel_id=1, source_target_pairs={{0,32},{16,48},{32,0},{48,16},{64,96},{80,112},{96,64},{112,80},{1... | collective-permute-start | bytes 76808 | tf_op jit(solution)/shard_map/inner_x/ppermute | solution.py:66
  96.6 4.5 %collective-permute-start.23 = (f32[80,80]{1,0:T(8,128)S(1)}, f32[80,80]{1,0:T(8,128)S(1)}, u32[]{:S(2)}, u32[]{:S(2)}) collective-permute-start(f32[80,80]{1,0:T(8,128)S(1)} %get-tuple-element.51.refs_0_), channel_id=1, source_target_pairs={{0,16},{16,32},{32,48},{48,0},{64,80},{80,96},{96,112},{112,64},{1... | collective-permute-start | bytes 76808 | tf_op jit(solution)/shard_map/inner_x/ppermute | solution.py:66
  103.9 4.4 %collective-permute-start.30 = (f32[80,80]{1,0:T(8,128)S(1)}, f32[80,80]{1,0:T(8,128)S(1)}, u32[]{:S(2)}, u32[]{:S(2)}) collective-permute-start(f32[80,80]{1,0:T(8,128)S(1)} %get-tuple-element.57), channel_id=1, source_target_pairs={{0,8},{1,9},{2,10},{3,11},{4,12},{5,13},{6,14},{7,15},{8,0},{9,1},... | collective-permute-start | bytes 76808 | tf_op jit(solution)/shard_map/inner_gy/ppermute | solution.py:66
  105.3 4.1 %collective-permute-start.29 = (f32[80,80]{1,0:T(8,128)S(1)}, f32[80,80]{1,0:T(8,128)S(1)}, u32[]{:S(2)}, u32[]{:S(2)}) collective-permute-start(f32[80,80]{1,0:T(8,128)S(1)} %get-tuple-element.57), channel_id=1, source_target_pairs={{0,4},{1,5},{2,6},{3,7},{4,8},{5,9},{6,10},{7,11},{8,12},{9,13},{1... | collective-permute-start | bytes 76808 | tf_op jit(solution)/shard_map/inner_gy/ppermute | solution.py:66
  109.9 20.1 %collective-permute-start.34 = (f32[2,4,80,256]{3,2,1,0:T(8,128)}, f32[2,4,80,256]{3,2,1,0:T(8,128)}, u32[]{:S(2)}, u32[]{:S(2)}) collective-permute-start(f32[2,4,80,256]{3,2,1,0:T(8,128)} %row_core.1.refs_1_), channel_id=1, source_target_pairs={{0,1},{1,0},{2,3},{3,2},{4,5},{5,4},{6,7},{7,6},{8,9},{9,8},{10,11... | collective-permute-start | bytes 1966088 | tf_op jit(solution)/shard_map/row_core/ppermute | solution.py:379
  122.8 6.0 %collective-permute-start.32 = (f32[4,80,80]{2,1,0:T(8,128)S(1)}, f32[4,80,80]{2,1,0:T(8,128)S(1)}, u32[]{:S(2)}, u32[]{:S(2)}) collective-permute-start(f32[4,80,80]{2,1,0:T(8,128)S(1)} %get-tuple-element.62), channel_id=1, source_target_pairs={{0,2},{1,3},{2,0},{3,1},{4,6},{5,7},{6,4},{7,5},{8,10},{9,11},{10,... | collective-permute-start | bytes 307208 | tf_op jit(solution)/shard_map/inner_zlo/ppermute | solution.py:381
  122.9 10.8 %collective-permute-start.27 = (f32[320,256]{1,0:T(8,128)}, f32[320,256]{1,0:T(8,128)S(1)}, u32[]{:S(2)}, u32[]{:S(2)}) collective-permute-start(f32[320,256]{1,0:T(8,128)} %get-tuple-element.55), channel_id=1, source_target_pairs={{0,16},{16,32},{32,48},{48,0},{64,80},{80,96},{96,112},{112,64},{1... | collective-permute-start | bytes 983048 | tf_op jit(solution)/shard_map/pair_two/ppermute | solution.py:373
  123.0 10.8 %collective-permute-start.28 = (f32[320,256]{1,0:T(8,128)}, f32[320,256]{1,0:T(8,128)}, u32[]{:S(2)}, u32[]{:S(2)}) collective-permute-start(f32[320,256]{1,0:T(8,128)} %get-tuple-element.56), channel_id=1, source_target_pairs={{0,48},{16,0},{32,16},{48,32},{64,112},{80,64},{96,80},{112,96},{1... | collective-permute-start | bytes 983048 | tf_op jit(solution)/shard_map/pair_two/ppermute | solution.py:373
  128.9 4.9 %collective-permute-start.33 = (f32[2,4,80,80]{3,2,1,0:T(8,128)S(1)}, f32[2,4,80,80]{3,2,1,0:T(8,128)}, u32[]{:S(2)}, u32[]{:S(2)}) collective-permute-start(f32[2,4,80,80]{3,2,1,0:T(8,128)S(1)} %pad_maximum_fusion.refs_3_.refs_0_), channel_id=1, source_target_pairs={{0,1},{1,0},{2,3},{3,2},{4,5},{5,4},{6,7},{7,6},{8,9},{9,8},{10,11... | collective-permute-start | bytes 614408 | tf_op jit(solution)/shard_map/inner_core/ppermute | solution.py:383
  (14 other events, 83.8 us)
